TPU v7x, 32 devices: a whole 2x2x4 slice. The times are simulated.
32 devices in a mesh: dp: 8 (over y, x, core), mp: 4 (over z).
Axes of the slice: x: 2, y: 2, z: 4, core: 2. Of those that a mesh axis runs over, the one named last changes fastest.
Arguments:
- inputs: bfloat16 [16, 48, 48, 800], P('dp', None, None, 'mp')
- crop_sizes: int32 [16, 2], P('dp'), may hold values from 24 to 48, as said below
- land_mask: int32 [16, 48, 48], P('dp'), may hold values 0 or 1
- conv_weight: bfloat16 [7, 7, 800], P(None, None, 'mp'), may hold values from -0.875 to 0.875
- norm_gain: bfloat16 [800], P('mp'), may hold values from 0.5 to 1.5
- norm_shift: bfloat16 [800], P('mp'), may hold values from -3 to 3
- up_weight: bfloat16 [800, 3200], P(None, 'mp'), may hold values from -0.21875 to 0.21875
- up_bias: bfloat16 [3200], P('mp'), may hold values from -3 to 3
- down_weight: bfloat16 [3200, 800], P('mp'), may hold values from -0.21875 to 0.21875
- down_bias: bfloat16 [800], P('mp'), may hold values from -3 to 3
- cotangent: bfloat16 [16, 48, 48, 800], P('dp', None, None, 'mp'), may hold values from -6 to 6
Outputs:
- output: bfloat16 [16, 48, 48, 800], P('dp', None, None, 'mp')
- input_grad: bfloat16 [16, 48, 48, 800], P('dp', None, None, 'mp')
- conv_weight_grad: float32 [7, 7, 800], P(None, None, 'mp')
- gain_grad: float32 [800], P('mp')
- shift_grad: float32 [800], P('mp')
- up_weight_grad: float32 [800, 3200], P(None, 'mp')
- up_bias_grad: float32 [3200], P('mp')
- down_weight_grad: float32 [3200, 800], P('mp')
- down_bias_grad: float32 [800], P('mp')
Inputs may be any that keep to these rules, and one draw needn't show every extreme that they name: `crop_sizes`: crop 0 always covers all 48 x 48 cells.
All inputs are finite; a program needn't handle non-finite values. No bound on the sum of `land_mask` on one device may be relied on, other than what follows from the above.
Results may differ from a plain program's by a relative error of at most 0.018.
Values may be sent and summed in bfloat16 or wider, within the bound.
No kernel may reach another device: no remote copies, remote signals or barrier semaphores. Data moves between devices by JAX's collectives and lax.ppermute only.
A program may use at most 128 MiB of HBM per device.

v0:
```python
import jax
import jax.numpy as jnp
from jax import lax
from jax.sharding import PartitionSpec as P

EPSILON = 1e-05
HALF_ROOT = 0.7071067811865476
INV_ROOT_TWO_PI = 0.3989422804014327


def validity(crop_dims, land_mask, side_cells):
    cell_index = jnp.arange(side_cells, dtype=jnp.int32)
    inside = (cell_index[None, :, None] < crop_dims[:, 0][:, None, None]) & (
        cell_index[None, None, :] < crop_dims[:, 1][:, None, None]
    )
    return jnp.where(inside, land_mask, 0).astype(jnp.float32)[..., None]


def pad_cells(field, half_width):
    return jnp.pad(field, ((0, 0), (half_width, half_width), (half_width, half_width), (0, 0)))


def depthwise(padded, kernel, side_cells, flipped):
    taps = kernel.shape[0]
    running = jnp.zeros((padded.shape[0], side_cells, side_cells, padded.shape[3]), jnp.float32)
    for row_tap in range(taps):
        for col_tap in range(taps):
            row_at = taps - 1 - row_tap if flipped else row_tap
            col_at = taps - 1 - col_tap if flipped else col_tap
            running = (
                running
                + padded[:, row_at : row_at + side_cells, col_at : col_at + side_cells, :]
                * kernel[row_tap, col_tap]
            )
    return running


def kernel_terms(padded, grad_conv, taps, side_cells):
    collected = []
    for row_tap in range(taps):
        for col_tap in range(taps):
            window = padded[:, row_tap : row_tap + side_cells, col_tap : col_tap + side_cells, :]
            collected.append(jnp.sum(window * grad_conv, axis=(0, 1, 2)))
    return jnp.stack(collected).reshape(taps, taps, -1)


def contract(left, right, left_dim, right_dim):
    return lax.dot_general(
        left, right, (((left_dim,), (right_dim,)), ((), ())), preferred_element_type=jnp.float32
    )


def gelu_exact(value):
    return 0.5 * value * (1.0 + lax.erf(value * HALF_ROOT))


def gelu_slope(value):
    return (
        0.5 * (1.0 + lax.erf(value * HALF_ROOT))
        + value * jnp.exp(-0.5 * value * value) * INV_ROOT_TWO_PI
    )


def per_device(
    inputs,
    crop_sizes,
    land_mask,
    conv_weight,
    norm_gain,
    norm_shift,
    up_weight,
    up_bias,
    down_weight,
    down_bias,
    cotangent,
):
    crop_count, side_cells = (inputs.shape[0], inputs.shape[1])
    owned_width = inputs.shape[3]
    pixel_count = crop_count * side_cells * side_cells
    taps = conv_weight.shape[0]
    half_width = taps // 2
    usable = validity(crop_sizes, land_mask, side_cells)
    source = inputs.astype(jnp.float32)
    kernel = conv_weight.astype(jnp.float32)
    masked = source * usable
    padded = pad_cells(masked, half_width)
    convolved = depthwise(padded, kernel, side_cells, False)
    first_sums, square_sums, ocean_count = lax.psum(
        (
            jnp.sum(usable * convolved, axis=(0, 1, 2)),
            jnp.sum(usable * convolved * convolved, axis=(0, 1, 2)),
            jnp.sum(usable),
        ),
        "dp",
    )
    channel_mean = first_sums / ocean_count
    inv_std = lax.rsqrt(square_sums / ocean_count - channel_mean * channel_mean + EPSILON)
    centred = (convolved - channel_mean) * inv_std
    gain_vec = norm_gain.astype(jnp.float32)
    normed = (
        (gain_vec * centred + norm_shift.astype(jnp.float32))
        .astype(jnp.bfloat16)
        .reshape(pixel_count, owned_width)
    )
    cot_float = cotangent.astype(jnp.float32)
    grad_branch = cot_float * usable
    grad_rows = grad_branch.astype(jnp.bfloat16).reshape(pixel_count, owned_width)
    preact = jnp.dot(
        lax.all_gather(normed, "mp", axis=1, tiled=True),
        up_weight,
        preferred_element_type=jnp.float32,
    ) + up_bias.astype(jnp.float32)
    hidden = gelu_exact(preact).astype(jnp.bfloat16)
    partial_value = jnp.dot(hidden, down_weight, preferred_element_type=jnp.float32)
    branch = lax.psum_scatter(
        partial_value.astype(jnp.bfloat16), "mp", scatter_dimension=1, tiled=True
    ).astype(jnp.float32)
    grad_full = lax.all_gather(grad_rows, "mp", axis=1, tiled=True)
    grad_hidden = contract(grad_full, down_weight, 1, 1)
    down_local = contract(hidden, grad_full, 0, 0)
    grad_preact = (grad_hidden * gelu_slope(preact)).astype(jnp.bfloat16)
    up_bias_local = jnp.sum(grad_preact.astype(jnp.float32), axis=0)
    up_local = contract(lax.all_gather(normed, "mp", axis=1, tiled=True), grad_preact, 0, 0)
    grad_normed = lax.psum_scatter(
        contract(grad_preact, up_weight, 1, 1).astype(jnp.bfloat16),
        "mp",
        scatter_dimension=1,
        tiled=True,
    ).astype(jnp.float32)
    branch = branch.reshape(crop_count, side_cells, side_cells, owned_width)
    output = (usable * (source + branch + down_bias.astype(jnp.float32))).astype(jnp.bfloat16)
    grad_normed = grad_normed.reshape(crop_count, side_cells, side_cells, owned_width)
    gain_local = jnp.sum(grad_normed * centred, axis=(0, 1, 2))
    shift_local = jnp.sum(grad_normed, axis=(0, 1, 2))
    down_bias_local = jnp.sum(grad_branch, axis=(0, 1, 2))
    up_weight_grad, up_bias_grad, down_weight_grad, down_bias_grad, gain_grad, shift_grad = (
        lax.psum(up_local.astype(jnp.bfloat16), "dp").astype(jnp.float32),
        lax.psum(up_bias_local.astype(jnp.bfloat16), "dp").astype(jnp.float32),
        lax.psum(down_local.astype(jnp.bfloat16), "dp").astype(jnp.float32),
        lax.psum(down_bias_local.astype(jnp.bfloat16), "dp").astype(jnp.float32),
        lax.psum(gain_local.astype(jnp.bfloat16), "dp").astype(jnp.float32),
        lax.psum(shift_local.astype(jnp.bfloat16), "dp").astype(jnp.float32),
    )
    grad_conv = inv_std * (
        gain_vec * grad_normed
        - usable * (gain_vec * shift_grad) / ocean_count
        - usable * centred * (gain_vec * gain_grad) / ocean_count
    )
    kernel_local = kernel_terms(padded, grad_conv, taps, side_cells)
    grad_masked = depthwise(pad_cells(grad_conv, half_width), kernel, side_cells, True)
    input_grad = (usable * (cot_float + grad_masked)).astype(jnp.bfloat16)
    conv_weight_grad = lax.psum(kernel_local, "dp")
    return (
        output,
        input_grad,
        conv_weight_grad,
        gain_grad,
        shift_grad,
        up_weight_grad,
        up_bias_grad,
        down_weight_grad,
        down_bias_grad,
    )


def solution(mesh):
    return jax.shard_map(
        per_device,
        mesh=mesh,
        in_specs=(
            P("dp", None, None, "mp"),
            P("dp", None),
            P("dp", None, None),
            P(None, None, "mp"),
            P("mp"),
            P("mp"),
            P(None, "mp"),
            P("mp"),
            P("mp", None),
            P("mp"),
            P("dp", None, None, "mp"),
        ),
        out_specs=(
            P("dp", None, None, "mp"),
            P("dp", None, None, "mp"),
            P(None, None, "mp"),
            P("mp"),
            P("mp"),
            P(None, "mp"),
            P("mp"),
            P("mp", None),
            P("mp"),
        ),
        check_vma=False,
    )
```

profile of v0, /device:TPU:0, one launch (start us, length us, event | category | flops | bytes accessed | tf_op | source)
XLA Modules:
  0.0 906.4 jit_solution(13780302398974220794)
XLA Ops:
  7.2 1.0 fusion.110
  8.3 1.0 fusion.111
  9.3 1.0 fusion.112
  10.2 1.0 slice_reduce_fusion.1
  12.6 1.5 fusion.109
  14.1 4.0 fusion.7
  18.1 44.6 %fusion.13 = (f32[200]{0:T(256)S(1)}, f32[200]{0:T(256)S(1)}, bf16[200]{0:T(256)(128)(2,1)S(1)}, f32[2,48,48,200]{3,2,1,0:T(8,128)}) fusion(f32[2,48,48]{2,1,0:T(8,128)S(1)} %get-tuple-element.80, bf16[2,48,48,200]{3,2,1,0:T(8,128)(2,1)S(1)} %copy-done.3, f32[200]{0:T(256)S(1)} %bitcast.215, f32[200]{0:T(256)S(1)} %bitcast.213, f32[200]{0:T(256)S(1)} %bitcast.211, ...), kind=kLoop, calls=%fused_computation.120 | loop fusion | flops 95845800 | bytes 9275632 | tf_op jit(solution)/shard_map/reduce_sum | solution.py:91
  62.7 15.7 %all-reduce.2 = (f32[200]{0:T(256)S(1)}, f32[]{:T(128)}, f32[200]{0:T(256)S(1)}) all-reduce(f32[200]{0:T(256)S(1)} %get-tuple-element.58, f32[]{:T(128)} %get-tuple-element.79, f32[200]{0:T(256)S(1)} %get-tuple-element.57), channel_id=1, replica_groups=mesh['dp'=8,'mp'=4] {'dp'}, use_global_device_ids=true, to_apply=%region_1.2 | all-reduce | flops 401 | bytes 3208 | tf_op jit(solution)/shard_map/psum | solution.py:88
  79.1 4.5 add_convert_fusion
  83.6 4.1 copy.25
  87.8 4.1 copy.27
  92.5 127.8 %all-gather.3.cloned.1.call-done = bf16[4608,800]{0,1:T(8,128)(2,1)} async-done(((bf16[4608,200]{0,1:T(8,128)(2,1)}), bf16[4608,800]{0,1:T(8,128)(2,1)}) %all-gather.3.cloned.1.call-update) | async-done | bytes 7372816 | tf_op jit(solution)/shard_map/all_gather | solution.py:109
  220.3 15.2 %multiply_convert_fusion = (bf16[4608,800]{0,1:T(8,128)(2,1)}, f32[4608,800]{0,1:T(8,128)}) fusion(f32[800]{0:T(1024)S(1)} %convert_element_type.92, bf16[4608,800]{0,1:T(8,128)(2,1)} %all-gather.3.cloned.1.call-done, bf16[800,800]{1,0:T(8,128)(2,1)S(1)} %copy-done), kind=kOutput, calls=%fused_computation.103 | convolution fusion | flops 5920358400 | bytes 30774400 | tf_op jit(solution)/shard_map/dot_general | solution.py:108
  235.4 118.3 %all-gather.5.cloned.1.call-done = bf16[4608,800]{0,1:T(8,128)(2,1)} async-done(((bf16[4608,200]{0,1:T(8,128)(2,1)}), bf16[4608,800]{0,1:T(8,128)(2,1)}) %all-gather.5.cloned.1.call-update) | async-done | bytes 7372816 | tf_op jit(solution)/shard_map/all_gather | solution.py:118
  353.7 15.6 %fusion.113 = (bf16[800]{0:T(1024)(128)(2,1)S(1)}, bf16[4608,800]{0,1:T(8,128)(2,1)}) fusion(f32[4608,800]{0,1:T(8,128)} %get-tuple-element.139, f32[800]{0:T(1024)S(1)} %convert_element_type.92, bf16[800,800]{1,0:T(8,128)(2,1)S(1)} %copy-done.10, bf16[4608,800]{0,1:T(8,128)(2,1)} %all-gather.5.cloned.1.call-done), kind=kOutput, calls=%fused_computation.286 | convolution fusion | flops 5942475776 | bytes 30776000 | tf_op jit(solution)/shard_map/dot_general | solution.py:48
  369.3 11.3 %convolution_convert_fusion.3 = bf16[800,800]{1,0:T(8,128)(2,1)} fusion(bf16[4608,800]{0,1:T(8,128)(2,1)S(1)} %copy-done.8, bf16[4608,800]{0,1:T(8,128)(2,1)} %get-tuple-element.137), kind=kOutput, calls=%fused_computation.271 | convolution fusion | flops 5898880000 | bytes 16025600 | tf_op jit(solution)/shard_map/dot_general | solution.py:48
  380.6 10.9 %convolution_convert_fusion.2 = bf16[800,800]{1,0:T(8,128)(2,1)} fusion(bf16[4608,800]{0,1:T(8,128)(2,1)} %get-tuple-element.138, bf16[4608,800]{0,1:T(8,128)(2,1)S(1)} %copy-done.9), kind=kOutput, calls=%fused_computation.270 | convolution fusion | flops 5898880000 | bytes 16025600 | tf_op jit(solution)/shard_map/dot_general | solution.py:48
  391.8 12.9 %convolution_convert_fusion = bf16[4608,800]{0,1:T(8,128)(2,1)} fusion(bf16[800,800]{1,0:T(8,128)(2,1)S(1)} %copy-done, bf16[4608,800]{0,1:T(8,128)(2,1)} %get-tuple-element.137), kind=kOutput, calls=%fused_computation.105 | convolution fusion | flops 5901926400 | bytes 16025600 | tf_op jit(solution)/shard_map/dot_general | solution.py:48
  404.8 12.1 %convolution_convert_fusion.1 = bf16[4608,800]{0,1:T(8,128)(2,1)} fusion(bf16[4608,800]{0,1:T(8,128)(2,1)} %get-tuple-element.138, bf16[800,800]{1,0:T(8,128)(2,1)S(1)} %copy-done.10), kind=kOutput, calls=%fused_computation.106 | convolution fusion | flops 5901926400 | bytes 16025600 | tf_op jit(solution)/shard_map/dot_general | solution.py:114
  417.5 39.5 %all-reduce.7.cloned.1.call-done = (bf16[800,800]{1,0:T(8,128)(2,1)}, bf16[800,800]{1,0:T(8,128)(2,1)}) async-done(((bf16[800,800]{1,0:T(8,128)(2,1)}, bf16[800,800]{1,0:T(8,128)(2,1)}), (bf16[800,800]{1,0:T(8,128)(2,1)}, bf16[800,800]{1,0:T(8,128)(2,1)})) %all-reduce.7.cloned.1.call-update) | async-done | bytes 2560016 | tf_op jit(solution)/shard_map/psum | solution.py:137
  457.0 3.2 convert_element_type.106
  460.2 1.8 convert_element_type.109
  462.0 125.5 %reduce-scatter.5.cloned.1.call-done = bf16[4608,200]{0,1:T(8,128)(2,1)} async-done(((bf16[4608,800]{0,1:T(8,128)(2,1)}), bf16[4608,200]{0,1:T(8,128)(2,1)}) %reduce-scatter.5.cloned.1.call-update) | async-done | bytes 1843216 | tf_op jit(solution)/shard_map/reduce_scatter | solution.py:124
  587.5 4.4 copy.28
  592.3 4.6 multiply_reduce_fusion.50
  596.8 14.3 %all-reduce.3 = (bf16[200]{0:T(256)(128)(2,1)S(1)}, bf16[200]{0:T(256)(128)(2,1)S(1)}, bf16[800]{0:T(1024)(128)(2,1)S(1)}, bf16[200]{0:T(256)(128)(2,1)S(1)}) all-reduce(bf16[200]{0:T(256)(128)(2,1)S(1)} %multiply_reduce_fusion.50, bf16[200]{0:T(256)(128)(2,1)S(1)} %reduce_sum.513, ...), channel_id=1, replica_groups=mesh['dp'=8,'mp'=4] {'dp'}, use_global_device_ids=true, to_apply=%region_11.12 | all-reduce | flops 1400 | bytes 5600 | tf_op jit(solution)/shard_map/psum | solution.py:141
  611.7 43.8 %multiply_reduce_fusion.1 = (f32[200]{0:T(256)S(1)}, f32[200]{0:T(256)S(1)}, f32[200]{0:T(256)S(1)}, f32[200]{0:T(256)S(1)}, f32[200]{0:T(256)S(1)}, /*index=5*/...) fusion(f32[2,48,48,200]{3,2,1,0:T(8,128)} %copy-done.2, ...), kind=kLoop, calls=%fused_computation.216 | loop fusion | flops 43311600 | bytes 14782436 | tf_op jit(solution)/shard_map/reduce_sum | solution.py:43
  655.6 41.0 %multiply_reduce_fusion.19 = (f32[200]{0:T(256)S(1)}, f32[200]{0:T(256)S(1)}, f32[200]{0:T(256)S(1)}, f32[200]{0:T(256)S(1)}, f32[200]{0:T(256)S(1)}, /*index=5*...) fusion(f32[2,48,48,200]{3,2,1,0:T(8,128)} %get-tuple-element.72, ...), kind=kLoop, calls=%fused_computation.234 | loop fusion | flops 33174000 | bytes 7387200 | tf_op jit(solution)/shard_map/reduce_sum | solution.py:43
  696.6 137.9 %fusion.12 = bf16[2,48,48,200]{3,2,1,0:T(8,128)(2,1)} fusion(bf16[2,48,48,200]{3,2,1,0:T(8,128)(2,1)} %param.21, f32[2,48,48,200]{3,2,1,0:T(8,128)} %get-tuple-element.72, f32[200]{0:T(256)S(1)} %bitcast.216, f32[200]{0:T(256)S(1)} %bitcast.214, f32[200]{0:T(256)S(1)} %bitcast.212, f32[200]{0:T(256)S(1)} %bitcast.210, f32[200]{0:T(256)S(1)} %bitcast.208, ...), kind=kLoop, calls=%fused_computation.119 | loop fusion | flops 93081600 | bytes 7430432 | tf_op jit(solution)/shard_map/convert_element_type | solution.py:151
  834.6 4.3 copy.26
  838.8 36.1 %multiply_reduce_fusion.38 = (f32[200]{0:T(256)S(1)}, f32[200]{0:T(256)S(1)}, f32[200]{0:T(256)S(1)}, f32[200]{0:T(256)S(1)}, f32[200]{0:T(256)S(1)}, /*index=5*...) fusion(f32[2,48,48,200]{3,2,1,0:T(8,128)} %get-tuple-element.72, ...), kind=kLoop, calls=%fused_computation.253 | loop fusion | flops 29488600 | bytes 14775232 | tf_op jit(solution)/shard_map/reduce_sum | solution.py:43
  875.1 23.4 %psum.75 = f32[7,7,200]{2,1,0:T(8,128)} all-reduce(f32[7,7,200]{2,1,0:T(8,128)S(1)} %reshape.153), channel_id=1, replica_groups=mesh['dp'=8,'mp'=4] {'dp'}, use_global_device_ids=true, to_apply=%region_61.62 | all-reduce | flops 9800 | bytes 78400 | tf_op jit(solution)/shard_map/psum | solution.py:152
  (47 shorter events, 6.0 us)
Async XLA Ops:
  7.2 213.1 %copy-start = (bf16[800,800]{1,0:T(8,128)(2,1)S(1)}, bf16[800,800]{1,0:T(8,128)(2,1)}, u32[]{:S(2)}) copy-start(bf16[800,800]{1,0:T(8,128)(2,1)} %param.17) | copy-start | bytes 3840004
  7.2 213.1 %all-gather.3.cloned.1.call-start = ((), (), s32[]{:S(2)}) async-start(), calls=%async_computation.2 | async-start | bytes 9216000 | tf_op jit(solution)/shard_map/all_gather | solution.py:109
  14.1 4.0 copy-start.3
  18.1 44.6 %copy-start.2 = (f32[2,48,48,200]{3,2,1,0:T(8,128)}, f32[2,48,48,200]{3,2,1,0:T(8,128)S(1)}, u32[]{:S(2)}) copy-start(f32[2,48,48,200]{3,2,1,0:T(8,128)S(1)} %get-tuple-element.84) | copy-start | bytes 11059204
  87.7 4.7 copy-start.6
  87.7 266.0 %all-gather.5.cloned.1.call-start = ((), (), s32[]{:S(2)}) async-start(), calls=%async_computation.4 | async-start | bytes 9216000 | tf_op jit(solution)/shard_map/all_gather | solution.py:118
  91.9 365.1 %all-reduce.7.cloned.1.call-start = ((), (), s32[]{:S(2)}) async-start(), calls=%async_computation.6 | async-start | bytes 5734400 | tf_op jit(solution)/shard_map/psum | solution.py:137
  92.5 261.3 %copy-start.10 = (bf16[800,800]{1,0:T(8,128)(2,1)S(1)}, bf16[800,800]{1,0:T(8,128)(2,1)}, u32[]{:S(2)}) copy-start(bf16[800,800]{1,0:T(8,128)(2,1)} %param.19) | copy-start | bytes 3840004
  353.7 15.6 %copy-start.8 = (bf16[4608,800]{0,1:T(8,128)(2,1)S(1)}, bf16[4608,800]{0,1:T(8,128)(2,1)}, u32[]{:S(2)}) copy-start(bf16[4608,800]{0,1:T(8,128)(2,1)} %all-gather.3.cloned.1.call-done) | copy-start | bytes 22118404
  369.3 11.3 %copy-start.9 = (bf16[4608,800]{0,1:T(8,128)(2,1)S(1)}, bf16[4608,800]{0,1:T(8,128)(2,1)}, u32[]{:S(2)}) copy-start(bf16[4608,800]{0,1:T(8,128)(2,1)} %all-gather.5.cloned.1.call-done) | copy-start | bytes 22118404
  391.5 196.0 %reduce-scatter.5.cloned.1.call-start = ((), (), s32[]{:S(2)}) async-start(), calls=%async_computation.5 | async-start | bytes 9216000 | tf_op jit(solution)/shard_map/reduce_scatter | solution.py:124
  404.7 429.9 %reduce-scatter.3.cloned.1.call-start = ((), (), s32[]{:S(2)}) async-start(), calls=%async_computation.3 | async-start | bytes 9216000 | tf_op jit(solution)/shard_map/reduce_scatter | solution.py:115
  416.9 0.7 copy-start.11
  457.0 3.2 copy-start.5
  587.5 4.4 copy-start.4
  592.3 18.9 %copy-start.7 = (bf16[200]{0:T(256)(128)(2,1)S(1)}, bf16[200]{0:T(256)(128)(2,1)}, u32[]{:S(2)}) copy-start(bf16[200]{0:T(256)(128)(2,1)} %param.15) | copy-start | bytes 1204
  838.8 60.8 %copy-start.1 = (bf16[800,800]{1,0:T(8,128)(2,1)S(1)}, bf16[800,800]{1,0:T(8,128)(2,1)}, u32[]{:S(2)}) copy-start(bf16[800,800]{1,0:T(8,128)(2,1)} %param.17) | copy-start | bytes 3840004
Sparse Core Ops, SparseCore 0:
  87.8 132.3 all-gather.2
  222.4 131.2 all-gather.4
  391.7 65.2 all-reduce.6
  459.3 128.1 reduce-scatter.4
  589.8 128.7 reduce-scatter.2
where the time goes:
time: 911 us; the launch traced here: 906 us
  waiting for transfers between devices  411 us (45%)
  other arithmetic  327 us (36%)
  matrix products  78 us (9%)
  blocking collectives  53.4 us (6%)
  local copies, waits for them, and re-layouts  21.6 us (2%)
  between operations  14.2 us (2%)
    convert_element_type x1, other arithmetic, per_device(): input_grad = (usable * (cot_float + grad_masked)).astype(jnp.bfloat16)  138 us
    all_gather x1, waiting for transfers between devices, per_device(): lax.all_gather(normed, 'mp', axis=1, tiled=True)  128 us
    reduce_scatter x1, waiting for transfers between devices, per_device(): lax.psum_scatter(contract(grad_preact, up_weight, 1, 1).astype(jnp.bfloat...  126 us
    reduce_sum x3, other arithmetic, kernel_terms(): collected.append(jnp.sum(window * grad_conv, axis=(0, 1, 2)))  121 us
    all_gather x1, waiting for transfers between devices, per_device(): grad_full = lax.all_gather(grad_rows, 'mp', axis=1, tiled=True)  118 us
    dot_general x4, matrix products, contract(): lax.dot_general(left, right, (((left_dim,), (right_dim,)), ((), ())), pre...  50.7 us
    reduce_sum x1, other arithmetic, per_device(): jnp.sum(usable * convolved * convolved, axis=(0, 1, 2))  44.6 us
    psum x1, waiting for transfers between devices, per_device(): lax.psum(up_local.astype(jnp.bfloat16), 'dp').astype(jnp.float32)  39.5 us
  transfers between devices with their start and end apart: 5, of which 4 were waited for; matrix products, arithmetic and copies ran while one was open for 31% of the time, Pallas kernels for 0%

commit v1 on v0

v1 whole, which is shorter than its diff:
```python
import functools

import jax
import jax.numpy as jnp
import numpy as np
from jax import lax
from jax.experimental import pallas as pl
from jax.experimental.pallas import tpu as pltpu
from jax.sharding import Mesh
from jax.sharding import PartitionSpec as P

F32 = jnp.float32
BF = jnp.bfloat16
EPSILON = 1e-05
INV_ROOT_TWO_PI = 0.3989422804014327
LANES = 128
LEFT = 8
MIB = 2**20
TILE = 256


def ceil_to(value, unit):
    return -(-value // unit) * unit


def lane_tiles(width):
    return -(-width // LANES)


def spread_rows(rows):
    count, width = rows.shape
    tiles = lane_tiles(width)
    flat = jnp.pad(rows.astype(F32), ((0, 0), (0, tiles * LANES - width)))
    flat = flat.reshape(count, tiles, 1, LANES).transpose(1, 0, 2, 3)
    return jnp.broadcast_to(flat, (tiles, count, 8, LANES))


def after(*values):
    return lax.optimization_barrier(values)


def params(mib, **more):
    return pltpu.CompilerParams(vmem_limit_bytes=mib * MIB, **more)


def cost(micros):
    return pl.CostEstimate(flops=int(micros * 1.15e9), bytes_accessed=0, transcendentals=0)


def clear_borders(dst, half, side):
    tiles, _, cols, _ = dst.shape
    for t in range(tiles):
        for r in list(range(half)) + list(range(half + side, side + 2 * half)):
            dst[t, r] = jnp.zeros((cols, LANES), F32)

        @pl.loop(0, side)
        def _(r):
            dst[t, r + half, 0:LEFT, :] = jnp.zeros((LEFT, LANES), F32)
            dst[t, r + half, LEFT + side : cols, :] = jnp.zeros((cols - LEFT - side, LANES), F32)


def fill_masked(dst, x_ref, m_ref, half):
    _, side, _, width = x_ref.shape
    for t in range(lane_tiles(width)):
        lo, hi = t * LANES, min((t + 1) * LANES, width)

        @pl.loop(0, side)
        def _(r):
            value = x_ref[0, r, :, lo:hi].astype(F32) * m_ref[0, r, :, : hi - lo].astype(F32)
            dst[t, r + half, LEFT : LEFT + side, 0 : hi - lo] = value


def conv_rows(src, w_ref, t, r0, c0, rows, groups, taps, flipped):
    half = taps // 2
    acc = [jnp.zeros((groups, 8, LANES), F32) for _ in range(rows)]
    for b in range(taps):
        shift = (taps - 1 - b) if flipped else b
        weights = [w_ref[t, a * taps + b] for a in range(taps)]
        for i in range(rows + taps - 1):
            x = src[t, r0 + i, pl.ds(LEFT + c0 + shift - half, groups * 8), :].reshape(groups, 8, LANES)
            for r in range(max(0, i - taps + 1), min(rows, i + 1)):
                a = taps - 1 - (i - r) if flipped else i - r
                acc[r] = acc[r] + x * weights[a][None]
    return acc


def forward_kernel(x_ref, m_ref, w_ref, conv_ref, stat_ref, xs, *, taps, rows, groups):
    _, side, _, width = x_ref.shape
    parts = conv_ref.shape[0]
    half = taps // 2
    clear_borders(xs, half, side)
    fill_masked(xs, x_ref, m_ref, half)
    for t in range(lane_tiles(width)):
        lo, hi = t * LANES, min((t + 1) * LANES, width)

        def block(i, carry):
            first, second = carry
            r0 = i * rows
            for c0 in range(0, side, groups * 8):
                acc = conv_rows(xs, w_ref, t, r0, c0, rows, groups, taps, False)
                for r in range(rows):
                    m = m_ref[0, r0 + r, c0 : c0 + groups * 8, :].astype(F32).reshape(groups, 8, LANES)
                    cm = acc[r] * m
                    first = first + jnp.sum(cm, axis=0)
                    second = second + jnp.sum(cm * acc[r], axis=0)
                    if rows % parts == 0:
                        part, row = r % parts, i * (rows // parts) + r // parts
                    else:
                        part, row = lax.rem(r0 + r, parts), lax.div(r0 + r, parts)
                    conv_ref[part, 0, row, c0 : c0 + groups * 8, lo:hi] = acc[r].reshape(groups * 8, LANES)[:, : hi - lo]
            return first, second

        zero = jnp.zeros((8, LANES), F32)
        first, second = lax.fori_loop(0, side // rows, block, (zero, zero))
        stat_ref[0, 0, t] = first
        stat_ref[0, 1, t] = second


def conv_forward(x, lane_mask, wide_taps, taps, parts, rows=12, groups=2):
    crops, side, _, width = x.shape
    tiles, half = lane_tiles(width), taps // 2
    return pl.pallas_call(
        functools.partial(forward_kernel, taps=taps, rows=rows, groups=groups),
        grid=(crops,),
        in_specs=[
            pl.BlockSpec((1, side, side, width), lambda n: (n, 0, 0, 0)),
            pl.BlockSpec((1, side, side, LANES), lambda n: (n, 0, 0, 0)),
            pl.BlockSpec(wide_taps.shape, lambda n: (0, 0, 0, 0)),
        ],
        out_specs=[
            pl.BlockSpec((parts, 1, side // parts, side, width), lambda n: (0, n, 0, 0, 0)),
            pl.BlockSpec((1, 2, tiles, 8, LANES), lambda n: (n, 0, 0, 0, 0)),
        ],
        out_shape=[
            jax.ShapeDtypeStruct((parts, crops, side // parts, side, width), F32),
            jax.ShapeDtypeStruct((crops, 2, tiles, 8, LANES), F32),
        ],
        scratch_shapes=[pltpu.VMEM((tiles, side + 2 * half, LEFT + side + 8, LANES), F32)],
        compiler_params=params(32),
        cost_estimate=cost(22),
        name="depthwise_forward",
    )(x, lane_mask, wide_taps)


def chooser(slot_of_cell, start, count):
    cells = slot_of_cell.shape[1]
    rows = lax.broadcasted_iota(jnp.int32, (count, cells), 0) + start
    return jnp.where(rows == slot_of_cell, 1.0, 0.0).astype(BF)


def nt(left, right):
    return lax.dot_general(left, right, (((1,), (1,)), ((), ())), preferred_element_type=F32)


def nn(left, right):
    return jnp.dot(left, right, preferred_element_type=F32)


def segments(base, over):
    return [
        (is_over, lo, lo + (base if is_over else 0), min(TILE, n - lo))
        for is_over, n in ((0, base), (1, over))
        for lo in range(0, n, TILE)
    ]


def pack_columns(k, values, slots, used, base_refs, over_refs):
    base, over = base_refs[0].shape[1], over_refs[0].shape[1]
    width = values.shape[0]
    for is_over, lo, start, count in segments(base, over):
        for j, ref in enumerate(over_refs if is_over else base_refs):

            @pl.when((k == j) & (start < used))
            def _():
                ref[:width, lo : lo + count] = nt(values, chooser(slots, start, count)).astype(BF)

            @pl.when((k == j) & (start >= used))
            def _():
                ref[:width, lo : lo + count] = jnp.zeros((width, count), BF)

            if width < ref.shape[0]:

                @pl.when(k == j)
                def _():
                    ref[width:, lo : lo + count] = jnp.zeros((ref.shape[0] - width, count), BF)


def packed_shapes(parts, width, base, over):
    wide = ceil_to(width, 8)
    specs = [pl.BlockSpec((wide, n), lambda k, at: (0, 0)) for n in (base, over) for _ in range(parts)]
    return specs, [jax.ShapeDtypeStruct((wide, n), BF) for n in (base, over) for _ in range(parts)]


def pack_normed_kernel(at_ref, conv_ref, vec_ref, slot_ref, *out_refs):
    k = pl.program_id(0)
    parts = len(out_refs) // 2
    normed = (conv_ref[0] * vec_ref[0:1, :] + vec_ref[1:2, :]).T.astype(BF)
    used = at_ref[1 + lax.rem(at_ref[0] + k, parts)]
    pack_columns(k, normed, slot_ref[0], used, out_refs[:parts], out_refs[parts:])


def pack_normed(at, conv, vec, slots, base, over):
    parts, cells, width = conv.shape
    part = lambda k, at: (lax.rem(at[0] + k, parts), 0, 0)
    specs, shapes = packed_shapes(parts, width, base, over)
    out = pl.pallas_call(
        pack_normed_kernel,
        grid_spec=pltpu.PrefetchScalarGridSpec(
            num_scalar_prefetch=1,
            grid=(parts,),
            in_specs=[
                pl.BlockSpec((1, cells, width), part),
                pl.BlockSpec(vec.shape, lambda k, at: (0, 0)),
                pl.BlockSpec((1, 1, cells), part),
            ],
            out_specs=specs,
        ),
        out_shape=shapes,
        compiler_params=params(32),
        cost_estimate=cost(8),
        name="pack_normed",
    )(at, conv, vec, slots)
    return out[:parts], out[parts:]


def pack_cotangent_kernel(at_ref, cot_ref, m_ref, slot_ref, *refs):
    out_refs, sum_ref, rows = refs[:-2], refs[-2], refs[-1]
    parts = len(out_refs) // 2
    crops, side, _, width = cot_ref.shape
    per = side // parts
    k = pl.program_id(0)
    part = lax.rem(at_ref[0] + k, parts)
    total = jnp.zeros((8, width), F32)
    for n in range(crops):

        def body(i, total):
            r = i * parts + part
            masks = [m_ref[n, r, :, : min(LANES, width - lo)] for lo in range(0, width, LANES)]
            mask = jnp.concatenate(masks, axis=1) if len(masks) > 1 else masks[0]
            value = cot_ref[n, r].astype(F32) * mask.astype(F32)
            rows[pl.ds(pl.multiple_of((n * per + i) * side, 8), side), :] = value
            return total + jnp.sum(value.reshape(side // 8, 8, width), axis=0)

        total = lax.fori_loop(0, per, body, total)

    @pl.when(k == 0)
    def _():
        sum_ref[...] = total

    @pl.when(k > 0)
    def _():
        sum_ref[...] += total

    pack_columns(k, rows[...].T.astype(BF), slot_ref[0], at_ref[1 + part], out_refs[:parts], out_refs[parts:])


def pack_cotangent(at, cot, lane_mask, slots, base, over):
    crops, side, _, width = cot.shape
    parts, _, cells = slots.shape
    specs, shapes = packed_shapes(parts, width, base, over)
    *out, sums = pl.pallas_call(
        pack_cotangent_kernel,
        grid_spec=pltpu.PrefetchScalarGridSpec(
            num_scalar_prefetch=1,
            grid=(parts,),
            in_specs=[
                pl.BlockSpec(cot.shape, lambda k, at: (0, 0, 0, 0)),
                pl.BlockSpec(lane_mask.shape, lambda k, at: (0, 0, 0, 0)),
                pl.BlockSpec((1, 1, cells), lambda k, at: (lax.rem(at[0] + k, parts), 0, 0)),
            ],
            out_specs=specs + [pl.BlockSpec((8, width), lambda k, at: (0, 0))],
            scratch_shapes=[pltpu.VMEM((cells, width), F32)],
        ),
        out_shape=shapes + [jax.ShapeDtypeStruct((8, width), F32)],
        compiler_params=params(40),
        cost_estimate=cost(10),
        name="pack_cotangent",
    )(at, cot, lane_mask, slots)
    return out[:parts], out[parts:], sums


def expand(base_ref, over_ref, slot_column, used, acc):
    cells, width = acc.shape
    acc[...] = jnp.zeros_like(acc)
    for is_over, lo, start, count in segments(base_ref.shape[1], over_ref.shape[1]):
        ref = over_ref if is_over else base_ref

        @pl.when(start < used)
        def _():
            lanes = lax.broadcasted_iota(jnp.int32, (cells, LANES), 1) + start
            choice = jnp.concatenate(
                [jnp.where(lanes + j == slot_column, 1.0, 0.0).astype(BF) for j in range(0, count, LANES)], axis=1
            )
            acc[...] += nt(choice, ref[:width, lo : lo + count])


def output_kernel(at_ref, x_ref, m_ref, bias_ref, column_ref, *refs):
    piece_refs, out_ref, acc = refs[:-2], refs[-2], refs[-1]
    parts = len(piece_refs) // 2
    _, side, _, width = x_ref.shape
    per = side // parts
    for k in range(parts):
        part = lax.rem(at_ref[0] + k, parts)
        expand(piece_refs[k], piece_refs[parts + k], column_ref[part, 0], at_ref[1 + part], acc)

        @pl.loop(0, per)
        def _(i):
            r = i * parts + part
            start = pl.multiple_of(i * side, 8)
            for lo in range(0, width, LANES):
                hi = min(lo + LANES, width)
                value = x_ref[0, r, :, lo:hi].astype(F32) + acc[pl.ds(start, side), lo:hi] + bias_ref[0:1, lo:hi]
                out_ref[0, r, :, lo:hi] = (m_ref[0, r, :, : hi - lo].astype(F32) * value).astype(BF)


def make_output(at, x, lane_mask, bias, columns, pieces):
    parts = len(pieces) // 2
    crops, side, _, width = x.shape
    cells = side * side // parts
    field = pl.BlockSpec((1, side, side, width), lambda n, at: (n, 0, 0, 0))
    return pl.pallas_call(
        output_kernel,
        grid_spec=pltpu.PrefetchScalarGridSpec(
            num_scalar_prefetch=1,
            grid=(crops,),
            in_specs=[
                field,
                pl.BlockSpec((1, side, side, LANES), lambda n, at: (n, 0, 0, 0)),
                pl.BlockSpec((1, width), lambda n, at: (0, 0)),
                pl.BlockSpec((parts, 1, cells, LANES), lambda n, at: (0, n, 0, 0)),
            ]
            + [pl.BlockSpec(p.shape, lambda n, at: (0, 0)) for p in pieces],
            out_specs=field,
            scratch_shapes=[pltpu.VMEM((cells, width), F32)],
        ),
        out_shape=jax.ShapeDtypeStruct(x.shape, BF),
        compiler_params=params(40),
        cost_estimate=cost(12),
        name="make_output",
    )(at, x, lane_mask, bias, columns, *pieces)


def backward_kernel(
    at_ref, x_ref, m_ref, cot_ref, conv_ref, w_ref, v_ref, column_ref, *refs, taps, rows, groups, rows2, groups2
):
    piece_refs, dx_ref, dw_ref, xs, gs, acc_ref = refs[:-5], refs[-5], refs[-4], refs[-3], refs[-2], refs[-1]
    parts = len(piece_refs) // 2
    _, side, _, width = x_ref.shape
    per = side // parts
    half = taps // 2

    @pl.when(pl.program_id(0) == 0)
    def _():
        dw_ref[...] = jnp.zeros_like(dw_ref)

    clear_borders(xs, half, side)
    clear_borders(gs, half, side)
    fill_masked(xs, x_ref, m_ref, half)
    for k in range(parts):
        part = lax.rem(at_ref[0] + k, parts)
        expand(piece_refs[k], piece_refs[parts + k], column_ref[part, 0], at_ref[1 + part], acc_ref)

        @pl.loop(0, per)
        def _(i):
            r = i * parts + part
            start = pl.multiple_of(i * side, 8)
            for t in range(lane_tiles(width)):
                lo, hi = t * LANES, min((t + 1) * LANES, width)
                n = hi - lo
                shape = (side // 8, 8, n)
                m = m_ref[0, r, :, :n].astype(F32).reshape(shape)
                centred = conv_ref[part, 0, i, :, lo:hi].reshape(shape) - v_ref[t, 0, :, :n][None]
                gn = acc_ref[pl.ds(start, side), lo:hi].reshape(shape)
                g = v_ref[t, 1, :, :n][None] * gn - m * (v_ref[t, 2, :, :n][None] + centred * v_ref[t, 3, :, :n][None])
                gs[t, r + half, LEFT : LEFT + side, 0:n] = g.reshape(side, n)

    for t in range(lane_tiles(width)):
        lo, hi = t * LANES, min((t + 1) * LANES, width)
        n = hi - lo

        @pl.loop(0, side // rows)
        def _(i):
            r0 = i * rows
            for c0 in range(0, side, groups * 8):
                acc = conv_rows(gs, w_ref, t, r0, c0, rows, groups, taps, True)
                for r in range(rows):
                    m = m_ref[0, r0 + r, c0 : c0 + groups * 8, :n].astype(F32)
                    cot = cot_ref[0, r0 + r, c0 : c0 + groups * 8, lo:hi].astype(F32)
                    value = m * (cot + acc[r].reshape(groups * 8, LANES)[:, :n])
                    dx_ref[0, r0 + r, c0 : c0 + groups * 8, lo:hi] = value.astype(BF)

        @pl.loop(0, side // rows2)
        def _(i):
            r0 = i * rows2
            for c0 in range(0, side, groups2 * 8):
                span = groups2 * 8
                grads = [
                    gs[t, r0 + half + r, LEFT + c0 : LEFT + c0 + span, :].reshape(groups2, 8, LANES)
                    for r in range(rows2)
                ]
                for b in range(taps):
                    acc = [jnp.zeros((groups2, 8, LANES), F32) for _ in range(taps)]
                    for j in range(rows2 + taps - 1):
                        x = xs[t, r0 + j, pl.ds(LEFT + c0 + b - half, span), :].reshape(groups2, 8, LANES)
                        for r in range(max(0, j - taps + 1), min(rows2, j + 1)):
                            acc[j - r] = acc[j - r] + x * grads[r]
                    for a in range(taps):
                        dw_ref[t, a * taps + b] += jnp.sum(acc[a], axis=0)


def conv_backward(
    at, x, lane_mask, cot, conv, wide_taps, vectors, columns, pieces, taps, rows=12, groups=2, rows2=8, groups2=2
):
    parts = len(pieces) // 2
    crops, side, _, width = x.shape
    tiles, half = lane_tiles(width), taps // 2
    cells = side * side // parts
    field = pl.BlockSpec((1, side, side, width), lambda n, at: (n, 0, 0, 0))
    padded = pltpu.VMEM((tiles, side + 2 * half, LEFT + side + 8, LANES), F32)
    return pl.pallas_call(
        functools.partial(
            backward_kernel, taps=taps, rows=rows, groups=groups, rows2=rows2, groups2=groups2
        ),
        grid_spec=pltpu.PrefetchScalarGridSpec(
            num_scalar_prefetch=1,
            grid=(crops,),
            in_specs=[
                field,
                pl.BlockSpec((1, side, side, LANES), lambda n, at: (n, 0, 0, 0)),
                field,
                pl.BlockSpec((parts, 1, side // parts, side, width), lambda n, at: (0, n, 0, 0, 0)),
                pl.BlockSpec(wide_taps.shape, lambda n, at: (0, 0, 0, 0)),
                pl.BlockSpec(vectors.shape, lambda n, at: (0, 0, 0, 0)),
                pl.BlockSpec((parts, 1, cells, LANES), lambda n, at: (0, n, 0, 0)),
            ]
            + [pl.BlockSpec(p.shape, lambda n, at: (0, 0)) for p in pieces],
            out_specs=[field, pl.BlockSpec(wide_taps.shape, lambda n, at: (0, 0, 0, 0))],
            scratch_shapes=[padded, padded, pltpu.VMEM((cells, width), F32)],
        ),
        out_shape=[jax.ShapeDtypeStruct(x.shape, BF), jax.ShapeDtypeStruct(wide_taps.shape, F32)],
        compiler_params=params(52),
        cost_estimate=cost(50),
        name="depthwise_backward",
    )(at, x, lane_mask, cot, conv, wide_taps, vectors, columns, *pieces)


def gelu_pair(value):
    size = jnp.abs(value)
    t = 1.0 / (1.0 + 0.23164189 * size)
    bell = jnp.exp(-0.5 * value * value)
    poly = 0.530702715
    for term in (-0.7265760135, 0.7107068705, -0.142248368, 0.127414796):
        poly = poly * t + term
    tail = poly * t * bell
    below = jnp.where(value >= 0, 1.0 - tail, tail)
    return value * below, below + value * bell * INV_ROOT_TWO_PI


def pointwise_kernel(at_ref, *refs, chips, parts, width, base, over):
    up_refs, down_refs = refs[:chips], refs[chips : 2 * chips]
    data, rest = refs[2 * chips : 2 * chips + 8], refs[2 * chips + 8 :]
    outs, (weight_grad_ref, sums_ref) = rest[:8], rest[8:10]
    up_w, down_w, up_t, down_t, up_acc, down_acc, x_place, g_place, hidden, grad_pre = rest[10:]
    whose, c = pl.program_id(0), pl.program_id(1)
    last = (whose == 1) & (c == pl.num_programs(1) - 1)
    _, slab, wide = up_refs[0].shape
    units = chips * parts * slab
    channels = parts * width
    block = units // 4
    me, chip = at_ref[0], at_ref[1 + 2 * parts]
    used = at_ref[1 + whose * parts + me]

    @pl.when((whose == 0) & (c == 0))
    def _():
        for refs, dst in ((up_refs, up_w), (down_refs, down_w)):
            for p in range(chips):
                for q in range(0, parts, 2):
                    pair = jnp.concatenate([refs[p][q].astype(F32), refs[p][q + 1].astype(F32)], axis=0)
                    row = (p * parts + q) * slab
                    dst[row : row + 2 * slab, :] = pair.astype(BF)
        for u in range(0, units, LANES):
            for src, dst in ((up_w, up_t), (down_w, down_t)):
                dst[:, u : u + LANES] = src[u : u + LANES, :].astype(F32).T[:channels, :].astype(BF)
        up_acc[...] = jnp.zeros_like(up_acc)
        down_acc[...] = jnp.zeros_like(down_acc)
        sums_ref[...] = jnp.zeros_like(sums_ref)
        ones = jnp.where(lax.broadcasted_iota(jnp.int32, (8, TILE), 0) == 0, 1.0, 0.0)
        x_place[channels:, :] = ones
        g_place[channels:, :] = jnp.zeros((8, TILE), F32)

    def spots(step):
        first, end = step * TILE, (step + 1) * TILE
        found = []
        if first < base:
            n = min(end, base) - first
            found.append((0, slice(0, n), slice(0, n)))
        if end > base and first < base + over:
            lo, hi = max(first, base), min(end, base + over)
            found.append((1, slice(lo - base, hi - base), slice(lo - first, hi - first)))
        return found

    whole = base // TILE
    steps = -(-(base + over) // TILE)
    cases = ([(c < whole, spots(0))] if whole else []) + [(c == step, spots(step)) for step in range(whole, steps)]
    for side in range(2):
        for case, found in cases:
            here = (whose == side) & case
            x_refs, g_refs = data[2 * side : 2 * side + 2], data[4 + 2 * side : 6 + 2 * side]

            @pl.when(here & (c * TILE < used))
            def _():
                for refs, place in ((x_refs, x_place), (g_refs, g_place)):
                    for k in range(parts):
                        at = pl.ds(pl.multiple_of(lax.rem(me - k + parts, parts) * width, 8), width)
                        values = [refs[is_over][k, :, lanes].astype(F32) for is_over, lanes, _ in found]
                        filled = sum(v.shape[1] for v in values)
                        if filled < TILE:
                            values.append(jnp.zeros((width, TILE - filled), F32))
                        place[at, :] = jnp.concatenate(values, axis=1) if len(values) > 1 else values[0]

            @pl.when(here & (c * TILE >= used))
            def _():
                for is_over, lanes, _ in found:
                    for ref in (outs[2 * side + is_over], outs[4 + 2 * side + is_over]):
                        ref[:, :, lanes] = jnp.zeros((parts, width, lanes.stop - lanes.start), ref.dtype)

    @pl.when(c * TILE < used)
    def _():
        x = x_place[...].astype(BF)
        g = g_place[...].astype(BF)

        @pl.loop(0, units // block)
        def _(i):
            at = pl.ds(pl.multiple_of(i * block, 16), block)
            pre = nn(up_w[at, :], x)
            grad_hidden = nn(down_w[at, :], g)
            value, slope = gelu_pair(pre)
            h = value.astype(BF)
            gp = (grad_hidden * slope).astype(BF)
            hidden[at, :] = h
            grad_pre[at, :] = gp
            up_acc[at, :] += nt(gp, x)
            down_acc[at, :] += nt(h, g)

        def fold(v):
            return sum(v[:, lo : lo + LANES] for lo in range(0, TILE, LANES))

        for s in range(parts):
            rows = slice(s * width, (s + 1) * width)
            k = lax.rem(me - s + parts, parts)
            branch = nn(down_t[rows, :], hidden[...])
            normed = nn(up_t[rows, :], grad_pre[...])
            sums_ref[0, rows, :] += fold(normed)
            sums_ref[1, rows, :] += fold(normed * x_place[rows, :])
            for side in range(2):
                for case, found in cases:

                    @pl.when((whose == side) & case)
                    def _():
                        for is_over, lanes, tile in found:
                            to = 2 * side + is_over
                            for value, ref in ((branch, outs[to]), (normed, outs[4 + to])):
                                ref[k, :, lanes] = value[:, tile].astype(ref.dtype)

    @pl.when(last)
    def _():
        for p in range(chips):
            for q in range(parts):
                row = (p * parts + q) * slab
                to = (chip ^ p, lax.rem(me - q + parts, parts))
                weight_grad_ref[to[0], to[1], 0] = up_acc[row : row + slab, :].astype(BF)
                weight_grad_ref[to[0], to[1], 1] = down_acc[row : row + slab, :].astype(BF)


def pointwise(at, ups, downs, data):
    chips = len(ups)
    parts, width, base = data[0].shape
    over = data[1].shape[2]
    _, slab, wide = ups[0].shape
    units, channels = chips * parts * slab, parts * width
    base_tiles = -(-base // TILE)

    def tile(side, is_over):
        if is_over:
            return pl.BlockSpec((parts, width, over), lambda whose, c, at: (0, 0, 0))

        def place(whose, c, at):
            return (0, 0, jnp.where(whose == side, jnp.minimum(c, base_tiles - 1), 0 if side else base_tiles - 1))

        return pl.BlockSpec((parts, width, TILE), place)

    tiles = [tile(side, is_over) for side in range(2) for is_over in range(2)]
    kinds = [F32, F32, BF, BF]
    result = [jax.ShapeDtypeStruct((parts, width, n), kind) for n, kind in zip((base, over, base, over), kinds)]
    return pl.pallas_call(
        functools.partial(pointwise_kernel, chips=chips, parts=parts, width=width, base=base, over=over),
        grid_spec=pltpu.PrefetchScalarGridSpec(
            num_scalar_prefetch=1,
            grid=(2, -(-(base + over) // TILE)),
            in_specs=[
                pl.BlockSpec(ups[0].shape, lambda w, c, at: (0, 0, 0), pipeline_mode=pl.Buffered(1))
                for _ in range(2 * chips)
            ]
            + tiles
            + tiles,
            out_specs=tiles
            + tiles
            + [
                pl.BlockSpec((chips, parts, 2, slab, wide), lambda w, c, at: (0, 0, 0, 0, 0)),
                pl.BlockSpec((2, channels, LANES), lambda w, c, at: (0, 0, 0)),
            ],
            scratch_shapes=[
                pltpu.VMEM((units, wide), BF),
                pltpu.VMEM((units, wide), BF),
                pltpu.VMEM((channels, units), BF),
                pltpu.VMEM((channels, units), BF),
                pltpu.VMEM((units, wide), F32),
                pltpu.VMEM((units, wide), F32),
                pltpu.VMEM((wide, TILE), F32),
                pltpu.VMEM((wide, TILE), F32),
                pltpu.VMEM((units, TILE), BF),
                pltpu.VMEM((units, TILE), BF),
            ],
        ),
        out_shape=result
        + result
        + [
            jax.ShapeDtypeStruct((chips, parts, 2, slab, wide), BF),
            jax.ShapeDtypeStruct((2, channels, LANES), F32),
        ],
        compiler_params=params(62),
        cost_estimate=cost(70),
        name="pointwise",
    )(at, *ups, *downs, *data)


def per_device(
    inputs,
    crop_sizes,
    land_mask,
    conv_weight,
    norm_gain,
    norm_shift,
    up_weight,
    up_bias,
    down_weight,
    down_bias,
    cotangent,
    *,
    sizes,
):
    chips, cores, parts = sizes
    crops, side, _, width = inputs.shape
    taps = conv_weight.shape[0]
    cells = crops * side * side // parts
    local_units = up_weight.shape[1]
    channels = up_weight.shape[0]
    me = lax.axis_index("mp")
    core = lax.axis_index("core")
    chip = lax.axis_index("xy")

    def ring(k):
        return [(i, (i + k) % parts) for i in range(parts)]

    def everywhere(value, axes):
        for axis in axes:
            size = {"xy": chips, "core": cores, "mp": parts}[axis]
            step = 1
            while step < size:
                value = value + lax.ppermute(value, axis, [(i, i ^ step) for i in range(size)])
                step *= 2
        return value

    def ring_back(k):
        return [(i, (i - k) % parts) for i in range(parts)]

    def to_parts(pieces, ring=ring):
        return [pieces[0]] + [lax.ppermute(pieces[k], "mp", ring(k)) for k in range(1, parts)]

    swap = [(i, cores - 1 - i) for i in range(cores)]

    def to_core(value):
        return lax.ppermute(value, "core", swap)

    share = -(-local_units // (chips * cores))
    slab = ceil_to(share, 8)
    wide_width = ceil_to(width, 8)
    wide = parts * wide_width + 8
    rank = chip * cores + core
    spare = chips * cores * share - local_units

    def take(rows):
        rows = jnp.pad(rows, ((0, spare), (0, 0))) if spare else rows
        rows = lax.dynamic_slice_in_dim(rows, rank * share, share, axis=0)
        if wide_width > width:
            rows = jnp.pad(rows.reshape(share, parts, width), ((0, 0), (0, 0), (0, wide_width - width)))
        return rows.reshape(share, -1)

    own_bias = up_bias[:, None]
    own_bias = jnp.pad(own_bias, ((0, spare), (0, 0))) if spare else own_bias
    own_bias = lax.dynamic_slice_in_dim(own_bias, rank * share, share, axis=0)
    up_rows = jnp.pad(jnp.concatenate([take(up_weight.T), own_bias], axis=1), ((0, slab - share), (0, 7)))
    down_rows = jnp.pad(take(down_weight), ((0, slab - share), (0, 8)))
    rows = to_parts([jnp.stack([up_rows, down_rows])] * parts)

    def over_plane(own, bits):
        held = {0: own}
        for bit in bits:
            pairs = [(i, i ^ bit) for i in range(chips)]
            held.update({p ^ bit: lax.ppermute(value, "xy", pairs) for p, value in list(held.items())})
        return [held[p] for p in range(chips)]

    index = jnp.arange(side, dtype=jnp.int32)
    inside = (index[None, :, None] < crop_sizes[:, 0][:, None, None]) & (
        index[None, None, :] < crop_sizes[:, 1][:, None, None]
    )
    usable = jnp.where(inside, land_mask, 0)
    lane_mask = jnp.broadcast_to(usable[..., None].astype(BF), usable.shape + (LANES,))
    by_part = usable.reshape(crops, side // parts, parts, side).transpose(2, 0, 1, 3).reshape(parts, -1, side)
    by_part = by_part.astype(F32)
    lines = by_part.shape[1]
    upto = jnp.dot(by_part, jnp.triu(jnp.ones((side, side), F32)))
    before = jnp.dot(upto[:, :, -1], jnp.triu(jnp.ones((lines, lines), F32), 1))
    slots = jnp.where(by_part > 0, upto + before[:, :, None] - 1, -1).astype(jnp.int32)
    counts = jnp.sum(by_part, axis=(1, 2)).astype(jnp.int32)
    columns = jnp.broadcast_to(slots.reshape(parts, crops, -1)[..., None], (parts, crops, cells // crops, LANES))
    slots = slots.reshape(parts, 1, cells)
    at = jnp.concatenate([me[None].astype(jnp.int32), counts, to_core(counts), chip[None].astype(jnp.int32)])

    base = ceil_to(cells * 7 // 9, LANES)
    over = ceil_to(cells, LANES) - base
    crowded = jnp.where(jnp.max(counts) > base, 1.0, 0.0)

    cot_base, cot_over, down_bias_local = pack_cotangent(at, cotangent, lane_mask, slots, base, over)
    inputs, *cot_base = after(inputs, *cot_base)

    wide_taps = spread_rows(conv_weight.reshape(taps * taps, width))
    convolved, stats = conv_forward(inputs, lane_mask, wide_taps, taps, parts)
    stats, *rows = after(stats, *rows)
    grad_pieces = to_parts(cot_base)
    bits = [1 << j for j in range(chips.bit_length() - 1)]

    def double(held, bit):
        pairs = [(i, i ^ bit) for i in range(chips)]
        return {**held, **{p ^ bit: lax.ppermute(value, "xy", pairs) for p, value in held.items()}}

    ups, downs = {0: jnp.stack([r[0] for r in rows])}, {0: jnp.stack([r[1] for r in rows])}
    ups, downs = double(ups, bits[0]), double(downs, bits[-1])
    stats = jnp.sum(stats, axis=(0, 3)).reshape(2, -1)[:, :width]
    extra = jnp.pad(jnp.stack([jnp.sum(by_part), crowded])[None], ((0, 0), (0, width - 2)))
    stats = everywhere(jnp.concatenate([stats, extra, jnp.sum(down_bias_local, axis=0)[None]]), ("core", "xy"))
    ocean_count = stats[2, 0]
    overflows = stats[2, 1] > 0
    down_bias_grad = stats[3]
    channel_mean = stats[0] / ocean_count
    inv_std = lax.rsqrt(stats[1] / ocean_count - channel_mean * channel_mean + EPSILON)
    gain = norm_gain.astype(F32)
    shift = norm_shift.astype(F32)
    scale = gain * inv_std

    affine = jnp.stack([scale, shift - channel_mean * scale])
    places = sorted(ups), sorted(downs)
    convolved, *held = after(convolved, *[ups[p] for p in places[0]], *[downs[p] for p in places[1]])
    ups = dict(zip(places[0], held))
    downs = dict(zip(places[1], held[len(ups) :]))
    for j in range(1, len(bits)):
        ups, downs = double(ups, bits[j]), double(downs, bits[-1 - j])
    ups, downs = [ups[p] for p in range(chips)], [downs[p] for p in range(chips)]
    normed_base, normed_over = pack_normed(at, convolved.reshape(parts, cells, width), affine, slots, base, over)
    *both, = after(*normed_base, *grad_pieces)
    normed_base, grad_base = both[:parts], jnp.stack(both[parts:])
    x_base = jnp.stack(to_parts(normed_base))
    none = jnp.zeros((parts, wide_width, over), BF)

    def overflow_in():
        x, g = jnp.stack(to_parts(normed_over)), jnp.stack(to_parts(cot_over))
        return x, g, to_core(x), to_core(g)

    x_over, g_over, x_far_over, g_far_over = lax.cond(overflows, overflow_in, lambda: (none,) * 4)
    data = [x_base, x_over, to_core(x_base), x_far_over, grad_base, g_over, to_core(grad_base), g_far_over]
    *sums_out, weight_grad, sums = pointwise(at, ups, downs, data)
    branch, normed = list(sums_out[:4]), list(sums_out[4:])

    def home(own, far):
        total = (own + to_core(far).astype(F32)).astype(BF)
        return to_parts([total[k] for k in range(parts)], ring_back)

    normed_base = home(normed[0], normed[2])
    branch[0], branch[2], _ = after(branch[0], branch[2], normed_base[-1])
    branch_base = home(branch[0], branch[2])
    nothing = [jnp.zeros((wide_width, over), BF)] * parts
    branch_over, normed_over = lax.cond(
        overflows, lambda: (home(branch[1], branch[3]), home(normed[1], normed[3])), lambda: (nothing, nothing)
    )

    sums = everywhere(jnp.sum(sums, axis=2), ("core", "xy", "mp"))
    sums = lax.dynamic_slice_in_dim(sums, me * wide_width, wide_width, axis=1)[:, :width]
    shift_grad = sums[0]
    gain_grad = (sums[1] - shift * shift_grad) / gain
    vectors = jnp.stack([channel_mean, scale, scale * shift_grad / ocean_count, scale * inv_std * gain_grad / ocean_count])
    input_grad, taps_local = conv_backward(
        at,
        inputs,
        lane_mask,
        cotangent,
        convolved,
        wide_taps,
        spread_rows(vectors),
        columns,
        [*normed_base, *normed_over],
        taps,
    )
    output = make_output(at, inputs, lane_mask, down_bias.astype(F32)[None], columns, [*branch_base, *branch_over])
    taps_local = jnp.sum(taps_local, axis=2).transpose(1, 0, 2).reshape(taps * taps, -1)
    conv_weight_grad = everywhere(taps_local, ("core", "xy"))[:, :width].reshape(taps, taps, width)

    own = lax.psum_scatter(weight_grad, "xy", scatter_dimension=0, tiled=False)
    own, _ = after(own, taps_local)
    own = lax.psum_scatter(own, "mp", scatter_dimension=0, tiled=False)
    both = lax.all_gather(own, ("xy", "core"), axis=0, tiled=False)
    both = both[:, :, :share].transpose(1, 0, 2, 3).reshape(2, -1, wide)[:, :local_units]
    up_bias_grad = both[0, :, -8].astype(F32)
    both = both[:, :, :-8].reshape(2, local_units, parts, wide_width)[..., :width].reshape(2, local_units, channels)
    up_weight_grad = both[0].T.astype(F32)
    down_weight_grad = both[1].astype(F32)
    return (
        output,
        input_grad,
        conv_weight_grad,
        gain_grad,
        shift_grad,
        up_weight_grad,
        up_bias_grad,
        down_weight_grad,
        down_bias_grad,
    )


def solution(mesh):
    cores = 2
    parts = mesh.shape["mp"]
    chips = mesh.shape["dp"] // cores
    fine = Mesh(np.asarray(mesh.devices).reshape(chips, cores, parts), ("xy", "core", "mp"))
    dp = ("xy", "core")
    specs = (
        P(dp, None, None, "mp"),
        P(dp, None),
        P(dp, None, None),
        P(None, None, "mp"),
        P("mp"),
        P("mp"),
        P(None, "mp"),
        P("mp"),
        P("mp", None),
        P("mp"),
        P(dp, None, None, "mp"),
    )
    results = (
        P(dp, None, None, "mp"),
        P(dp, None, None, "mp"),
        P(None, None, "mp"),
        P("mp"),
        P("mp"),
        P(None, "mp"),
        P("mp"),
        P("mp", None),
        P("mp"),
    )
    return jax.shard_map(
        functools.partial(per_device, sizes=(chips, cores, parts)),
        mesh=fine,
        in_specs=specs,
        out_specs=results,
        check_vma=False,
    )
```

time: 911 us -> 480 us (0.53)
  other arithmetic: 327 us -> 18.5 us
  waiting for transfers between devices: 411 us -> 178 us
  Pallas kernels: 0 us -> 163 us
  matrix products: 78 us -> 0.32 us
  blocking collectives: 53.4 us -> 0 us
  starting transfers between devices: 0.9 us -> 49.8 us
  local copies, waits for them, and re-layouts: 21.6 us -> 47.1 us
    all_gather x2 -> x1, waiting for transfers between devices: 246 us -> 0.01 us  [per_device(): both = lax.all_gather(own, ('xy', 'core'), axis=0, tiled=False)]
    reduce_sum x7 -> x6, other arithmetic: 172 us -> 2.32 us  [the longest x1 1.46 us: per_device(): sums = everywhere(jnp.sum(sums, axis=2), ('core', 'xy', 'mp'))]
    pallas_call x0 -> x6, Pallas kernels: none -> 163 us  [the longest x1 64.5 us: pointwise(): pl.pallas_call(functools.partial(pointwise_kernel, chips=chips, parts=par...]
    convert_element_type x11 -> x7, other arithmetic: 154 us -> 7.77 us  [the longest x2 3.88 us: home(): total = (own + to_core(far).astype(F32)).astype(BF)]
    ppermute x0 -> x37, waiting for transfers between devices: none -> 146 us  [the longest x15 63.7 us: to_parts(): lax.ppermute(pieces[k], 'mp', ring(k))]
    reduce_scatter x2 -> x1, waiting for transfers between devices: 126 us -> 31.8 us  [per_device(): own = lax.psum_scatter(own, 'mp', scatter_dimension=0, tiled=False)]
    dot_general x6 -> x2, matrix products: 78 us -> 0.32 us  [the longest x1 0.19 us: per_device(): upto = jnp.dot(by_part, jnp.triu(jnp.ones((side, side), F32)))]
    psum x3 -> x0, blocking collectives: 53.4 us -> none  [the longest x1 23.4 us: per_device(): conv_weight_grad = lax.psum(kernel_local, 'dp')]
  transfers between devices with their start and end apart: 5 -> 40, of which waited for: 4 -> 21; matrix products, arithmetic and copies ran while one was open for 31% -> 7% of each run, Pallas kernels for 0% -> 21%
where the time goes in v1:
time: 480 us; the launch traced here: 472 us
  waiting for transfers between devices  178 us (37%)
  Pallas kernels  163 us (34%)
  starting transfers between devices  49.8 us (10%)
  local copies, waits for them, and re-layouts  47.1 us (10%)
  other arithmetic  18.5 us (4%)
  between operations  16 us (3%)
    pallas_call x1, Pallas kernels, pointwise(): pl.pallas_call(functools.partial(pointwise_kernel, chips=chips, parts=par...  64.5 us
    ppermute x15, waiting for transfers between devices, to_parts(): lax.ppermute(pieces[k], 'mp', ring(k))  63.7 us
    pallas_call x1, Pallas kernels, conv_backward(): pl.pallas_call(functools.partial(backward_kernel, taps=taps, rows=rows, g...  49.7 us
    ppermute x6, waiting for transfers between devices, double(): lax.ppermute(value, 'xy', pairs)  45.9 us
    ppermute x11, waiting for transfers between devices, everywhere(): lax.ppermute(value, axis, [(i, i ^ step) for i in range(size)])  33.4 us
    reduce_scatter x1, waiting for transfers between devices, per_device(): own = lax.psum_scatter(own, 'mp', scatter_dimension=0, tiled=False)  31.8 us
    ppermute x15, starting transfers between devices, to_parts(): lax.ppermute(pieces[k], 'mp', ring(k))  23.8 us
    pallas_call x1, Pallas kernels, conv_forward(): pl.pallas_call(functools.partial(forward_kernel, taps=taps, rows=rows, gr...  22 us
  transfers between devices with their start and end apart: 40, of which 21 were waited for; matrix products, arithmetic and copies ran while one was open for 7% of the time, Pallas kernels for 21%

profile of v1, /device:TPU:0, one launch (start us, length us, event | category | flops | bytes accessed | tf_op | source)
XLA Modules:
  0.0 472.3 jit_solution(16466711280864544598)
XLA Ops:
  11.6 3.0 collective-permute-start.17
  25.2 8.8 %pack_cotangent.1 = (bf16[200,896]{1,0:T(8,128)(2,1)S(1)}, bf16[200,896]{1,0:T(8,128)(2,1)S(1)}, bf16[200,896]{1,0:T(8,128)(2,1)S(1)}, bf16[200,896]{1,0:T(8,128...) custom-call(s32[10]{0:T(128)S(1)} %pad_add_fusion.at_ref, ...), custom_call_target="tpu_custom_call" | custom-call | flops 11500000256 | tf_op jit(solution)/shard_map/pack_cotangent/pallas_call | solution.py:261
  36.7 22.0 %depthwise_forward.1 = (f32[4,2,12,48,200]{4,3,2,1,0:T(8,128)S(1)}, f32[2,2,2,8,128]{4,3,2,1,0:T(8,128)S(1)}) custom-call(bf16[2,48,48,200]{3,2,1,0:T(8,128)(2,1)S(1)} %copy-done.10, bf16[2,48,48,128]{3,2,1,0:T(8,128)(2,1)S(1)} %broadcast_in_dim.80.m_ref, f32[2,49,8,128]{3,2,1,0:T(8,128)S(1)} %broadcast_in_dim.91.w_ref), custom_call_target="tpu_custom_call" | custom-call | flops 25300000768 | tf_op jit(solution)/shard_map/depthwise_forward/pallas_call | solution.py:122
  60.9 3.3 collective-permute-start.31
  69.4 3.2 collective-permute-start.21
  74.4 14.8 %collective-permute-done.28 = f32[4,200]{1,0:T(4,128)S(1)} collective-permute-done((f32[4,200]{1,0:T(4,128)S(1)}, f32[4,200]{1,0:T(4,128)S(1)}, u32[]{:S(2)}, u32[]{:S(2)}) %collective-permute-start.28) | collective-permute-done | bytes 3232 | tf_op jit(solution)/shard_map/ppermute | solution.py:670
  92.7 14.2 %collective-permute-done.20.refs_1_ = bf16[4,104,808]{2,1,0:T(8,128)(2,1)S(1)} collective-permute-done((bf16[4,104,808]{2,1,0:T(8,128)(2,1)S(1)}, bf16[4,104,808]{2,1,0:T(8,128)(2,1)S(1)}, u32[]{:S(2)}, u32[]{:S(2)}) %collective-permute-start.20) | collective-permute-done | bytes 672288 | tf_op jit(solution)/shard_map/ppermute | solution.py:745
  107.9 6.7 %pack_normed.1 = (bf16[200,896]{1,0:T(8,128)(2,1)S(1)}, bf16[200,896]{1,0:T(8,128)(2,1)S(1)}, bf16[200,896]{1,0:T(8,128)(2,1)S(1)}, bf16[200,896]{1,0:T(8,128)(2...) custom-call(s32[10]{0:T(128)S(1)} %pad_add_fusion.at_ref, ...), custom_call_target="tpu_custom_call" | custom-call | flops 9200000000 | tf_op jit(solution)/shard_map/pack_normed/pallas_call | solution.py:206
  114.6 3.2 conditional.2
  120.0 2.7 collective-permute-start.34
  124.2 6.8 %collective-permute-done.32 = bf16[200,896]{1,0:T(8,128)(2,1)S(1)} collective-permute-done((bf16[200,896]{1,0:T(8,128)(2,1)S(1)}, bf16[200,896]{1,0:T(8,128)(2,1)S(1)}, u32[]{:S(2)}, u32[]{:S(2)}) %collective-permute-start.32) | collective-permute-done | bytes 358432 | tf_op jit(solution)/shard_map/ppermute | solution.py:678
  131.1 12.6 %collective-permute-done.33 = bf16[200,896]{1,0:T(8,128)(2,1)S(1)} collective-permute-done((bf16[200,896]{1,0:T(8,128)(2,1)S(1)}, bf16[200,896]{1,0:T(8,128)(2,1)S(1)}, u32[]{:S(2)}, u32[]{:S(2)}) %collective-permute-start.33) | collective-permute-done | bytes 358432 | tf_op jit(solution)/shard_map/ppermute | solution.py:678
  148.1 16.2 %collective-permute-done.22.refs_2_ = bf16[4,104,808]{2,1,0:T(8,128)(2,1)S(1)} collective-permute-done((bf16[4,104,808]{2,1,0:T(8,128)(2,1)S(1)}, bf16[4,104,808]{2,1,0:T(8,128)(2,1)S(1)}, u32[]{:S(2)}, u32[]{:S(2)}) %collective-permute-start.22) | collective-permute-done | bytes 672288 | tf_op jit(solution)/shard_map/ppermute | solution.py:745
  165.5 13.7 %collective-permute-done.23.refs_3_ = bf16[4,104,808]{2,1,0:T(8,128)(2,1)S(1)} collective-permute-done((bf16[4,104,808]{2,1,0:T(8,128)(2,1)S(1)}, bf16[4,104,808]{2,1,0:T(8,128)(2,1)S(1)}, u32[]{:S(2)}, u32[]{:S(2)}) %collective-permute-start.23) | collective-permute-done | bytes 672288 | tf_op jit(solution)/shard_map/ppermute | solution.py:745
  183.3 64.5 %pointwise.1 = (f32[4,200,896]{2,1,0:T(8,128)}, f32[4,200,256]{2,1,0:T(8,128)}, bf16[4,200,896]{2,1,0:T(8,128)(2,1)}, bf16[4,200,256]{2,1,0:T(8,128)(2,1)}, f32[...) custom-call(s32[10]{0:T(128)} %copy-done.7, ...), custom_call_target="tpu_custom_call" | custom-call | flops 80499998720 | tf_op jit(solution)/shard_map/pointwise/pallas_call | solution.py:595
  247.9 4.6 conditional.3
  255.7 3.6 collective-permute-done.44
  263.0 8.6 %collective-permute-start.46 = (f32[2,800]{1,0:T(2,128)S(1)}, f32[2,800]{1,0:T(2,128)S(1)}, u32[]{:S(2)}, u32[]{:S(2)}) collective-permute-start(f32[2,800]{1,0:T(2,128)S(1)} %add.109), channel_id=1, source_target_pairs={{0,1},{1,0},{2,3},{3,2},{4,5},{5,4},{6,7},{7,6},{8,9},{9,8},{10,11... | collective-permute-start | bytes 19208 | tf_op jit(solution)/shard_map/ppermute | solution.py:670
  274.3 3.4 collective-permute-done.47
  284.9 7.9 %collective-permute-done.38.refs_3_ = bf16[200,896]{1,0:T(8,128)(2,1)S(1)} collective-permute-done((bf16[200,896]{1,0:T(8,128)(2,1)S(1)}, bf16[200,896]{1,0:T(8,128)(2,1)S(1)}, u32[]{:S(2)}, u32[]{:S(2)}) %collective-permute-start.38) | collective-permute-done | bytes 358432 | tf_op jit(solution)/shard_map/ppermute | solution.py:678
  292.8 5.2 %collective-permute-done.48.refs_1_ = bf16[200,896]{1,0:T(8,128)(2,1)S(1)} collective-permute-done((bf16[200,896]{1,0:T(8,128)(2,1)S(1)}, bf16[200,896]{1,0:T(8,128)(2,1)S(1)}, u32[]{:S(2)}, u32[]{:S(2)}) %collective-permute-start.48) | collective-permute-done | bytes 358432 | tf_op jit(solution)/shard_map/ppermute | solution.py:678
  297.9 13.7 %collective-permute-done.49.refs_2_ = bf16[200,896]{1,0:T(8,128)(2,1)S(1)} collective-permute-done((bf16[200,896]{1,0:T(8,128)(2,1)S(1)}, bf16[200,896]{1,0:T(8,128)(2,1)S(1)}, u32[]{:S(2)}, u32[]{:S(2)}) %collective-permute-start.49) | collective-permute-done | bytes 358432 | tf_op jit(solution)/shard_map/ppermute | solution.py:678
  313.9 49.7 %depthwise_backward.1 = (bf16[2,48,48,200]{3,2,1,0:T(8,128)(2,1)}, f32[2,49,8,128]{3,2,1,0:T(8,128)S(1)}) custom-call(s32[10]{0:T(128)S(1)} %copy-done.8, bf16[2,48,48,200]{3,2,1,0:T(8,128)(2,1)} %x_ref.2, bf16[2,48,48,128]{3,2,1,0:T(8,128)(2,1)} %copy-done.3, bf16[2,48,48,200]{3,2,1,0:T(8,128)(2,1)} %cot_ref.3, f32[4,2,12,48,200]{4,3,2,1,0:T(8,128)} %copy-done.12, ...), custom_call_target="tpu_custom_call" | custom-call | flops 57500000256 | tf_op jit(solution)/shard_map/depthwise_backward/pallas_call | solution.py:420
  364.6 31.8 %reduce-scatter.5.cloned.1.call-done = bf16[1,2,104,808]{3,2,1,0:T(8,128)(2,1)} async-done(((bf16[4,2,104,808]{3,2,1,0:T(8,128)(2,1)}), bf16[1,2,104,808]{3,2,1,0:T(8,128)(2,1)}) %reduce-scatter.5.cloned.1.call-update) | async-done | bytes 336144 | tf_op jit(solution)/shard_map/reduce_scatter | solution.py:819
  396.9 2.8 collective-permute-done.39
  409.0 3.6 collective-permute-done.51
  414.2 2.7 collective-permute-done.52
  419.1 17.4 %collective-permute-done.41.refs_2_ = bf16[200,896]{1,0:T(8,128)(2,1)} collective-permute-done((bf16[200,896]{1,0:T(8,128)(2,1)}, bf16[200,896]{1,0:T(8,128)(2,1)}, u32[]{:S(2)}, u32[]{:S(2)}) %collective-permute-start.41) | collective-permute-done | bytes 358432 | tf_op jit(solution)/shard_map/ppermute | solution.py:678
  439.2 11.2 %make_output.1 = bf16[2,48,48,200]{3,2,1,0:T(8,128)(2,1)} custom-call(s32[10]{0:T(128)S(1)} %copy-done.8, bf16[2,48,48,200]{3,2,1,0:T(8,128)(2,1)S(1)} %copy-done.11, bf16[2,48,48,128]{3,2,1,0:T(8,128)(2,1)S(1)} %copy-done.4, f32[1,200]{1,0:T(1,128)S(1)} %bitcast.121, s32[4,2,576,128]{3,2,1,0:T(8,128)S(1)} %copy-done.2, bf16[200,896]{1,0:T(8,128)(2,1)S(1)} %copy-done.6, ...), custom_call_target="tpu_custom_call" | custom-call | flops 13799999488 | tf_op jit(solution)/shard_map/make_output/pallas_call | solution.py:321
  454.3 3.2 reshape.128
  457.5 2.9 fusion
  461.2 4.2 copy.49
  (240 shorter events, 91.6 us)
Async XLA Ops:
  7.2 357.3 %reduce-scatter.7.cloned.1.call-start = ((), (), s32[]{:S(2)}) async-start(), calls=%async_computation.4 | async-start | bytes 7454720
  11.6 49.3 %collective-permute-start.17 = (bf16[2,104,808]{2,1,0:T(8,128)(2,1)}, bf16[2,104,808]{2,1,0:T(8,128)(2,1)}, u32[]{:S(2)}, u32[]{:S(2)}) collective-permute-start(bf16[2,104,808]{2,1,0:T(8,128)(2,1)} %pad_maximum_fusion.6), channel_id=1, source_target_pairs={{0,1},{1,2},{2,3},{3,0},{4,5},{5,6},{6,7},{7,4},{8,9},{9,10},{10,1... | collective-permute-start | bytes 1008392 | tf_op jit(solution)/shard_map/ppermute | solution.py:678
  14.7 49.6 %collective-permute-start.18 = (bf16[2,104,808]{2,1,0:T(8,128)(2,1)}, bf16[2,104,808]{2,1,0:T(8,128)(2,1)}, u32[]{:S(2)}, u32[]{:S(2)}) collective-permute-start(bf16[2,104,808]{2,1,0:T(8,128)(2,1)} %pad_maximum_fusion.6), channel_id=1, source_target_pairs={{0,2},{1,3},{2,0},{3,1},{4,6},{5,7},{6,4},{7,5},{8,10},{9,11},{10,... | collective-permute-start | bytes 1008392 | tf_op jit(solution)/shard_map/ppermute | solution.py:678
  17.2 47.0 %collective-permute-start.19 = (bf16[2,104,808]{2,1,0:T(8,128)(2,1)}, bf16[2,104,808]{2,1,0:T(8,128)(2,1)}, u32[]{:S(2)}, u32[]{:S(2)}) collective-permute-start(bf16[2,104,808]{2,1,0:T(8,128)(2,1)} %pad_maximum_fusion.6), channel_id=1, source_target_pairs={{0,3},{1,0},{2,1},{3,2},{4,7},{5,4},{6,5},{7,6},{8,11},{9,8},{10,9... | collective-permute-start | bytes 1008392 | tf_op jit(solution)/shard_map/ppermute | solution.py:678
  34.0 80.6 %collective-permute-start.29 = (bf16[200,896]{1,0:T(8,128)(2,1)S(1)}, bf16[200,896]{1,0:T(8,128)(2,1)}, u32[]{:S(2)}, u32[]{:S(2)}) collective-permute-start(bf16[200,896]{1,0:T(8,128)(2,1)S(1)} %get-tuple-element.137), channel_id=1, source_target_pairs={{0,1},{1,2},{2,3},{3,0},{4,5},{5,6},{6,7},{7,4},{8,9},{9,10},{10,1... | collective-permute-start | bytes 1075208 | tf_op jit(solution)/shard_map/ppermute | solution.py:678
  34.7 79.9 %collective-permute-start.30 = (bf16[200,896]{1,0:T(8,128)(2,1)S(1)}, bf16[200,896]{1,0:T(8,128)(2,1)}, u32[]{:S(2)}, u32[]{:S(2)}) collective-permute-start(bf16[200,896]{1,0:T(8,128)(2,1)S(1)} %get-tuple-element.138), channel_id=1, source_target_pairs={{0,2},{1,3},{2,0},{3,1},{4,6},{5,7},{6,4},{7,5},{8,10},{9,11},{10,... | collective-permute-start | bytes 1075208 | tf_op jit(solution)/shard_map/ppermute | solution.py:678
  60.9 53.7 %collective-permute-start.31 = (bf16[200,896]{1,0:T(8,128)(2,1)S(1)}, bf16[200,896]{1,0:T(8,128)(2,1)}, u32[]{:S(2)}, u32[]{:S(2)}) collective-permute-start(bf16[200,896]{1,0:T(8,128)(2,1)S(1)} %get-tuple-element.139), channel_id=1, source_target_pairs={{0,3},{1,0},{2,1},{3,2},{4,7},{5,4},{6,5},{7,6},{8,11},{9,8},{10,9... | collective-permute-start | bytes 1075208 | tf_op jit(solution)/shard_map/ppermute | solution.py:678
  64.3 4.7 %collective-permute-start.26 = (f32[4,200]{1,0:T(4,128)S(1)}, f32[4,200]{1,0:T(4,128)S(1)}, u32[]{:S(2)}, u32[]{:S(2)}) collective-permute-start(f32[4,200]{1,0:T(4,128)S(1)} %fusion.22), channel_id=1, source_target_pairs={{0,4},{4,0},{1,5},{5,1},{2,6},{6,2},{3,7},{7,3},{8,12},{12,8},{9,1... | collective-permute-start | bytes 9608 | tf_op jit(solution)/shard_map/ppermute | solution.py:670
  69.4 23.3 %collective-permute-start.21 = (bf16[4,104,808]{2,1,0:T(8,128)(2,1)S(1)}, bf16[4,104,808]{2,1,0:T(8,128)(2,1)S(1)}, u32[]{:S(2)}, u32[]{:S(2)}) collective-permute-start(bf16[4,104,808]{2,1,0:T(8,128)(2,1)S(1)} %pad_maximum_fusion.5.refs_4_), channel_id=1, source_target_pairs={{0,16},{8,24},{16,0},{24,8},{1,17},{9,25},{17,1},{25,9},{2,18},{10... | collective-permute-start | bytes 2016776 | tf_op jit(solution)/shard_map/ppermute | solution.py:745
  72.8 16.5 %collective-permute-start.28 = (f32[4,200]{1,0:T(4,128)S(1)}, f32[4,200]{1,0:T(4,128)S(1)}, u32[]{:S(2)}, u32[]{:S(2)}) collective-permute-start(f32[4,200]{1,0:T(4,128)S(1)} %add.101), channel_id=1, source_target_pairs={{0,16},{8,24},{16,0},{24,8},{1,17},{9,25},{17,1},{25,9},{2,18},{10... | collective-permute-start | bytes 9608 | tf_op jit(solution)/shard_map/ppermute | solution.py:670
  89.2 17.7 %collective-permute-start.20 = (bf16[4,104,808]{2,1,0:T(8,128)(2,1)S(1)}, bf16[4,104,808]{2,1,0:T(8,128)(2,1)S(1)}, u32[]{:S(2)}, u32[]{:S(2)}) collective-permute-start(bf16[4,104,808]{2,1,0:T(8,128)(2,1)S(1)} %pad_maximum_fusion.4.refs_0_), channel_id=1, source_target_pairs={{0,8},{8,0},{16,24},{24,16},{1,9},{9,1},{17,25},{25,17},{2,10},{10... | collective-permute-start | bytes 2016776 | tf_op jit(solution)/shard_map/ppermute | solution.py:745
  117.8 13.2 %collective-permute-start.32 = (bf16[200,896]{1,0:T(8,128)(2,1)S(1)}, bf16[200,896]{1,0:T(8,128)(2,1)S(1)}, u32[]{:S(2)}, u32[]{:S(2)}) collective-permute-start(bf16[200,896]{1,0:T(8,128)(2,1)S(1)} %get-tuple-element.141), channel_id=1, source_target_pairs={{0,1},{1,2},{2,3},{3,0},{4,5},{5,6},{6,7},{7,4},{8,9},{9,10},{10,1... | collective-permute-start | bytes 1075208 | tf_op jit(solution)/shard_map/ppermute | solution.py:678
  120.0 23.7 %collective-permute-start.33 = (bf16[200,896]{1,0:T(8,128)(2,1)S(1)}, bf16[200,896]{1,0:T(8,128)(2,1)S(1)}, u32[]{:S(2)}, u32[]{:S(2)}) collective-permute-start(bf16[200,896]{1,0:T(8,128)(2,1)S(1)} %get-tuple-element.142), channel_id=1, source_target_pairs={{0,2},{1,3},{2,0},{3,1},{4,6},{5,7},{6,4},{7,5},{8,10},{9,11},{10,... | collective-permute-start | bytes 1075208 | tf_op jit(solution)/shard_map/ppermute | solution.py:678
  120.0 23.7 %collective-permute-start.34 = (bf16[200,896]{1,0:T(8,128)(2,1)S(1)}, bf16[200,896]{1,0:T(8,128)(2,1)S(1)}, u32[]{:S(2)}, u32[]{:S(2)}) collective-permute-start(bf16[200,896]{1,0:T(8,128)(2,1)S(1)} %get-tuple-element.143), channel_id=1, source_target_pairs={{0,3},{1,0},{2,1},{3,2},{4,7},{5,4},{6,5},{7,6},{8,11},{9,8},{10,9... | collective-permute-start | bytes 1075208 | tf_op jit(solution)/shard_map/ppermute | solution.py:678
  124.1 56.9 %collective-permute-start.36 = (bf16[4,200,896]{2,1,0:T(8,128)(2,1)S(1)}, bf16[4,200,896]{2,1,0:T(8,128)(2,1)S(1)}, u32[]{:S(2)}, u32[]{:S(2)}) collective-permute-start(bf16[4,200,896]{2,1,0:T(8,128)(2,1)S(1)} %pad_maximum_fusion.3.refs_12_), channel_id=1, source_target_pairs={{0,4},{4,0},{1,5},{5,1},{2,6},{6,2},{3,7},{7,3},{8,12},{12,8},{9,1... | collective-permute-start | bytes 4300808 | tf_op jit(solution)/shard_map/ppermute | solution.py:683
  143.9 37.1 %collective-permute-start.35 = (bf16[4,200,896]{2,1,0:T(8,128)(2,1)S(1)}, bf16[4,200,896]{2,1,0:T(8,128)(2,1)S(1)}, u32[]{:S(2)}, u32[]{:S(2)}) collective-permute-start(bf16[4,200,896]{2,1,0:T(8,128)(2,1)S(1)} %pad_maximum_fusion.2.refs_8_), channel_id=1, source_target_pairs={{0,4},{4,0},{1,5},{5,1},{2,6},{6,2},{3,7},{7,3},{8,12},{12,8},{9,1... | collective-permute-start | bytes 4300808 | tf_op jit(solution)/shard_map/ppermute | solution.py:683
  144.8 19.5 %collective-permute-start.22 = (bf16[4,104,808]{2,1,0:T(8,128)(2,1)S(1)}, bf16[4,104,808]{2,1,0:T(8,128)(2,1)S(1)}, u32[]{:S(2)}, u32[]{:S(2)}) collective-permute-start(bf16[4,104,808]{2,1,0:T(8,128)(2,1)S(1)} %copy-done.20), channel_id=1, source_target_pairs={{0,16},{8,24},{16,0},{24,8},{1,17},{9,25},{17,1},{25,9},{2,18},{10... | collective-permute-start | bytes 2016776 | tf_op jit(solution)/shard_map/ppermute | solution.py:745
  145.9 33.4 %collective-permute-start.23 = (bf16[4,104,808]{2,1,0:T(8,128)(2,1)S(1)}, bf16[4,104,808]{2,1,0:T(8,128)(2,1)S(1)}, u32[]{:S(2)}, u32[]{:S(2)}) collective-permute-start(bf16[4,104,808]{2,1,0:T(8,128)(2,1)S(1)} %copy-done.36), channel_id=1, source_target_pairs={{0,16},{8,24},{16,0},{24,8},{1,17},{9,25},{17,1},{25,9},{2,18},{10... | collective-permute-start | bytes 2016776 | tf_op jit(solution)/shard_map/ppermute | solution.py:745
  146.8 32.4 %collective-permute-start.24 = (bf16[4,104,808]{2,1,0:T(8,128)(2,1)S(1)}, bf16[4,104,808]{2,1,0:T(8,128)(2,1)S(1)}, u32[]{:S(2)}, u32[]{:S(2)}) collective-permute-start(bf16[4,104,808]{2,1,0:T(8,128)(2,1)S(1)} %copy-done.18), channel_id=1, source_target_pairs={{0,8},{8,0},{16,24},{24,16},{1,9},{9,1},{17,25},{25,17},{2,10},{10... | collective-permute-start | bytes 2016776 | tf_op jit(solution)/shard_map/ppermute | solution.py:745
  164.3 16.7 %collective-permute-start.25 = (bf16[4,104,808]{2,1,0:T(8,128)(2,1)S(1)}, bf16[4,104,808]{2,1,0:T(8,128)(2,1)S(1)}, u32[]{:S(2)}, u32[]{:S(2)}) collective-permute-start(bf16[4,104,808]{2,1,0:T(8,128)(2,1)S(1)} %copy-done.34), channel_id=1, source_target_pairs={{0,8},{8,0},{16,24},{24,16},{1,9},{9,1},{17,25},{25,17},{2,10},{10... | collective-permute-start | bytes 2016776 | tf_op jit(solution)/shard_map/ppermute | solution.py:745
  247.8 148.5 %reduce-scatter.5.cloned.1.call-start = ((), (), s32[]{:S(2)}) async-start(), calls=%async_computation.2 | async-start | bytes 1863680 | tf_op jit(solution)/shard_map/reduce_scatter | solution.py:819
  252.5 25.4 %collective-permute-start.37 = (bf16[4,200,896]{2,1,0:T(8,128)(2,1)}, bf16[4,200,896]{2,1,0:T(8,128)(2,1)}, u32[]{:S(2)}, u32[]{:S(2)}) collective-permute-start(bf16[4,200,896]{2,1,0:T(8,128)(2,1)} %get-tuple-element.163), channel_id=1, source_target_pairs={{0,4},{4,0},{1,5},{5,1},{2,6},{6,2},{3,7},{7,3},{8,12},{12,8},{9,1... | collective-permute-start | bytes 4300808 | tf_op jit(solution)/shard_map/ppermute | solution.py:683
  263.0 10.2 %collective-permute-start.46 = (f32[2,800]{1,0:T(2,128)S(1)}, f32[2,800]{1,0:T(2,128)S(1)}, u32[]{:S(2)}, u32[]{:S(2)}) collective-permute-start(f32[2,800]{1,0:T(2,128)S(1)} %add.109), channel_id=1, source_target_pairs={{0,1},{1,0},{2,3},{3,2},{4,5},{5,4},{6,7},{7,6},{8,9},{9,8},{10,11... | collective-permute-start | bytes 19208 | tf_op jit(solution)/shard_map/ppermute | solution.py:670
  279.6 13.2 %collective-permute-start.38 = (bf16[200,896]{1,0:T(8,128)(2,1)S(1)}, bf16[200,896]{1,0:T(8,128)(2,1)S(1)}, u32[]{:S(2)}, u32[]{:S(2)}) collective-permute-start(bf16[200,896]{1,0:T(8,128)(2,1)S(1)} %get-tuple-element.241), channel_id=1, source_target_pairs={{0,1},{1,2},{2,3},{3,0},{4,5},{5,6},{6,7},{7,4},{8,9},{9,10},{10,1... | collective-permute-start | bytes 1075208 | tf_op jit(solution)/shard_map/ppermute | solution.py:678
  281.8 16.2 %collective-permute-start.48 = (bf16[200,896]{1,0:T(8,128)(2,1)S(1)}, bf16[200,896]{1,0:T(8,128)(2,1)S(1)}, u32[]{:S(2)}, u32[]{:S(2)}) collective-permute-start(bf16[200,896]{1,0:T(8,128)(2,1)S(1)} %get-tuple-element.239), channel_id=1, source_target_pairs={{0,3},{1,0},{2,1},{3,2},{4,7},{5,4},{6,5},{7,6},{8,11},{9,8},{10,9... | collective-permute-start | bytes 1075208 | tf_op jit(solution)/shard_map/ppermute | solution.py:678
  283.7 28.0 %collective-permute-start.49 = (bf16[200,896]{1,0:T(8,128)(2,1)S(1)}, bf16[200,896]{1,0:T(8,128)(2,1)S(1)}, u32[]{:S(2)}, u32[]{:S(2)}) collective-permute-start(bf16[200,896]{1,0:T(8,128)(2,1)S(1)} %get-tuple-element.238), channel_id=1, source_target_pairs={{0,2},{1,3},{2,0},{3,1},{4,6},{5,7},{6,4},{7,5},{8,10},{9,11},{10,... | collective-permute-start | bytes 1075208 | tf_op jit(solution)/shard_map/ppermute | solution.py:678
  364.5 85.9 %all-gather.2.cloned.1.call-start = ((), (), s32[]{:S(2)}) async-start(), calls=%async_computation.3 | async-start | bytes 3354624 | tf_op jit(solution)/shard_map/all_gather | solution.py:820
  396.4 10.3 %collective-permute-start.50 = (f32[49,256]{1,0:T(8,128)}, f32[49,256]{1,0:T(8,128)S(1)}, u32[]{:S(2)}, u32[]{:S(2)}) collective-permute-start(f32[49,256]{1,0:T(8,128)} %bitcast.82), channel_id=1, source_target_pairs={{0,4},{4,0},{1,5},{5,1},{2,6},{6,2},{3,7},{7,3},{8,12},{12,8},{9,1... | collective-permute-start | bytes 150536 | tf_op jit(solution)/shard_map/ppermute | solution.py:670
  403.1 15.9 %collective-permute-start.40 = (bf16[200,896]{1,0:T(8,128)(2,1)}, bf16[200,896]{1,0:T(8,128)(2,1)}, u32[]{:S(2)}, u32[]{:S(2)}) collective-permute-start(bf16[200,896]{1,0:T(8,128)(2,1)} %get-tuple-element.244), channel_id=1, source_target_pairs={{0,3},{1,0},{2,1},{3,2},{4,7},{5,4},{6,5},{7,6},{8,11},{9,8},{10,9... | collective-permute-start | bytes 1075208 | tf_op jit(solution)/shard_map/ppermute | solution.py:678
  404.5 32.0 %collective-permute-start.41 = (bf16[200,896]{1,0:T(8,128)(2,1)}, bf16[200,896]{1,0:T(8,128)(2,1)}, u32[]{:S(2)}, u32[]{:S(2)}) collective-permute-start(bf16[200,896]{1,0:T(8,128)(2,1)} %get-tuple-element.243), channel_id=1, source_target_pairs={{0,2},{1,3},{2,0},{3,1},{4,6},{5,7},{6,4},{7,5},{8,10},{9,11},{10,... | collective-permute-start | bytes 1075208 | tf_op jit(solution)/shard_map/ppermute | solution.py:678
  404.5 32.0 %collective-permute-start.42 = (bf16[200,896]{1,0:T(8,128)(2,1)}, bf16[200,896]{1,0:T(8,128)(2,1)}, u32[]{:S(2)}, u32[]{:S(2)}) collective-permute-start(bf16[200,896]{1,0:T(8,128)(2,1)} %get-tuple-element.242), channel_id=1, source_target_pairs={{0,1},{1,2},{2,3},{3,0},{4,5},{5,6},{6,7},{7,4},{8,9},{9,10},{10,1... | collective-permute-start | bytes 1075208 | tf_op jit(solution)/shard_map/ppermute | solution.py:678
  407.6 5.1 %collective-permute-start.51 = (f32[49,256]{1,0:T(8,128)S(1)}, f32[49,256]{1,0:T(8,128)S(1)}, u32[]{:S(2)}, u32[]{:S(2)}) collective-permute-start(f32[49,256]{1,0:T(8,128)S(1)} %add.113), channel_id=1, source_target_pairs={{0,8},{8,0},{16,24},{24,16},{1,9},{9,1},{17,25},{25,17},{2,10},{10... | collective-permute-start | bytes 150536 | tf_op jit(solution)/shard_map/ppermute | solution.py:670
  (53 other events, 834.2 us)
Sparse Core Ops, SparseCore 0:
  247.9 72.5 reduce-scatter.6
  364.6 31.6 reduce-scatter.4
  398.4 31.5 all-gather.1

commit v2 on v1

--- a/solution.py
+++ b/solution.py
@@ -43,8 +43,16 @@
     return pltpu.CompilerParams(vmem_limit_bytes=mib * MIB, **more)
 
 
+def whole(array):
+    zeros = (0,) * array.ndim
+    return pl.BlockSpec(array.shape, lambda n, at: zeros)
+
+
+EAGERNESS = 6
+
+
 def cost(micros):
-    return pl.CostEstimate(flops=int(micros * 1.15e9), bytes_accessed=0, transcendentals=0)
+    return pl.CostEstimate(flops=int(micros * 1.15e9 / EAGERNESS), bytes_accessed=0, transcendentals=0)
 
 
 def clear_borders(dst, half, side):
@@ -157,53 +165,46 @@
 
 
 def segments(base, over):
+    cuts = sorted({*range(0, base + over, TILE), base, base + over})
     return [
-        (is_over, lo, lo + (base if is_over else 0), min(TILE, n - lo))
-        for is_over, n in ((0, base), (1, over))
-        for lo in range(0, n, TILE)
+        (int(lo >= base), lo - base if lo >= base else lo, lo, hi - lo) for lo, hi in zip(cuts, cuts[1:]) if hi <= base + over
     ]
 
 
-def pack_columns(k, values, slots, used, base_refs, over_refs):
-    base, over = base_refs[0].shape[1], over_refs[0].shape[1]
+def pack_columns(values, slots, used, base_ref, over_ref):
     width = values.shape[0]
-    for is_over, lo, start, count in segments(base, over):
-        for j, ref in enumerate(over_refs if is_over else base_refs):
-
-            @pl.when((k == j) & (start < used))
-            def _():
-                ref[:width, lo : lo + count] = nt(values, chooser(slots, start, count)).astype(BF)
-
-            @pl.when((k == j) & (start >= used))
-            def _():
-                ref[:width, lo : lo + count] = jnp.zeros((width, count), BF)
-
-            if width < ref.shape[0]:
-
-                @pl.when(k == j)
-                def _():
-                    ref[width:, lo : lo + count] = jnp.zeros((ref.shape[0] - width, count), BF)
-
-
-def packed_shapes(parts, width, base, over):
-    wide = ceil_to(width, 8)
-    specs = [pl.BlockSpec((wide, n), lambda k, at: (0, 0)) for n in (base, over) for _ in range(parts)]
-    return specs, [jax.ShapeDtypeStruct((wide, n), BF) for n in (base, over) for _ in range(parts)]
+    for is_over, lo, start, count in segments(base_ref.shape[1], over_ref.shape[1]):
+        ref = over_ref if is_over else base_ref
+
+        @pl.when(start < used)
+        def _():
+            ref[:width, lo : lo + count] = nt(values, chooser(slots, start, count)).astype(BF)
+
+        @pl.when(start >= used)
+        def _():
+            ref[:width, lo : lo + count] = jnp.zeros((width, count), BF)
+
+        if width < ref.shape[0]:
+            ref[width:, lo : lo + count] = jnp.zeros((ref.shape[0] - width, count), BF)
 
 
 def pack_normed_kernel(at_ref, conv_ref, vec_ref, slot_ref, *out_refs):
     k = pl.program_id(0)
-    parts = len(out_refs) // 2
+    base_refs, over_ref = out_refs[:-1], out_refs[-1]
+    part = lax.rem(at_ref[0] + k, len(base_refs))
     normed = (conv_ref[0] * vec_ref[0:1, :] + vec_ref[1:2, :]).T.astype(BF)
-    used = at_ref[1 + lax.rem(at_ref[0] + k, parts)]
-    pack_columns(k, normed, slot_ref[0], used, out_refs[:parts], out_refs[parts:])
+    for j, base_ref in enumerate(base_refs):
+
+        @pl.when(k == j)
+        def _():
+            pack_columns(normed, slot_ref[0], at_ref[1 + part], base_ref, over_ref.at[part])
 
 
 def pack_normed(at, conv, vec, slots, base, over):
     parts, cells, width = conv.shape
+    wide = ceil_to(width, 8)
     part = lambda k, at: (lax.rem(at[0] + k, parts), 0, 0)
-    specs, shapes = packed_shapes(parts, width, base, over)
-    out = pl.pallas_call(
+    *pieces, more = pl.pallas_call(
         pack_normed_kernel,
         grid_spec=pltpu.PrefetchScalarGridSpec(
             num_scalar_prefetch=1,
@@ -213,23 +214,21 @@
                 pl.BlockSpec(vec.shape, lambda k, at: (0, 0)),
                 pl.BlockSpec((1, 1, cells), part),
             ],
-            out_specs=specs,
+            out_specs=[pl.BlockSpec((wide, base), lambda k, at: (0, 0))] * parts
+            + [pl.BlockSpec((parts, wide, over), lambda k, at: (0, 0, 0))],
         ),
-        out_shape=shapes,
+        out_shape=[jax.ShapeDtypeStruct((wide, base), BF)] * parts + [jax.ShapeDtypeStruct((parts, wide, over), BF)],
         compiler_params=params(32),
         cost_estimate=cost(8),
         name="pack_normed",
     )(at, conv, vec, slots)
-    return out[:parts], out[parts:]
-
-
-def pack_cotangent_kernel(at_ref, cot_ref, m_ref, slot_ref, *refs):
-    out_refs, sum_ref, rows = refs[:-2], refs[-2], refs[-1]
-    parts = len(out_refs) // 2
+    return pieces, more
+
+
+def pack_cotangent_kernel(at_ref, cot_ref, m_ref, slot_ref, base_ref, over_ref, sum_ref, rows):
     crops, side, _, width = cot_ref.shape
-    per = side // parts
-    k = pl.program_id(0)
-    part = lax.rem(at_ref[0] + k, parts)
+    part, parts = pl.program_id(0), pl.num_programs(0)
+    per = rows.shape[0] // (crops * side)
     total = jnp.zeros((8, width), F32)
     for n in range(crops):
 
@@ -243,22 +242,22 @@
 
         total = lax.fori_loop(0, per, body, total)
 
-    @pl.when(k == 0)
+    @pl.when(part == 0)
     def _():
         sum_ref[...] = total
 
-    @pl.when(k > 0)
+    @pl.when(part > 0)
     def _():
         sum_ref[...] += total
 
-    pack_columns(k, rows[...].T.astype(BF), slot_ref[0], at_ref[1 + part], out_refs[:parts], out_refs[parts:])
+    pack_columns(rows[...].T.astype(BF), slot_ref[0], at_ref[1 + part], base_ref.at[0], over_ref.at[0])
 
 
 def pack_cotangent(at, cot, lane_mask, slots, base, over):
     crops, side, _, width = cot.shape
     parts, _, cells = slots.shape
-    specs, shapes = packed_shapes(parts, width, base, over)
-    *out, sums = pl.pallas_call(
+    wide = ceil_to(width, 8)
+    return pl.pallas_call(
         pack_cotangent_kernel,
         grid_spec=pltpu.PrefetchScalarGridSpec(
             num_scalar_prefetch=1,
@@ -266,17 +265,24 @@
             in_specs=[
                 pl.BlockSpec(cot.shape, lambda k, at: (0, 0, 0, 0)),
                 pl.BlockSpec(lane_mask.shape, lambda k, at: (0, 0, 0, 0)),
-                pl.BlockSpec((1, 1, cells), lambda k, at: (lax.rem(at[0] + k, parts), 0, 0)),
+                pl.BlockSpec((1, 1, cells), lambda k, at: (k, 0, 0)),
             ],
-            out_specs=specs + [pl.BlockSpec((8, width), lambda k, at: (0, 0))],
+            out_specs=[
+                pl.BlockSpec((1, wide, base), lambda k, at: (k, 0, 0)),
+                pl.BlockSpec((1, wide, over), lambda k, at: (k, 0, 0)),
+                pl.BlockSpec((8, width), lambda k, at: (0, 0)),
+            ],
             scratch_shapes=[pltpu.VMEM((cells, width), F32)],
         ),
-        out_shape=shapes + [jax.ShapeDtypeStruct((8, width), F32)],
+        out_shape=[
+            jax.ShapeDtypeStruct((parts, wide, base), BF),
+            jax.ShapeDtypeStruct((parts, wide, over), BF),
+            jax.ShapeDtypeStruct((8, width), F32),
+        ],
         compiler_params=params(40),
         cost_estimate=cost(10),
         name="pack_cotangent",
     )(at, cot, lane_mask, slots)
-    return out[:parts], out[parts:], sums
 
 
 def expand(base_ref, over_ref, slot_column, used, acc):
@@ -296,12 +302,12 @@
 
 def output_kernel(at_ref, x_ref, m_ref, bias_ref, column_ref, *refs):
     piece_refs, out_ref, acc = refs[:-2], refs[-2], refs[-1]
-    parts = len(piece_refs) // 2
+    parts = len(piece_refs) - 1
     _, side, _, width = x_ref.shape
     per = side // parts
     for k in range(parts):
         part = lax.rem(at_ref[0] + k, parts)
-        expand(piece_refs[k], piece_refs[parts + k], column_ref[part, 0], at_ref[1 + part], acc)
+        expand(piece_refs[k], piece_refs[parts].at[0, part], column_ref[part, 0], at_ref[1 + part], acc)
 
         @pl.loop(0, per)
         def _(i):
@@ -314,7 +320,7 @@
 
 
 def make_output(at, x, lane_mask, bias, columns, pieces):
-    parts = len(pieces) // 2
+    parts = len(pieces) - 1
     crops, side, _, width = x.shape
     cells = side * side // parts
     field = pl.BlockSpec((1, side, side, width), lambda n, at: (n, 0, 0, 0))
@@ -329,7 +335,7 @@
                 pl.BlockSpec((1, width), lambda n, at: (0, 0)),
                 pl.BlockSpec((parts, 1, cells, LANES), lambda n, at: (0, n, 0, 0)),
             ]
-            + [pl.BlockSpec(p.shape, lambda n, at: (0, 0)) for p in pieces],
+            + [whole(p) for p in pieces],
             out_specs=field,
             scratch_shapes=[pltpu.VMEM((cells, width), F32)],
         ),
@@ -340,25 +346,17 @@
     )(at, x, lane_mask, bias, columns, *pieces)
 
 
-def backward_kernel(
-    at_ref, x_ref, m_ref, cot_ref, conv_ref, w_ref, v_ref, column_ref, *refs, taps, rows, groups, rows2, groups2
-):
-    piece_refs, dx_ref, dw_ref, xs, gs, acc_ref = refs[:-5], refs[-5], refs[-4], refs[-3], refs[-2], refs[-1]
-    parts = len(piece_refs) // 2
-    _, side, _, width = x_ref.shape
+def input_gradient_kernel(at_ref, m_ref, cot_ref, conv_ref, w_ref, v_ref, column_ref, *refs, taps, rows, groups):
+    piece_refs, dx_ref, gs_ref, acc_ref = refs[:-3], refs[-3], refs[-2], refs[-1]
+    gs = gs_ref.at[0]
+    parts = len(piece_refs) - 1
+    _, side, _, width = cot_ref.shape
     per = side // parts
     half = taps // 2
-
-    @pl.when(pl.program_id(0) == 0)
-    def _():
-        dw_ref[...] = jnp.zeros_like(dw_ref)
-
-    clear_borders(xs, half, side)
     clear_borders(gs, half, side)
-    fill_masked(xs, x_ref, m_ref, half)
     for k in range(parts):
         part = lax.rem(at_ref[0] + k, parts)
-        expand(piece_refs[k], piece_refs[parts + k], column_ref[part, 0], at_ref[1 + part], acc_ref)
+        expand(piece_refs[k], piece_refs[parts].at[1, part], column_ref[part, 0], at_ref[1 + part], acc_ref)
 
         @pl.loop(0, per)
         def _(i):
@@ -389,43 +387,20 @@
                     value = m * (cot + acc[r].reshape(groups * 8, LANES)[:, :n])
                     dx_ref[0, r0 + r, c0 : c0 + groups * 8, lo:hi] = value.astype(BF)
 
-        @pl.loop(0, side // rows2)
-        def _(i):
-            r0 = i * rows2
-            for c0 in range(0, side, groups2 * 8):
-                span = groups2 * 8
-                grads = [
-                    gs[t, r0 + half + r, LEFT + c0 : LEFT + c0 + span, :].reshape(groups2, 8, LANES)
-                    for r in range(rows2)
-                ]
-                for b in range(taps):
-                    acc = [jnp.zeros((groups2, 8, LANES), F32) for _ in range(taps)]
-                    for j in range(rows2 + taps - 1):
-                        x = xs[t, r0 + j, pl.ds(LEFT + c0 + b - half, span), :].reshape(groups2, 8, LANES)
-                        for r in range(max(0, j - taps + 1), min(rows2, j + 1)):
-                            acc[j - r] = acc[j - r] + x * grads[r]
-                    for a in range(taps):
-                        dw_ref[t, a * taps + b] += jnp.sum(acc[a], axis=0)
-
-
-def conv_backward(
-    at, x, lane_mask, cot, conv, wide_taps, vectors, columns, pieces, taps, rows=12, groups=2, rows2=8, groups2=2
-):
-    parts = len(pieces) // 2
-    crops, side, _, width = x.shape
+
+def input_gradient(at, lane_mask, cot, conv, wide_taps, vectors, columns, pieces, taps, rows=12, groups=2):
+    parts = len(pieces) - 1
+    crops, side, _, width = cot.shape
     tiles, half = lane_tiles(width), taps // 2
     cells = side * side // parts
     field = pl.BlockSpec((1, side, side, width), lambda n, at: (n, 0, 0, 0))
-    padded = pltpu.VMEM((tiles, side + 2 * half, LEFT + side + 8, LANES), F32)
+    padded = (tiles, side + 2 * half, LEFT + side + 8, LANES)
     return pl.pallas_call(
-        functools.partial(
-            backward_kernel, taps=taps, rows=rows, groups=groups, rows2=rows2, groups2=groups2
-        ),
+        functools.partial(input_gradient_kernel, taps=taps, rows=rows, groups=groups),
         grid_spec=pltpu.PrefetchScalarGridSpec(
             num_scalar_prefetch=1,
             grid=(crops,),
             in_specs=[
-                field,
                 pl.BlockSpec((1, side, side, LANES), lambda n, at: (n, 0, 0, 0)),
                 field,
                 pl.BlockSpec((parts, 1, side // parts, side, width), lambda n, at: (0, n, 0, 0, 0)),
@@ -433,21 +408,109 @@
                 pl.BlockSpec(vectors.shape, lambda n, at: (0, 0, 0, 0)),
                 pl.BlockSpec((parts, 1, cells, LANES), lambda n, at: (0, n, 0, 0)),
             ]
-            + [pl.BlockSpec(p.shape, lambda n, at: (0, 0)) for p in pieces],
-            out_specs=[field, pl.BlockSpec(wide_taps.shape, lambda n, at: (0, 0, 0, 0))],
-            scratch_shapes=[padded, padded, pltpu.VMEM((cells, width), F32)],
+            + [whole(p) for p in pieces],
+            out_specs=[field, pl.BlockSpec((1, *padded), lambda n, at: (n, 0, 0, 0, 0))],
+            scratch_shapes=[pltpu.VMEM((cells, width), F32)],
         ),
-        out_shape=[jax.ShapeDtypeStruct(x.shape, BF), jax.ShapeDtypeStruct(wide_taps.shape, F32)],
-        compiler_params=params(52),
-        cost_estimate=cost(50),
-        name="depthwise_backward",
-    )(at, x, lane_mask, cot, conv, wide_taps, vectors, columns, *pieces)
+        out_shape=[jax.ShapeDtypeStruct(cot.shape, BF), jax.ShapeDtypeStruct((crops, *padded), F32)],
+        compiler_params=params(48),
+        cost_estimate=cost(28),
+        name="input_gradient",
+    )(at, lane_mask, cot, conv, wide_taps, vectors, columns, *pieces)
+
+
+def taps_gradient_kernel(x_ref, m_ref, gs_ref, dw_ref, xs, *, taps, rows, groups):
+    _, side, _, width = x_ref.shape
+    half = taps // 2
+    span = groups * 8
+
+    @pl.when(pl.program_id(0) == 0)
+    def _():
+        dw_ref[...] = jnp.zeros_like(dw_ref)
+
+    clear_borders(xs, half, side)
+    fill_masked(xs, x_ref, m_ref, half)
+    for t in range(lane_tiles(width)):
+
+        @pl.loop(0, side // rows)
+        def _(i):
+            r0 = i * rows
+            for c0 in range(0, side, span):
+                grads = [
+                    gs_ref[0, t, r0 + half + r, LEFT + c0 : LEFT + c0 + span, :].reshape(groups, 8, LANES)
+                    for r in range(rows)
+                ]
+                for b in range(taps):
+                    acc = [jnp.zeros((groups, 8, LANES), F32) for _ in range(taps)]
+                    for j in range(rows + taps - 1):
+                        x = xs[t, r0 + j, pl.ds(LEFT + c0 + b - half, span), :].reshape(groups, 8, LANES)
+                        for r in range(max(0, j - taps + 1), min(rows, j + 1)):
+                            acc[j - r] = acc[j - r] + x * grads[r]
+                    for a in range(taps):
+                        dw_ref[t, a * taps + b] += jnp.sum(acc[a], axis=0)
+
+
+def taps_gradient(x, lane_mask, gs, taps, rows=8, groups=2):
+    crops, side, _, width = x.shape
+    tiles = lane_tiles(width)
+    return pl.pallas_call(
+        functools.partial(taps_gradient_kernel, taps=taps, rows=rows, groups=groups),
+        grid=(crops,),
+        in_specs=[
+            pl.BlockSpec((1, side, side, width), lambda n: (n, 0, 0, 0)),
+            pl.BlockSpec((1, side, side, LANES), lambda n: (n, 0, 0, 0)),
+            pl.BlockSpec((1, *gs.shape[1:]), lambda n: (n, 0, 0, 0, 0)),
+        ],
+        out_specs=pl.BlockSpec((tiles, taps * taps, 8, LANES), lambda n: (0, 0, 0, 0)),
+        out_shape=jax.ShapeDtypeStruct((tiles, taps * taps, 8, LANES), F32),
+        scratch_shapes=[pltpu.VMEM(gs.shape[1:], F32)],
+        compiler_params=params(40),
+        cost_estimate=cost(22),
+        name="taps_gradient",
+    )(x, lane_mask, gs)
+
+
+def finish_kernel(both_ref, up_ref, down_ref, bias_ref, rows, *, parts, width, share):
+    ranks, _, _, wide = both_ref.shape
+    units = down_ref.shape[0]
+    wide_width = (wide - 8) // parts
+    for which in range(2):
+        for d in range(ranks):
+            count = min(share, units - d * share)
+            if count > 0:
+                rows[d * share : d * share + count, :] = both_ref[d, which].astype(F32)[:count]
+        if which == 0:
+            turned = rows[...].T
+            for s in range(parts):
+                up_ref[s * width : (s + 1) * width, :] = turned[s * wide_width : s * wide_width + width, :units]
+            bias_ref[...] = turned[wide - 8 :, :units]
+        else:
+            for s in range(parts):
+                down_ref[:, s * width : (s + 1) * width] = rows[:units, s * wide_width : s * wide_width + width]
+
+
+def finish(both, parts, width, share, units):
+    ranks, _, slab, wide = both.shape
+    channels = parts * width
+    return pl.pallas_call(
+        functools.partial(finish_kernel, parts=parts, width=width, share=share),
+        out_shape=[
+            jax.ShapeDtypeStruct((channels, units), F32),
+            jax.ShapeDtypeStruct((units, channels), F32),
+            jax.ShapeDtypeStruct((8, units), F32),
+        ],
+        scratch_shapes=[pltpu.VMEM((ceil_to(units, LANES), wide), F32)],
+        compiler_params=params(40),
+        cost_estimate=cost(5),
+        name="finish_weight_gradients",
+    )(both)
 
 
 def gelu_pair(value):
-    size = jnp.abs(value)
-    t = 1.0 / (1.0 + 0.23164189 * size)
-    bell = jnp.exp(-0.5 * value * value)
+    u = 1.0 + 0.23164189 * jnp.abs(value)
+    t = pl.reciprocal(u, approx=True)
+    t = t * (2.0 - u * t)
+    bell = jnp.exp2(value * value * -0.72134752)
     poly = 0.530702715
     for term in (-0.7265760135, 0.7107068705, -0.142248368, 0.127414796):
         poly = poly * t + term
@@ -458,7 +521,7 @@
 
 def pointwise_kernel(at_ref, *refs, chips, parts, width, base, over):
     up_refs, down_refs = refs[:chips], refs[chips : 2 * chips]
-    data, rest = refs[2 * chips : 2 * chips + 8], refs[2 * chips + 8 :]
+    data, more_ref, rest = refs[2 * chips : 2 * chips + 4], refs[2 * chips + 4], refs[2 * chips + 5 :]
     outs, (weight_grad_ref, sums_ref) = rest[:8], rest[8:10]
     up_w, down_w, up_t, down_t, up_acc, down_acc, x_place, g_place, hidden, grad_pre = rest[10:]
     whose, c = pl.program_id(0), pl.program_id(1)
@@ -466,7 +529,7 @@
     _, slab, wide = up_refs[0].shape
     units = chips * parts * slab
     channels = parts * width
-    block = units // 4
+    block = units // 8
     me, chip = at_ref[0], at_ref[1 + 2 * parts]
     used = at_ref[1 + whose * parts + me]
 
@@ -505,33 +568,28 @@
     for side in range(2):
         for case, found in cases:
             here = (whose == side) & case
-            x_refs, g_refs = data[2 * side : 2 * side + 2], data[4 + 2 * side : 6 + 2 * side]
+            x_refs = (data[side], more_ref.at[side, 0])
+            g_refs = (data[2 + side], more_ref.at[side, 1])
 
             @pl.when(here & (c * TILE < used))
             def _():
                 for refs, place in ((x_refs, x_place), (g_refs, g_place)):
-                    for k in range(parts):
-                        at = pl.ds(pl.multiple_of(lax.rem(me - k + parts, parts) * width, 8), width)
-                        values = [refs[is_over][k, :, lanes].astype(F32) for is_over, lanes, _ in found]
+                    for s in range(parts):
+                        k = lax.rem(me - s + parts, parts) if place is x_place else s
+                        at = slice(s * width, (s + 1) * width)
+                        values = [refs[is_over][s if is_over else k, :, lanes].astype(F32) for is_over, lanes, _ in found]
                         filled = sum(v.shape[1] for v in values)
                         if filled < TILE:
                             values.append(jnp.zeros((width, TILE - filled), F32))
                         place[at, :] = jnp.concatenate(values, axis=1) if len(values) > 1 else values[0]
 
-            @pl.when(here & (c * TILE >= used))
-            def _():
-                for is_over, lanes, _ in found:
-                    for ref in (outs[2 * side + is_over], outs[4 + 2 * side + is_over]):
-                        ref[:, :, lanes] = jnp.zeros((parts, width, lanes.stop - lanes.start), ref.dtype)
-
     @pl.when(c * TILE < used)
     def _():
         x = x_place[...].astype(BF)
         g = g_place[...].astype(BF)
 
-        @pl.loop(0, units // block)
-        def _(i):
-            at = pl.ds(pl.multiple_of(i * block, 16), block)
+        for i in range(units // block):
+            at = pl.ds(i * block, block)
             pre = nn(up_w[at, :], x)
             grad_hidden = nn(down_w[at, :], g)
             value, slope = gelu_pair(pre)
@@ -539,8 +597,11 @@
             gp = (grad_hidden * slope).astype(BF)
             hidden[at, :] = h
             grad_pre[at, :] = gp
-            up_acc[at, :] += nt(gp, x)
-            down_acc[at, :] += nt(h, g)
+
+        for lo in range(0, wide, 2 * LANES):
+            hi = min(lo + 2 * LANES, wide)
+            up_acc[:, lo:hi] += nt(grad_pre[...], x[lo:hi, :])
+            down_acc[:, lo:hi] += nt(hidden[...], g[lo:hi, :])
 
         def fold(v):
             return sum(v[:, lo : lo + LANES] for lo in range(0, TILE, LANES))
@@ -550,8 +611,8 @@
             k = lax.rem(me - s + parts, parts)
             branch = nn(down_t[rows, :], hidden[...])
             normed = nn(up_t[rows, :], grad_pre[...])
-            sums_ref[0, rows, :] += fold(normed)
-            sums_ref[1, rows, :] += fold(normed * x_place[rows, :])
+            sums_ref[k, 0] += fold(normed)
+            sums_ref[k, 1] += fold(normed * x_place[rows, :])
             for side in range(2):
                 for case, found in cases:
 
@@ -560,14 +621,14 @@
                         for is_over, lanes, tile in found:
                             to = 2 * side + is_over
                             for value, ref in ((branch, outs[to]), (normed, outs[4 + to])):
-                                ref[k, :, lanes] = value[:, tile].astype(ref.dtype)
+                                ref[s if is_over else k, :, lanes] = value[:, tile].astype(ref.dtype)
 
     @pl.when(last)
     def _():
         for p in range(chips):
             for q in range(parts):
                 row = (p * parts + q) * slab
-                to = (chip ^ p, lax.rem(me - q + parts, parts))
+                to = (chip ^ p, q)
                 weight_grad_ref[to[0], to[1], 0] = up_acc[row : row + slab, :].astype(BF)
                 weight_grad_ref[to[0], to[1], 1] = down_acc[row : row + slab, :].astype(BF)
 
@@ -575,7 +636,7 @@
 def pointwise(at, ups, downs, data):
     chips = len(ups)
     parts, width, base = data[0].shape
-    over = data[1].shape[2]
+    over = data[4].shape[4]
     _, slab, wide = ups[0].shape
     units, channels = chips * parts * slab, parts * width
     base_tiles = -(-base // TILE)
@@ -585,7 +646,8 @@
             return pl.BlockSpec((parts, width, over), lambda whose, c, at: (0, 0, 0))
 
         def place(whose, c, at):
-            return (0, 0, jnp.where(whose == side, jnp.minimum(c, base_tiles - 1), 0 if side else base_tiles - 1))
+            end = jnp.minimum(jnp.maximum((at[1 + side * parts + at[0]] - 1) // TILE, 0), base_tiles - 1)
+            return (0, 0, jnp.where(whose == side, jnp.minimum(c, end), 0 if side else end))
 
         return pl.BlockSpec((parts, width, TILE), place)
 
@@ -601,13 +663,13 @@
                 pl.BlockSpec(ups[0].shape, lambda w, c, at: (0, 0, 0), pipeline_mode=pl.Buffered(1))
                 for _ in range(2 * chips)
             ]
-            + tiles
-            + tiles,
+            + [tile(0, 0), tile(1, 0), tile(0, 0), tile(1, 0)]
+            + [pl.BlockSpec(data[4].shape, lambda w, c, at: (0, 0, 0, 0, 0), pipeline_mode=pl.Buffered(1))],
             out_specs=tiles
             + tiles
             + [
                 pl.BlockSpec((chips, parts, 2, slab, wide), lambda w, c, at: (0, 0, 0, 0, 0)),
-                pl.BlockSpec((2, channels, LANES), lambda w, c, at: (0, 0, 0)),
+                pl.BlockSpec((parts, 2, width, LANES), lambda w, c, at: (0, 0, 0, 0)),
             ],
             scratch_shapes=[
                 pltpu.VMEM((units, wide), BF),
@@ -626,7 +688,7 @@
         + result
         + [
             jax.ShapeDtypeStruct((chips, parts, 2, slab, wide), BF),
-            jax.ShapeDtypeStruct((2, channels, LANES), F32),
+            jax.ShapeDtypeStruct((parts, 2, width, LANES), F32),
         ],
         compiler_params=params(62),
         cost_estimate=cost(70),
@@ -665,6 +727,10 @@
     def everywhere(value, axes):
         for axis in axes:
             size = {"xy": chips, "core": cores, "mp": parts}[axis]
+            if size <= 4:
+                others = [lax.ppermute(value, axis, [(i, i ^ j) for i in range(size)]) for j in range(1, size)]
+                value = sum(others, value)
+                continue
             step = 1
             while step < size:
                 value = value + lax.ppermute(value, axis, [(i, i ^ step) for i in range(size)])
@@ -676,6 +742,9 @@
 
     def to_parts(pieces, ring=ring):
         return [pieces[0]] + [lax.ppermute(pieces[k], "mp", ring(k)) for k in range(1, parts)]
+
+    def exchange(by_part):
+        return lax.all_to_all(by_part, "mp", 0, 0, tiled=True)
 
     swap = [(i, cores - 1 - i) for i in range(cores)]
 
@@ -701,7 +770,7 @@
     own_bias = lax.dynamic_slice_in_dim(own_bias, rank * share, share, axis=0)
     up_rows = jnp.pad(jnp.concatenate([take(up_weight.T), own_bias], axis=1), ((0, slab - share), (0, 7)))
     down_rows = jnp.pad(take(down_weight), ((0, slab - share), (0, 8)))
-    rows = to_parts([jnp.stack([up_rows, down_rows])] * parts)
+    rows = lax.all_gather(jnp.stack([up_rows, down_rows]), "mp", axis=1, tiled=False)
 
     def over_plane(own, bits):
         held = {0: own}
@@ -729,26 +798,26 @@
 
     base = ceil_to(cells * 7 // 9, LANES)
     over = ceil_to(cells, LANES) - base
-    crowded = jnp.where(jnp.max(counts) > base, 1.0, 0.0)
+    over_full = jnp.where(jnp.max(counts) > base, 1.0, 0.0)
 
     cot_base, cot_over, down_bias_local = pack_cotangent(at, cotangent, lane_mask, slots, base, over)
-    inputs, *cot_base = after(inputs, *cot_base)
+    inputs, cot_base = after(inputs, cot_base)
+    grad_base = exchange(cot_base)
 
     wide_taps = spread_rows(conv_weight.reshape(taps * taps, width))
     convolved, stats = conv_forward(inputs, lane_mask, wide_taps, taps, parts)
-    stats, *rows = after(stats, *rows)
-    grad_pieces = to_parts(cot_base)
+    stats = jnp.sum(stats, axis=(0, 3)).reshape(2, -1)[:, :width]
+    extra = jnp.pad(jnp.stack([jnp.sum(by_part), over_full])[None], ((0, 0), (0, width - 2)))
+    stats = everywhere(jnp.concatenate([stats, extra, jnp.sum(down_bias_local, axis=0)[None]]), ("core", "xy"))
+    stats, rows = after(stats, rows)
     bits = [1 << j for j in range(chips.bit_length() - 1)]
 
     def double(held, bit):
         pairs = [(i, i ^ bit) for i in range(chips)]
         return {**held, **{p ^ bit: lax.ppermute(value, "xy", pairs) for p, value in held.items()}}
 
-    ups, downs = {0: jnp.stack([r[0] for r in rows])}, {0: jnp.stack([r[1] for r in rows])}
+    ups, downs = {0: rows[0]}, {0: rows[1]}
     ups, downs = double(ups, bits[0]), double(downs, bits[-1])
-    stats = jnp.sum(stats, axis=(0, 3)).reshape(2, -1)[:, :width]
-    extra = jnp.pad(jnp.stack([jnp.sum(by_part), crowded])[None], ((0, 0), (0, width - 2)))
-    stats = everywhere(jnp.concatenate([stats, extra, jnp.sum(down_bias_local, axis=0)[None]]), ("core", "xy"))
     ocean_count = stats[2, 0]
     overflows = stats[2, 1] > 0
     down_bias_grad = stats[3]
@@ -759,70 +828,65 @@
     scale = gain * inv_std
 
     affine = jnp.stack([scale, shift - channel_mean * scale])
+    normed_base, normed_over = pack_normed(at, convolved.reshape(parts, cells, width), affine, slots, base, over)
     places = sorted(ups), sorted(downs)
-    convolved, *held = after(convolved, *[ups[p] for p in places[0]], *[downs[p] for p in places[1]])
-    ups = dict(zip(places[0], held))
-    downs = dict(zip(places[1], held[len(ups) :]))
+    *both, grad_base = after(*normed_base, *[ups[p] for p in places[0]], *[downs[p] for p in places[1]], grad_base)
+    normed_base, held = both[:parts], both[parts:]
+    ups, downs = dict(zip(places[0], held)), dict(zip(places[1], held[len(ups) :]))
     for j in range(1, len(bits)):
         ups, downs = double(ups, bits[j]), double(downs, bits[-1 - j])
     ups, downs = [ups[p] for p in range(chips)], [downs[p] for p in range(chips)]
-    normed_base, normed_over = pack_normed(at, convolved.reshape(parts, cells, width), affine, slots, base, over)
-    *both, = after(*normed_base, *grad_pieces)
-    normed_base, grad_base = both[:parts], jnp.stack(both[parts:])
-    x_base = jnp.stack(to_parts(normed_base))
-    none = jnp.zeros((parts, wide_width, over), BF)
+    *both, crowded, columns = after(*to_parts(normed_base), *ups, *downs, overflows, columns)
+    x_base, ups, downs = jnp.stack(both[:parts]), both[parts : parts + chips], both[parts + chips :]
 
     def overflow_in():
-        x, g = jnp.stack(to_parts(normed_over)), jnp.stack(to_parts(cot_over))
-        return x, g, to_core(x), to_core(g)
-
-    x_over, g_over, x_far_over, g_far_over = lax.cond(overflows, overflow_in, lambda: (none,) * 4)
-    data = [x_base, x_over, to_core(x_base), x_far_over, grad_base, g_over, to_core(grad_base), g_far_over]
+        own = jnp.stack([exchange(normed_over), exchange(cot_over)])
+        return jnp.stack([own, to_core(own)])
+
+    more = lax.cond(crowded, overflow_in, lambda: jnp.zeros((2, 2, parts, wide_width, over), BF))
+    data = [x_base, to_core(x_base), grad_base, to_core(grad_base), more]
     *sums_out, weight_grad, sums = pointwise(at, ups, downs, data)
     branch, normed = list(sums_out[:4]), list(sums_out[4:])
 
-    def home(own, far):
-        total = (own + to_core(far).astype(F32)).astype(BF)
+    def over_cores(own, far):
+        return (own + to_core(far).astype(F32)).astype(BF)
+
+    def home(total):
         return to_parts([total[k] for k in range(parts)], ring_back)
 
-    normed_base = home(normed[0], normed[2])
-    branch[0], branch[2], _ = after(branch[0], branch[2], normed_base[-1])
-    branch_base = home(branch[0], branch[2])
-    nothing = [jnp.zeros((wide_width, over), BF)] * parts
-    branch_over, normed_over = lax.cond(
-        overflows, lambda: (home(branch[1], branch[3]), home(normed[1], normed[3])), lambda: (nothing, nothing)
-    )
-
-    sums = everywhere(jnp.sum(sums, axis=2), ("core", "xy", "mp"))
-    sums = lax.dynamic_slice_in_dim(sums, me * wide_width, wide_width, axis=1)[:, :width]
+    sums = everywhere(jnp.sum(sums, axis=3), ("core", "xy"))
+    sums = sum(to_parts([sums[k] for k in range(parts)], ring_back))[:, :width]
+    total, sums = after(over_cores(normed[0], normed[2]), sums)
+    normed_base = home(total)
+    total = over_cores(branch[0], branch[2])
+    crowded, total, sums, *normed_base = after(overflows, total, sums, *normed_base)
+
+    def overflow_out():
+        return jnp.stack([exchange(over_cores(v[1], v[3])) for v in (branch, normed)])
+
+    more = lax.cond(crowded, overflow_out, lambda: jnp.zeros((2, parts, wide_width, over), BF))
+    total, more = after(total, more)
+    branch_base = home(total)
+
     shift_grad = sums[0]
     gain_grad = (sums[1] - shift * shift_grad) / gain
     vectors = jnp.stack([channel_mean, scale, scale * shift_grad / ocean_count, scale * inv_std * gain_grad / ocean_count])
-    input_grad, taps_local = conv_backward(
-        at,
-        inputs,
-        lane_mask,
-        cotangent,
-        convolved,
-        wide_taps,
-        spread_rows(vectors),
-        columns,
-        [*normed_base, *normed_over],
-        taps,
+    input_grad, grad_conv = input_gradient(
+        at, lane_mask, cotangent, convolved, wide_taps, spread_rows(vectors), columns, [*normed_base, more], taps
     )
-    output = make_output(at, inputs, lane_mask, down_bias.astype(F32)[None], columns, [*branch_base, *branch_over])
+
+    own = lax.psum_scatter(weight_grad, "xy", scatter_dimension=0, tiled=False)
+    own, grad_conv, *branch_base = after(own, grad_conv, *branch_base)
+    taps_local = taps_gradient(inputs, lane_mask, grad_conv, taps)
+    own = lax.psum_scatter(own, "mp", scatter_dimension=0, tiled=False)
+    own, taps_local = after(own, taps_local)
+    both = lax.all_gather(own, ("xy", "core"), axis=0, tiled=False)
+    taps_local, *branch_base = after(taps_local, *branch_base)
+    output = make_output(at, inputs, lane_mask, down_bias.astype(F32)[None], columns, [*branch_base, more])
     taps_local = jnp.sum(taps_local, axis=2).transpose(1, 0, 2).reshape(taps * taps, -1)
     conv_weight_grad = everywhere(taps_local, ("core", "xy"))[:, :width].reshape(taps, taps, width)
-
-    own = lax.psum_scatter(weight_grad, "xy", scatter_dimension=0, tiled=False)
-    own, _ = after(own, taps_local)
-    own = lax.psum_scatter(own, "mp", scatter_dimension=0, tiled=False)
-    both = lax.all_gather(own, ("xy", "core"), axis=0, tiled=False)
-    both = both[:, :, :share].transpose(1, 0, 2, 3).reshape(2, -1, wide)[:, :local_units]
-    up_bias_grad = both[0, :, -8].astype(F32)
-    both = both[:, :, :-8].reshape(2, local_units, parts, wide_width)[..., :width].reshape(2, local_units, channels)
-    up_weight_grad = both[0].T.astype(F32)
-    down_weight_grad = both[1].astype(F32)
+    up_weight_grad, down_weight_grad, bias_rows = finish(both, parts, width, share, local_units)
+    up_bias_grad = bias_rows[0]
     return (
         output,
         input_grad,

time: 480 us -> 369 us (0.77)
  waiting for transfers between devices: 178 us -> 87.5 us
  starting transfers between devices: 49.8 us -> 40.1 us
    ppermute x6, waiting for transfers between devices: 45.9 us -> 5.93 us  [double(): lax.ppermute(value, 'xy', pairs)]
    reduce_scatter x1, waiting for transfers between devices: 31.8 us -> 8.18 us  [per_device(): own = lax.psum_scatter(own, 'mp', scatter_dimension=0, tiled=False)]
    ppermute x11 -> x12, waiting for transfers between devices: 33.4 us -> 10.7 us  [everywhere(): lax.ppermute(value, axis, [(i, i ^ j) for i in range(size)])]
    ppermute x15 -> x12, waiting for transfers between devices: 63.7 us -> 54.1 us  [to_parts(): lax.ppermute(pieces[k], 'mp', ring(k))]
    ppermute x15 -> x12, starting transfers between devices: 23.8 us -> 14.6 us  [to_parts(): lax.ppermute(pieces[k], 'mp', ring(k))]
    unnamed x95 -> x100, local copies, waits for them, and re-layouts: 18.5 us -> 27 us
    broadcast_in_dim x12 -> x0, local copies, waits for them, and re-layouts: 7.74 us -> none  [the longest x8 4.56 us: per_device(): nothing = [jnp.zeros((wide_width, over), BF)] * parts]
    all_gather x1, waiting for transfers between devices: 0.01 us -> 7.63 us  [per_device(): both = lax.all_gather(own, ('xy', 'core'), axis=0, tiled=False)]
  transfers between devices with their start and end apart: 40 -> 40, of which waited for: 21 -> 21; matrix products, arithmetic and copies ran while one was open for 7% -> 8% of each run, Pallas kernels for 21% -> 27%
where the time goes in v2:
time: 369 us; the launch traced here: 363 us
  Pallas kernels  159 us (43%)
  waiting for transfers between devices  87.5 us (24%)
  local copies, waits for them, and re-layouts  44 us (12%)
  starting transfers between devices  40.1 us (11%)
  other arithmetic  16.4 us (4%)
  between operations  16.1 us (4%)
    pallas_call x1, Pallas kernels, pointwise(): pl.pallas_call(functools.partial(pointwise_kernel, chips=chips, parts=par...  57.2 us
    ppermute x12, waiting for transfers between devices, to_parts(): lax.ppermute(pieces[k], 'mp', ring(k))  54.1 us
    pallas_call x1, Pallas kernels, input_gradient(): pl.pallas_call(functools.partial(input_gradient_kernel, taps=taps, rows=r...  32.3 us
    unnamed x100, local copies, waits for them, and re-layouts  27 us
    pallas_call x1, Pallas kernels, conv_forward(): pl.pallas_call(functools.partial(forward_kernel, taps=taps, rows=rows, gr...  22 us
    pallas_call x1, Pallas kernels, taps_gradient(): pl.pallas_call(functools.partial(taps_gradient_kernel, taps=taps, rows=ro...  17.8 us
    ppermute x12, starting transfers between devices, to_parts(): lax.ppermute(pieces[k], 'mp', ring(k))  14.6 us
    pallas_call x1, Pallas kernels, make_output(): pl.pallas_call(output_kernel, grid_spec=pltpu.PrefetchScalarGridSpec(num_...  11 us
  transfers between devices with their start and end apart: 40, of which 21 were waited for; matrix products, arithmetic and copies ran while one was open for 8% of the time, Pallas kernels for 27%

profile of v2, /device:TPU:0, one launch (start us, length us, event | category | flops | bytes accessed | tf_op | source)
XLA Modules:
  0.0 363.1 jit_solution(1437166593771782238)
XLA Ops:
  19.0 8.1 %pack_cotangent.1 = (bf16[4,200,896]{2,1,0:T(8,128)(2,1)S(1)}, bf16[4,200,256]{2,1,0:T(8,128)(2,1)}, f32[8,200]{1,0:T(8,128)S(1)}) custom-call(s32[10]{0:T(128)S(1)} %pad_add_fusion.at_ref, bf16[2,48,48,200]{3,2,1,0:T(8,128)(2,1)S(1)} %copy-done.23, bf16[2,48,48,128]{3,2,1,0:T(8,128)(2,1)S(1)} %broadcast_in_dim.74.m_ref, s32[4,1,1152]{2,1,0:T(1,128)S(1)} %reshape.110.slot_ref), custom_call_target="tpu_custom_call" | custom-call | flops 1916666624 | tf_op jit(solution)/shard_map/pack_cotangent/pallas_call | solution.py:260
  28.2 6.0 %all-to-all-start.4 = ((bf16[4,200,896]{2,1,0:T(8,128)(2,1)}), bf16[4,200,896]{2,1,0:T(8,128)(2,1)}, u32[]{:S(2)}, u32[]{:S(2)}) async-start(bf16[4,200,896]{2,1,0:T(8,128)(2,1)} %copy-done.7), calls=%async_computation.4 | async-start | bytes 2867200 | tf_op jit(solution)/shard_map/all_to_all | solution.py:747
  36.4 22.0 %depthwise_forward.1 = (f32[4,2,12,48,200]{4,3,2,1,0:T(8,128)S(1)}, f32[2,2,2,8,128]{4,3,2,1,0:T(8,128)S(1)}) custom-call(bf16[2,48,48,200]{3,2,1,0:T(8,128)(2,1)S(1)} %copy-done.3, bf16[2,48,48,128]{3,2,1,0:T(8,128)(2,1)S(1)} %broadcast_in_dim.74.m_ref, f32[2,49,8,128]{3,2,1,0:T(8,128)S(1)} %broadcast_in_dim.83.w_ref), custom_call_target="tpu_custom_call" | custom-call | flops 4216666624 | tf_op jit(solution)/shard_map/depthwise_forward/pallas_call | solution.py:130
  59.0 2.2 copy-done.25
  63.4 2.8 collective-permute-start.6
  67.8 2.9 collective-permute-done.7
  70.8 2.3 slice_bitcast_fusion
  76.2 2.3 copy-done.26
  78.5 7.0 %pack_normed.1 = (bf16[200,896]{1,0:T(8,128)(2,1)S(1)}, bf16[200,896]{1,0:T(8,128)(2,1)S(1)}, bf16[200,896]{1,0:T(8,128)(2,1)S(1)}, bf16[200,896]{1,0:T(8,128)(2,1)S(1)}, bf16[4,200,256]{2,1,0:T(8,128)(2,1)}) custom-call(s32[10]{0:T(128)S(1)} %pad_add_fusion.at_ref, f32[4,1152,200]{2,1,0:T(8,128)S(1)} %bitcast.112, f32[2,200]{1,0:T(2,128)S(1)} %pad_maximum_fusion.5.vec_ref, ...), custom_call_target="tpu_custom_call" | custom-call | flops 1533333376 | tf_op jit(solution)/shard_map/pack_normed/pallas_call | solution.py:207
  85.5 5.6 %collective-permute-done.8.refs_1_ = bf16[4,104,808]{2,1,0:T(8,128)(2,1)} collective-permute-done((bf16[4,104,808]{2,1,0:T(8,128)(2,1)}, bf16[4,104,808]{2,1,0:T(8,128)(2,1)}, u32[]{:S(2)}, u32[]{:S(2)}) %collective-permute-start.8) | collective-permute-done | bytes 672288 | tf_op jit(solution)/shard_map/ppermute | solution.py:817
  98.3 5.9 %collective-permute-done.10 = bf16[200,896]{1,0:T(8,128)(2,1)S(1)} collective-permute-done((bf16[200,896]{1,0:T(8,128)(2,1)S(1)}, bf16[200,896]{1,0:T(8,128)(2,1)S(1)}, u32[]{:S(2)}, u32[]{:S(2)}) %collective-permute-start.10) | collective-permute-done | bytes 358432 | tf_op jit(solution)/shard_map/ppermute | solution.py:744
  105.7 10.8 %collective-permute-done.11 = bf16[200,896]{1,0:T(8,128)(2,1)S(1)} collective-permute-done((bf16[200,896]{1,0:T(8,128)(2,1)S(1)}, bf16[200,896]{1,0:T(8,128)(2,1)S(1)}, u32[]{:S(2)}, u32[]{:S(2)}) %collective-permute-start.11) | collective-permute-done | bytes 358432 | tf_op jit(solution)/shard_map/ppermute | solution.py:744
  119.9 7.7 %collective-permute-done.12 = bf16[200,896]{1,0:T(8,128)(2,1)S(1)} collective-permute-done((bf16[200,896]{1,0:T(8,128)(2,1)S(1)}, bf16[200,896]{1,0:T(8,128)(2,1)S(1)}, u32[]{:S(2)}, u32[]{:S(2)}) %collective-permute-start.12) | collective-permute-done | bytes 358432 | tf_op jit(solution)/shard_map/ppermute | solution.py:744
  128.0 2.3 broadcast_in_dim.87.column_ref
  135.0 57.2 %pointwise.1 = (f32[4,200,896]{2,1,0:T(8,128)}, f32[4,200,256]{2,1,0:T(8,128)}, bf16[4,200,896]{2,1,0:T(8,128)(2,1)}, bf16[4,200,256]{2,1,0:T(8,128)(2,1)}, f32[...) custom-call(s32[10]{0:T(128)} %copy-done.20, ...), custom_call_target="tpu_custom_call" | custom-call | flops 13416667136 | tf_op jit(solution)/shard_map/pointwise/pallas_call | solution.py:657
  193.9 2.7 collective-permute-done.21
  196.7 3.4 collective-permute-start.22
  209.0 2.6 add_convert_fusion.2
  211.7 2.1 collective-permute-start.28
  214.5 3.0 add_convert_fusion.3
  217.5 5.2 %collective-permute-done.28.refs_1_ = bf16[200,896]{1,0:T(8,128)(2,1)S(1)} collective-permute-done((bf16[200,896]{1,0:T(8,128)(2,1)S(1)}, bf16[200,896]{1,0:T(8,128)(2,1)S(1)}, u32[]{:S(2)}, u32[]{:S(2)}) %collective-permute-start.28) | collective-permute-done | bytes 358432 | tf_op jit(solution)/shard_map/ppermute | solution.py:744
  222.7 20.4 %collective-permute-done.29.refs_2_ = bf16[200,896]{1,0:T(8,128)(2,1)S(1)} collective-permute-done((bf16[200,896]{1,0:T(8,128)(2,1)S(1)}, bf16[200,896]{1,0:T(8,128)(2,1)S(1)}, u32[]{:S(2)}, u32[]{:S(2)}) %collective-permute-start.29) | collective-permute-done | bytes 358432 | tf_op jit(solution)/shard_map/ppermute | solution.py:744
  243.3 2.5 slice_bitcast_fusion.2
  245.8 2.3 collective-permute-start.32
  248.1 2.0 collective-permute-start.33
  251.5 32.3 %input_gradient.1 = (bf16[2,48,48,200]{3,2,1,0:T(8,128)(2,1)}, f32[2,2,54,64,128]{4,3,2,1,0:T(8,128)}) custom-call(s32[10]{0:T(128)S(1)} %copy-done.21, bf16[2,48,48,128]{3,2,1,0:T(8,128)(2,1)S(1)} %broadcast_in_dim.74.m_ref, bf16[2,48,48,200]{3,2,1,0:T(8,128)(2,1)S(1)} %copy-done.24, f32[4,2,12,48,200]{4,3,2,1,0:T(8,128)} %copy-done.25, ...), custom_call_target="tpu_custom_call" | custom-call | flops 5366666752 | tf_op jit(solution)/shard_map/input_gradient/pallas_call | solution.py:398
  287.9 3.3 copy-done.27
  291.2 17.8 %taps_gradient.1 = f32[2,49,8,128]{3,2,1,0:T(8,128)S(1)} custom-call(bf16[2,48,48,200]{3,2,1,0:T(8,128)(2,1)S(1)} %copy-done.4, bf16[2,48,48,128]{3,2,1,0:T(8,128)(2,1)S(1)} %broadcast_in_dim.74.m_ref, f32[2,2,54,64,128]{4,3,2,1,0:T(8,128)S(1)} %copy-done.27), custom_call_target="tpu_custom_call" | custom-call | flops 4216666624 | tf_op jit(solution)/shard_map/taps_gradient/pallas_call | solution.py:456
  309.8 8.2 %reduce-scatter.5.cloned.1.call-done = bf16[1,2,104,808]{3,2,1,0:T(8,128)(2,1)} async-done(((bf16[4,2,104,808]{3,2,1,0:T(8,128)(2,1)}), bf16[1,2,104,808]{3,2,1,0:T(8,128)(2,1)}) %reduce-scatter.5.cloned.1.call-update) | async-done | bytes 336144 | tf_op jit(solution)/shard_map/reduce_scatter | solution.py:881
  331.2 11.0 %make_output.1 = bf16[2,48,48,200]{3,2,1,0:T(8,128)(2,1)} custom-call(s32[10]{0:T(128)S(1)} %copy-done.21, bf16[2,48,48,200]{3,2,1,0:T(8,128)(2,1)S(1)} %copy-done.5, bf16[2,48,48,128]{3,2,1,0:T(8,128)(2,1)S(1)} %broadcast_in_dim.74.m_ref, f32[1,200]{1,0:T(1,128)S(1)} %bitcast.110, s32[4,2,576,128]{3,2,1,0:T(8,128)S(1)} %copy-done.2, ...), custom_call_target="tpu_custom_call" | custom-call | flops 2300000000 | tf_op jit(solution)/shard_map/make_output/pallas_call | solution.py:327
  342.9 7.6 %all-gather.7.cloned.1.call-done = bf16[16,104,808]{2,1,0:T(8,128)(2,1)} async-done(((bf16[2,104,808]{2,1,0:T(8,128)(2,1)}), bf16[16,104,808]{2,1,0:T(8,128)(2,1)}) %all-gather.7.cloned.1.call-update) | async-done | bytes 2689040 | tf_op jit(solution)/shard_map/all_gather | solution.py:883
  352.5 3.2 finish_weight_gradients.1
  (225 shorter events, 73.3 us)
Async XLA Ops:
  7.2 63.5 %all-gather.5.cloned.1.call-start = ((), (), s32[]{:S(2)}) async-start(), calls=%async_computation.8 | async-start | bytes 1863680 | tf_op jit(solution)/shard_map/all_gather | solution.py:773
  9.9 6.5 %collective-permute-start.3 = (s32[4]{0:T(128)S(1)}, s32[4]{0:T(128)S(1)}, u32[]{:S(2)}, u32[]{:S(2)}) collective-permute-start(s32[4]{0:T(128)S(1)} %convert_element_type.80), channel_id=1, source_target_pairs={{0,4},{4,0},{1,5},{5,1},{2,6},{6,2},{3,7},{7,3},{8,12},{12,8},{9,1... | collective-permute-start | bytes 56 | tf_op jit(solution)/shard_map/ppermute | solution.py:752
  28.2 57.3 %all-to-all-start.4 = ((bf16[4,200,896]{2,1,0:T(8,128)(2,1)}), bf16[4,200,896]{2,1,0:T(8,128)(2,1)}, u32[]{:S(2)}, u32[]{:S(2)}) async-start(bf16[4,200,896]{2,1,0:T(8,128)(2,1)} %copy-done.7), calls=%async_computation.4 | async-start | bytes 2867200 | tf_op jit(solution)/shard_map/all_to_all | solution.py:747
  34.2 251.7 %reduce-scatter.7.cloned.1.call-start = ((), (), s32[]{:S(2)}) async-start(), calls=%async_computation.10 | async-start | bytes 7454720
  73.1 17.9 %collective-permute-start.8 = (bf16[4,104,808]{2,1,0:T(8,128)(2,1)}, bf16[4,104,808]{2,1,0:T(8,128)(2,1)}, u32[]{:S(2)}, u32[]{:S(2)}) collective-permute-start(bf16[4,104,808]{2,1,0:T(8,128)(2,1)} %get-tuple-element.130.refs_0_), channel_id=1, source_target_pairs={{0,8},{8,0},{16,24},{24,16},{1,9},{9,1},{17,25},{25,17},{2,10},{10... | collective-permute-start | bytes 2016776 | tf_op jit(solution)/shard_map/ppermute | solution.py:817
  73.2 17.8 %collective-permute-start.9 = (bf16[4,104,808]{2,1,0:T(8,128)(2,1)S(1)}, bf16[4,104,808]{2,1,0:T(8,128)(2,1)}, u32[]{:S(2)}, u32[]{:S(2)}) collective-permute-start(bf16[4,104,808]{2,1,0:T(8,128)(2,1)S(1)} %get-tuple-element.134.refs_4_), channel_id=1, source_target_pairs={{0,16},{8,24},{16,0},{24,8},{1,17},{9,25},{17,1},{25,9},{2,18},{10... | collective-permute-start | bytes 2016776 | tf_op jit(solution)/shard_map/ppermute | solution.py:817
  91.0 13.2 %collective-permute-start.10 = (bf16[200,896]{1,0:T(8,128)(2,1)S(1)}, bf16[200,896]{1,0:T(8,128)(2,1)S(1)}, u32[]{:S(2)}, u32[]{:S(2)}) collective-permute-start(bf16[200,896]{1,0:T(8,128)(2,1)S(1)} %get-tuple-element.122), channel_id=1, source_target_pairs={{0,1},{1,2},{2,3},{3,0},{4,5},{5,6},{6,7},{7,4},{8,9},{9,10},{10,1... | collective-permute-start | bytes 1075208 | tf_op jit(solution)/shard_map/ppermute | solution.py:744
  92.8 23.8 %collective-permute-start.11 = (bf16[200,896]{1,0:T(8,128)(2,1)S(1)}, bf16[200,896]{1,0:T(8,128)(2,1)S(1)}, u32[]{:S(2)}, u32[]{:S(2)}) collective-permute-start(bf16[200,896]{1,0:T(8,128)(2,1)S(1)} %get-tuple-element.123), channel_id=1, source_target_pairs={{0,2},{1,3},{2,0},{3,1},{4,6},{5,7},{6,4},{7,5},{8,10},{9,11},{10,... | collective-permute-start | bytes 1075208 | tf_op jit(solution)/shard_map/ppermute | solution.py:744
  94.7 32.9 %collective-permute-start.13 = (bf16[4,104,808]{2,1,0:T(8,128)(2,1)}, bf16[4,104,808]{2,1,0:T(8,128)(2,1)}, u32[]{:S(2)}, u32[]{:S(2)}) collective-permute-start(bf16[4,104,808]{2,1,0:T(8,128)(2,1)} %get-tuple-element.130.refs_0_), channel_id=1, source_target_pairs={{0,16},{8,24},{16,0},{24,8},{1,17},{9,25},{17,1},{25,9},{2,18},{10... | collective-permute-start | bytes 2016776 | tf_op jit(solution)/shard_map/ppermute | solution.py:817
  95.9 31.7 %collective-permute-start.14 = (bf16[4,104,808]{2,1,0:T(8,128)(2,1)}, bf16[4,104,808]{2,1,0:T(8,128)(2,1)}, u32[]{:S(2)}, u32[]{:S(2)}) collective-permute-start(bf16[4,104,808]{2,1,0:T(8,128)(2,1)} %collective-permute-done.8.refs_1_), channel_id=1, source_target_pairs={{0,16},{8,24},{16,0},{24,8},{1,17},{9,25},{17,1},{25,9},{2,18},{10... | collective-permute-start | bytes 2016776 | tf_op jit(solution)/shard_map/ppermute | solution.py:817
  96.8 30.9 %collective-permute-start.15 = (bf16[4,104,808]{2,1,0:T(8,128)(2,1)S(1)}, bf16[4,104,808]{2,1,0:T(8,128)(2,1)}, u32[]{:S(2)}, u32[]{:S(2)}) collective-permute-start(bf16[4,104,808]{2,1,0:T(8,128)(2,1)S(1)} %get-tuple-element.134.refs_4_), channel_id=1, source_target_pairs={{0,8},{8,0},{16,24},{24,16},{1,9},{9,1},{17,25},{25,17},{2,10},{10... | collective-permute-start | bytes 2016776 | tf_op jit(solution)/shard_map/ppermute | solution.py:817
  104.2 23.8 %collective-permute-start.16 = (bf16[4,104,808]{2,1,0:T(8,128)(2,1)}, bf16[4,104,808]{2,1,0:T(8,128)(2,1)}, u32[]{:S(2)}, u32[]{:S(2)}) collective-permute-start(bf16[4,104,808]{2,1,0:T(8,128)(2,1)} %collective-permute-done.9.refs_6_), channel_id=1, source_target_pairs={{0,8},{8,0},{16,24},{24,16},{1,9},{9,1},{17,25},{25,17},{2,10},{10... | collective-permute-start | bytes 2016776 | tf_op jit(solution)/shard_map/ppermute | solution.py:817
  117.3 10.3 %collective-permute-start.12 = (bf16[200,896]{1,0:T(8,128)(2,1)S(1)}, bf16[200,896]{1,0:T(8,128)(2,1)S(1)}, u32[]{:S(2)}, u32[]{:S(2)}) collective-permute-start(bf16[200,896]{1,0:T(8,128)(2,1)S(1)} %get-tuple-element.124), channel_id=1, source_target_pairs={{0,3},{1,0},{2,1},{3,2},{4,7},{5,4},{6,5},{7,6},{8,11},{9,8},{10,9... | collective-permute-start | bytes 1075208 | tf_op jit(solution)/shard_map/ppermute | solution.py:744
  127.6 6.5 %collective-permute-start.18 = (bf16[4,200,896]{2,1,0:T(8,128)(2,1)}, bf16[4,200,896]{2,1,0:T(8,128)(2,1)}, u32[]{:S(2)}, u32[]{:S(2)}) collective-permute-start(bf16[4,200,896]{2,1,0:T(8,128)(2,1)} %all-to-all-done.4.refs_10_), channel_id=1, source_target_pairs={{0,4},{4,0},{1,5},{5,1},{2,6},{6,2},{3,7},{7,3},{8,12},{12,8},{9,1... | collective-permute-start | bytes 4300808 | tf_op jit(solution)/shard_map/ppermute | solution.py:752
  192.2 125.7 %reduce-scatter.5.cloned.1.call-start = ((), (), s32[]{:S(2)}) async-start(), calls=%async_computation.7 | async-start | bytes 1863680 | tf_op jit(solution)/shard_map/reduce_scatter | solution.py:881
  192.3 15.6 %collective-permute-start.20 = (bf16[4,200,896]{2,1,0:T(8,128)(2,1)}, bf16[4,200,896]{2,1,0:T(8,128)(2,1)S(1)}, u32[]{:S(2)}, u32[]{:S(2)}) collective-permute-start(bf16[4,200,896]{2,1,0:T(8,128)(2,1)} %get-tuple-element.150), channel_id=1, source_target_pairs={{0,4},{4,0},{1,5},{5,1},{2,6},{6,2},{3,7},{7,3},{8,12},{12,8},{9,1... | collective-permute-start | bytes 4300808 | tf_op jit(solution)/shard_map/ppermute | solution.py:752
  192.5 22.1 %collective-permute-start.19 = (bf16[4,200,896]{2,1,0:T(8,128)(2,1)}, bf16[4,200,896]{2,1,0:T(8,128)(2,1)}, u32[]{:S(2)}, u32[]{:S(2)}) collective-permute-start(bf16[4,200,896]{2,1,0:T(8,128)(2,1)} %get-tuple-element.148), channel_id=1, source_target_pairs={{0,4},{4,0},{1,5},{5,1},{2,6},{6,2},{3,7},{7,3},{8,12},{12,8},{9,1... | collective-permute-start | bytes 4300808 | tf_op jit(solution)/shard_map/ppermute | solution.py:752
  196.6 4.7 %collective-permute-start.24 = (f32[4,2,200]{2,1,0:T(2,128)S(1)}, f32[4,2,200]{2,1,0:T(2,128)S(1)}, u32[]{:S(2)}, u32[]{:S(2)}) collective-permute-start(f32[4,2,200]{2,1,0:T(2,128)S(1)} %add.117), channel_id=1, source_target_pairs={{0,24},{8,16},{16,8},{24,0},{1,25},{9,17},{17,9},{25,1},{2,26},{10... | collective-permute-start | bytes 19208 | tf_op jit(solution)/shard_map/ppermute | solution.py:731
  196.6 4.7 %collective-permute-start.23 = (f32[4,2,200]{2,1,0:T(2,128)S(1)}, f32[4,2,200]{2,1,0:T(2,128)S(1)}, u32[]{:S(2)}, u32[]{:S(2)}) collective-permute-start(f32[4,2,200]{2,1,0:T(2,128)S(1)} %add.117), channel_id=1, source_target_pairs={{0,16},{8,24},{16,0},{24,8},{1,17},{9,25},{17,1},{25,9},{2,18},{10... | collective-permute-start | bytes 19208 | tf_op jit(solution)/shard_map/ppermute | solution.py:731
  196.7 5.2 %collective-permute-start.22 = (f32[4,2,200]{2,1,0:T(2,128)S(1)}, f32[4,2,200]{2,1,0:T(2,128)S(1)}, u32[]{:S(2)}, u32[]{:S(2)}) collective-permute-start(f32[4,2,200]{2,1,0:T(2,128)S(1)} %add.117), channel_id=1, source_target_pairs={{0,8},{8,0},{16,24},{24,16},{1,9},{9,1},{17,25},{25,17},{2,10},{10... | collective-permute-start | bytes 19208 | tf_op jit(solution)/shard_map/ppermute | solution.py:731
  201.9 4.5 %collective-permute-start.26 = (f32[2,200]{1,0:T(2,128)S(1)}, f32[2,200]{1,0:T(2,128)S(1)}, u32[]{:S(2)}, u32[]{:S(2)}) collective-permute-start(f32[2,200]{1,0:T(2,128)S(1)} %get-tuple-element.208), channel_id=1, source_target_pairs={{0,2},{1,3},{2,0},{3,1},{4,6},{5,7},{6,4},{7,5},{8,10},{9,11},{10,... | collective-permute-start | bytes 4808 | tf_op jit(solution)/shard_map/ppermute | solution.py:744
  202.0 5.9 %collective-permute-start.27 = (f32[2,200]{1,0:T(2,128)S(1)}, f32[2,200]{1,0:T(2,128)S(1)}, u32[]{:S(2)}, u32[]{:S(2)}) collective-permute-start(f32[2,200]{1,0:T(2,128)S(1)} %get-tuple-element.207), channel_id=1, source_target_pairs={{0,1},{1,2},{2,3},{3,0},{4,5},{5,6},{6,7},{7,4},{8,9},{9,10},{10,1... | collective-permute-start | bytes 4808 | tf_op jit(solution)/shard_map/ppermute | solution.py:744
  211.7 11.0 %collective-permute-start.28 = (bf16[200,896]{1,0:T(8,128)(2,1)S(1)}, bf16[200,896]{1,0:T(8,128)(2,1)S(1)}, u32[]{:S(2)}, u32[]{:S(2)}) collective-permute-start(bf16[200,896]{1,0:T(8,128)(2,1)S(1)} %get-tuple-element.204), channel_id=1, source_target_pairs={{0,3},{1,0},{2,1},{3,2},{4,7},{5,4},{6,5},{7,6},{8,11},{9,8},{10,9... | collective-permute-start | bytes 1075208 | tf_op jit(solution)/shard_map/ppermute | solution.py:744
  213.9 29.3 %collective-permute-start.29 = (bf16[200,896]{1,0:T(8,128)(2,1)S(1)}, bf16[200,896]{1,0:T(8,128)(2,1)S(1)}, u32[]{:S(2)}, u32[]{:S(2)}) collective-permute-start(bf16[200,896]{1,0:T(8,128)(2,1)S(1)} %get-tuple-element.203), channel_id=1, source_target_pairs={{0,2},{1,3},{2,0},{3,1},{4,6},{5,7},{6,4},{7,5},{8,10},{9,11},{10,... | collective-permute-start | bytes 1075208 | tf_op jit(solution)/shard_map/ppermute | solution.py:744
  213.9 29.3 %collective-permute-start.30 = (bf16[200,896]{1,0:T(8,128)(2,1)S(1)}, bf16[200,896]{1,0:T(8,128)(2,1)S(1)}, u32[]{:S(2)}, u32[]{:S(2)}) collective-permute-start(bf16[200,896]{1,0:T(8,128)(2,1)S(1)} %get-tuple-element.202), channel_id=1, source_target_pairs={{0,1},{1,2},{2,3},{3,0},{4,5},{5,6},{6,7},{7,4},{8,9},{9,10},{10,1... | collective-permute-start | bytes 1075208 | tf_op jit(solution)/shard_map/ppermute | solution.py:744
  245.8 37.9 %collective-permute-start.31 = (bf16[200,896]{1,0:T(8,128)(2,1)S(1)}, bf16[200,896]{1,0:T(8,128)(2,1)S(1)}, u32[]{:S(2)}, u32[]{:S(2)}) collective-permute-start(bf16[200,896]{1,0:T(8,128)(2,1)S(1)} %get-tuple-element.200), channel_id=1, source_target_pairs={{0,3},{1,0},{2,1},{3,2},{4,7},{5,4},{6,5},{7,6},{8,11},{9,8},{10,9... | collective-permute-start | bytes 1075208 | tf_op jit(solution)/shard_map/ppermute | solution.py:744
  245.8 38.7 %collective-permute-start.32 = (bf16[200,896]{1,0:T(8,128)(2,1)S(1)}, bf16[200,896]{1,0:T(8,128)(2,1)S(1)}, u32[]{:S(2)}, u32[]{:S(2)}) collective-permute-start(bf16[200,896]{1,0:T(8,128)(2,1)S(1)} %get-tuple-element.199), channel_id=1, source_target_pairs={{0,2},{1,3},{2,0},{3,1},{4,6},{5,7},{6,4},{7,5},{8,10},{9,11},{10,... | collective-permute-start | bytes 1075208 | tf_op jit(solution)/shard_map/ppermute | solution.py:744
  248.1 37.1 %collective-permute-start.33 = (bf16[200,896]{1,0:T(8,128)(2,1)S(1)}, bf16[200,896]{1,0:T(8,128)(2,1)S(1)}, u32[]{:S(2)}, u32[]{:S(2)}) collective-permute-start(bf16[200,896]{1,0:T(8,128)(2,1)S(1)} %get-tuple-element.198), channel_id=1, source_target_pairs={{0,1},{1,2},{2,3},{3,0},{4,5},{5,6},{6,7},{7,4},{8,9},{9,10},{10,1... | collective-permute-start | bytes 1075208 | tf_op jit(solution)/shard_map/ppermute | solution.py:744
  286.0 64.6 %all-gather.7.cloned.1.call-start = ((), (), s32[]{:S(2)}) async-start(), calls=%async_computation.9 | async-start | bytes 3354624 | tf_op jit(solution)/shard_map/all_gather | solution.py:883
  321.9 20.3 %collective-permute-start.35 = (f32[49,256]{1,0:T(8,128)S(1)}, f32[49,256]{1,0:T(8,128)S(1)}, u32[]{:S(2)}, u32[]{:S(2)}) collective-permute-start(f32[49,256]{1,0:T(8,128)S(1)} %add.124), channel_id=1, source_target_pairs={{0,8},{8,0},{16,24},{24,16},{1,9},{9,1},{17,25},{25,17},{2,10},{10... | collective-permute-start | bytes 150536 | tf_op jit(solution)/shard_map/ppermute | solution.py:731
  323.5 18.8 %collective-permute-start.36 = (f32[49,256]{1,0:T(8,128)S(1)}, f32[49,256]{1,0:T(8,128)S(1)}, u32[]{:S(2)}, u32[]{:S(2)}) collective-permute-start(f32[49,256]{1,0:T(8,128)S(1)} %add.124), channel_id=1, source_target_pairs={{0,16},{8,24},{16,0},{24,8},{1,17},{9,25},{17,1},{25,9},{2,18},{10... | collective-permute-start | bytes 150536 | tf_op jit(solution)/shard_map/ppermute | solution.py:731
  325.0 17.3 %collective-permute-start.37 = (f32[49,256]{1,0:T(8,128)S(1)}, f32[49,256]{1,0:T(8,128)S(1)}, u32[]{:S(2)}, u32[]{:S(2)}) collective-permute-start(f32[49,256]{1,0:T(8,128)S(1)} %add.124), channel_id=1, source_target_pairs={{0,24},{8,16},{16,8},{24,0},{1,25},{9,17},{17,9},{25,1},{2,26},{10... | collective-permute-start | bytes 150536 | tf_op jit(solution)/shard_map/ppermute | solution.py:731
  (56 other events, 438.5 us)
Sparse Core Ops, SparseCore 0:
  13.7 52.9 all-gather.4
  192.4 63.3 reduce-scatter.6
  286.1 31.8 reduce-scatter.4
  319.9 30.6 all-gather.6

commit v3 on v2

--- a/solution.py
+++ b/solution.py
@@ -285,19 +285,25 @@
     )(at, cot, lane_mask, slots)
 
 
-def expand(base_ref, over_ref, slot_column, used, acc):
+def expand(base_ref, over_ref, slot_column, reach, acc):
     cells, width = acc.shape
     acc[...] = jnp.zeros_like(acc)
     for is_over, lo, start, count in segments(base_ref.shape[1], over_ref.shape[1]):
         ref = over_ref if is_over else base_ref
 
-        @pl.when(start < used)
+        @pl.when((start < reach[1]) & (start + count > reach[0]))
         def _():
             lanes = lax.broadcasted_iota(jnp.int32, (cells, LANES), 1) + start
             choice = jnp.concatenate(
                 [jnp.where(lanes + j == slot_column, 1.0, 0.0).astype(BF) for j in range(0, count, LANES)], axis=1
             )
             acc[...] += nt(choice, ref[:width, lo : lo + count])
+
+
+def reach_of(at_ref, parts, part, crop):
+    crops = (at_ref.shape[0] - (2 + 2 * parts)) // parts - 1
+    place = 2 + 2 * parts + part * (crops + 1) + crop
+    return at_ref[place], at_ref[place + 1]
 
 
 def output_kernel(at_ref, x_ref, m_ref, bias_ref, column_ref, *refs):
@@ -307,7 +313,8 @@
     per = side // parts
     for k in range(parts):
         part = lax.rem(at_ref[0] + k, parts)
-        expand(piece_refs[k], piece_refs[parts].at[0, part], column_ref[part, 0], at_ref[1 + part], acc)
+        reach = reach_of(at_ref, parts, part, pl.program_id(0))
+        expand(piece_refs[k], piece_refs[parts].at[0, part], column_ref[part, 0], reach, acc)
 
         @pl.loop(0, per)
         def _(i):
@@ -340,7 +347,7 @@
             scratch_shapes=[pltpu.VMEM((cells, width), F32)],
         ),
         out_shape=jax.ShapeDtypeStruct(x.shape, BF),
-        compiler_params=params(40),
+        compiler_params=params(60),
         cost_estimate=cost(12),
         name="make_output",
     )(at, x, lane_mask, bias, columns, *pieces)
@@ -356,7 +363,8 @@
     clear_borders(gs, half, side)
     for k in range(parts):
         part = lax.rem(at_ref[0] + k, parts)
-        expand(piece_refs[k], piece_refs[parts].at[1, part], column_ref[part, 0], at_ref[1 + part], acc_ref)
+        reach = reach_of(at_ref, parts, part, pl.program_id(0))
+        expand(piece_refs[k], piece_refs[parts].at[1, part], column_ref[part, 0], reach, acc_ref)
 
         @pl.loop(0, per)
         def _(i):
@@ -413,7 +421,7 @@
             scratch_shapes=[pltpu.VMEM((cells, width), F32)],
         ),
         out_shape=[jax.ShapeDtypeStruct(cot.shape, BF), jax.ShapeDtypeStruct((crops, *padded), F32)],
-        compiler_params=params(48),
+        compiler_params=params(60),
         cost_estimate=cost(28),
         name="input_gradient",
     )(at, lane_mask, cot, conv, wide_taps, vectors, columns, *pieces)
@@ -464,7 +472,7 @@
         out_specs=pl.BlockSpec((tiles, taps * taps, 8, LANES), lambda n: (0, 0, 0, 0)),
         out_shape=jax.ShapeDtypeStruct((tiles, taps * taps, 8, LANES), F32),
         scratch_shapes=[pltpu.VMEM(gs.shape[1:], F32)],
-        compiler_params=params(40),
+        compiler_params=params(60),
         cost_estimate=cost(22),
         name="taps_gradient",
     )(x, lane_mask, gs)
@@ -794,7 +802,9 @@
     counts = jnp.sum(by_part, axis=(1, 2)).astype(jnp.int32)
     columns = jnp.broadcast_to(slots.reshape(parts, crops, -1)[..., None], (parts, crops, cells // crops, LANES))
     slots = slots.reshape(parts, 1, cells)
-    at = jnp.concatenate([me[None].astype(jnp.int32), counts, to_core(counts), chip[None].astype(jnp.int32)])
+    ends = jnp.cumsum(jnp.sum(by_part.reshape(parts, crops, -1), axis=2), axis=1)
+    reaches = jnp.pad(ends, ((0, 0), (1, 0))).astype(jnp.int32).reshape(-1)
+    at = jnp.concatenate([me[None].astype(jnp.int32), counts, to_core(counts), chip[None].astype(jnp.int32), reaches])
 
     base = ceil_to(cells * 7 // 9, LANES)
     over = ceil_to(cells, LANES) - base
@@ -836,7 +846,7 @@
     for j in range(1, len(bits)):
         ups, downs = double(ups, bits[j]), double(downs, bits[-1 - j])
     ups, downs = [ups[p] for p in range(chips)], [downs[p] for p in range(chips)]
-    *both, crowded, columns = after(*to_parts(normed_base), *ups, *downs, overflows, columns)
+    *both, crowded = after(*to_parts(normed_base), *ups, *downs, overflows)
     x_base, ups, downs = jnp.stack(both[:parts]), both[parts : parts + chips], both[parts + chips :]
 
     def overflow_in():
@@ -849,39 +859,39 @@
     branch, normed = list(sums_out[:4]), list(sums_out[4:])
 
     def over_cores(own, far):
-        return (own + to_core(far).astype(F32)).astype(BF)
+        far = to_core(far)
+        return [(own[k] + far[k].astype(F32)).astype(BF) for k in range(parts)]
 
     def home(total):
-        return to_parts([total[k] for k in range(parts)], ring_back)
+        return to_parts(total, ring_back)
 
     sums = everywhere(jnp.sum(sums, axis=3), ("core", "xy"))
     sums = sum(to_parts([sums[k] for k in range(parts)], ring_back))[:, :width]
-    total, sums = after(over_cores(normed[0], normed[2]), sums)
+    total, sums = after(tuple(over_cores(normed[0], normed[2])), sums)
     normed_base = home(total)
     total = over_cores(branch[0], branch[2])
-    crowded, total, sums, *normed_base = after(overflows, total, sums, *normed_base)
+    crowded, total, sums, columns, *normed_base = after(overflows, tuple(total), sums, columns, *normed_base)
 
     def overflow_out():
-        return jnp.stack([exchange(over_cores(v[1], v[3])) for v in (branch, normed)])
+        return jnp.stack([exchange(jnp.stack(over_cores(v[1], v[3]))) for v in (branch, normed)])
 
     more = lax.cond(crowded, overflow_out, lambda: jnp.zeros((2, parts, wide_width, over), BF))
-    total, more = after(total, more)
-    branch_base = home(total)
 
     shift_grad = sums[0]
     gain_grad = (sums[1] - shift * shift_grad) / gain
     vectors = jnp.stack([channel_mean, scale, scale * shift_grad / ocean_count, scale * inv_std * gain_grad / ocean_count])
+    total, more = after(total, more)
+    branch_base = home(total)
+
+    own = lax.psum_scatter(weight_grad, "xy", scatter_dimension=0, tiled=False)
+    own, vectors, *normed_base = after(own, spread_rows(vectors), *normed_base)
+    own = lax.psum_scatter(own, "mp", scatter_dimension=0, tiled=False)
     input_grad, grad_conv = input_gradient(
-        at, lane_mask, cotangent, convolved, wide_taps, spread_rows(vectors), columns, [*normed_base, more], taps
+        at, lane_mask, cotangent, convolved, wide_taps, vectors, columns, [*normed_base, more], taps
     )
-
-    own = lax.psum_scatter(weight_grad, "xy", scatter_dimension=0, tiled=False)
-    own, grad_conv, *branch_base = after(own, grad_conv, *branch_base)
+    own, grad_conv = after(own, grad_conv)
+    both = lax.all_gather(own, ("xy", "core"), axis=0, tiled=False)
     taps_local = taps_gradient(inputs, lane_mask, grad_conv, taps)
-    own = lax.psum_scatter(own, "mp", scatter_dimension=0, tiled=False)
-    own, taps_local = after(own, taps_local)
-    both = lax.all_gather(own, ("xy", "core"), axis=0, tiled=False)
-    taps_local, *branch_base = after(taps_local, *branch_base)
     output = make_output(at, inputs, lane_mask, down_bias.astype(F32)[None], columns, [*branch_base, more])
     taps_local = jnp.sum(taps_local, axis=2).transpose(1, 0, 2).reshape(taps * taps, -1)
     conv_weight_grad = everywhere(taps_local, ("core", "xy"))[:, :width].reshape(taps, taps, width)

time: 369 us -> 358 us (0.970)
  local copies, waits for them, and re-layouts: 44 us -> 24.9 us
  starting transfers between devices: 40.1 us -> 49.1 us
  waiting for transfers between devices: 87.5 us -> 95 us
  Pallas kernels: 159 us -> 153 us
    unnamed x100 -> x72, local copies, waits for them, and re-layouts: 27 us -> 13.7 us
    unnamed x5, waiting for transfers between devices: 0.07 us -> 9.32 us
    all_gather x1, waiting for transfers between devices: 7.63 us -> 0.01 us  [per_device(): both = lax.all_gather(own, ('xy', 'core'), axis=0, tiled=False)]
    pallas_call x1, Pallas kernels: 57.2 us -> 49.8 us  [pointwise(): pl.pallas_call(functools.partial(pointwise_kernel, chips=chips, parts=par...]
    ppermute x12, waiting for transfers between devices: 54.1 us -> 61.1 us  [to_parts(): lax.ppermute(pieces[k], 'mp', ring(k))]
    ppermute x12, starting transfers between devices: 10.9 us -> 17.3 us  [everywhere(): lax.ppermute(value, axis, [(i, i ^ j) for i in range(size)])]
    ppermute x12, starting transfers between devices: 14.6 us -> 18.6 us  [to_parts(): lax.ppermute(pieces[k], 'mp', ring(k))]
  transfers between devices with their start and end apart: 40 -> 40, of which waited for: 21 -> 25; matrix products, arithmetic and copies ran while one was open for 8% -> 7% of each run, Pallas kernels for 27% -> 28%
where the time goes in v3:
time: 358 us; the launch traced here: 354 us
  Pallas kernels  153 us (43%)
  waiting for transfers between devices  95 us (27%)
  starting transfers between devices  49.1 us (14%)
  local copies, waits for them, and re-layouts  24.9 us (7%)
  other arithmetic  16.2 us (5%)
  between operations  15.9 us (4%)
    ppermute x12, waiting for transfers between devices, to_parts(): lax.ppermute(pieces[k], 'mp', ring(k))  61.1 us
    pallas_call x1, Pallas kernels, pointwise(): pl.pallas_call(functools.partial(pointwise_kernel, chips=chips, parts=par...  49.8 us
    pallas_call x1, Pallas kernels, input_gradient(): pl.pallas_call(functools.partial(input_gradient_kernel, taps=taps, rows=r...  31.2 us
    pallas_call x1, Pallas kernels, conv_forward(): pl.pallas_call(functools.partial(forward_kernel, taps=taps, rows=rows, gr...  22 us
    pallas_call x1, Pallas kernels, taps_gradient(): pl.pallas_call(functools.partial(taps_gradient_kernel, taps=taps, rows=ro...  21 us
    ppermute x12, starting transfers between devices, to_parts(): lax.ppermute(pieces[k], 'mp', ring(k))  18.6 us
    ppermute x12, starting transfers between devices, everywhere(): lax.ppermute(value, axis, [(i, i ^ j) for i in range(size)])  17.3 us
    unnamed x72, local copies, waits for them, and re-layouts  13.7 us
  transfers between devices with their start and end apart: 40, of which 25 were waited for; matrix products, arithmetic and copies ran while one was open for 7% of the time, Pallas kernels for 28%

profile of v3, /device:TPU:0, one launch (start us, length us, event | category | flops | bytes accessed | tf_op | source)
XLA Modules:
  0.0 354.1 jit_solution(5280372836618305012)
XLA Ops:
  18.7 8.2 %pack_cotangent.1 = (bf16[4,200,896]{2,1,0:T(8,128)(2,1)}, bf16[4,200,256]{2,1,0:T(8,128)(2,1)}, f32[8,200]{1,0:T(8,128)S(1)}) custom-call(s32[22]{0:T(128)S(1)} %concatenate.9.at_ref, bf16[2,48,48,200]{3,2,1,0:T(8,128)(2,1)S(1)} %copy-done.7, bf16[2,48,48,128]{3,2,1,0:T(8,128)(2,1)S(1)} %broadcast_in_dim.74.m_ref, s32[4,1,1152]{2,1,0:T(1,128)S(1)} %reshape.141.slot_ref), custom_call_target="tpu_custom_call" | custom-call | flops 1916666624 | tf_op jit(solution)/shard_map/pack_cotangent/pallas_call | solution.py:260
  27.0 5.9 %all-to-all-start.4 = ((bf16[4,200,896]{2,1,0:T(8,128)(2,1)}), bf16[4,200,896]{2,1,0:T(8,128)(2,1)}, u32[]{:S(2)}, u32[]{:S(2)}) async-start(bf16[4,200,896]{2,1,0:T(8,128)(2,1)} %get-tuple-element.124), calls=%async_computation.4 | async-start | bytes 2867200 | tf_op jit(solution)/shard_map/all_to_all | solution.py:755
  35.9 22.0 %depthwise_forward.1 = (f32[4,2,12,48,200]{4,3,2,1,0:T(8,128)S(1)}, f32[2,2,2,8,128]{4,3,2,1,0:T(8,128)S(1)}) custom-call(bf16[2,48,48,200]{3,2,1,0:T(8,128)(2,1)S(1)} %copy-done.3, bf16[2,48,48,128]{3,2,1,0:T(8,128)(2,1)S(1)} %broadcast_in_dim.74.m_ref, f32[2,49,8,128]{3,2,1,0:T(8,128)S(1)} %broadcast_in_dim.83.w_ref), custom_call_target="tpu_custom_call" | custom-call | flops 4216666624 | tf_op jit(solution)/shard_map/depthwise_forward/pallas_call | solution.py:130
  57.9 2.2 copy-done.8
  63.0 1.9 collective-permute-start.7
  65.2 2.4 collective-permute-done.7
  74.4 2.3 copy-done.9
  76.7 7.0 %pack_normed.1 = (bf16[200,896]{1,0:T(8,128)(2,1)S(1)}, bf16[200,896]{1,0:T(8,128)(2,1)S(1)}, bf16[200,896]{1,0:T(8,128)(2,1)S(1)}, bf16[200,896]{1,0:T(8,128)(2,1)S(1)}, bf16[4,200,256]{2,1,0:T(8,128)(2,1)}) custom-call(s32[22]{0:T(128)S(1)} %concatenate.9.at_ref, f32[4,1152,200]{2,1,0:T(8,128)S(1)} %bitcast.112, f32[2,200]{1,0:T(2,128)S(1)} %pad_maximum_fusion.7.vec_ref, ...), custom_call_target="tpu_custom_call" | custom-call | flops 1533333376 | tf_op jit(solution)/shard_map/pack_normed/pallas_call | solution.py:207
  83.7 3.8 %collective-permute-done.8.refs_1_ = bf16[4,104,808]{2,1,0:T(8,128)(2,1)} collective-permute-done((bf16[4,104,808]{2,1,0:T(8,128)(2,1)S(1)}, bf16[4,104,808]{2,1,0:T(8,128)(2,1)}, u32[]{:S(2)}, u32[]{:S(2)}) %collective-permute-start.8) | collective-permute-done | bytes 672288 | tf_op jit(solution)/shard_map/ppermute | solution.py:827
  90.1 8.4 %collective-permute-start.11 = (bf16[200,896]{1,0:T(8,128)(2,1)S(1)}, bf16[200,896]{1,0:T(8,128)(2,1)S(1)}, u32[]{:S(2)}, u32[]{:S(2)}) collective-permute-start(bf16[200,896]{1,0:T(8,128)(2,1)S(1)} %get-tuple-element.127), channel_id=1, source_target_pairs={{0,2},{1,3},{2,0},{3,1},{4,6},{5,7},{6,4},{7,5},{8,10},{9,11},{10,... | collective-permute-start | bytes 1075208 | tf_op jit(solution)/shard_map/ppermute | solution.py:752
  100.9 6.4 %collective-permute-done.10 = bf16[200,896]{1,0:T(8,128)(2,1)S(1)} collective-permute-done((bf16[200,896]{1,0:T(8,128)(2,1)S(1)}, bf16[200,896]{1,0:T(8,128)(2,1)S(1)}, u32[]{:S(2)}, u32[]{:S(2)}) %collective-permute-start.10) | collective-permute-done | bytes 358432 | tf_op jit(solution)/shard_map/ppermute | solution.py:752
  107.7 13.0 %collective-permute-done.11 = bf16[200,896]{1,0:T(8,128)(2,1)S(1)} collective-permute-done((bf16[200,896]{1,0:T(8,128)(2,1)S(1)}, bf16[200,896]{1,0:T(8,128)(2,1)S(1)}, u32[]{:S(2)}, u32[]{:S(2)}) %collective-permute-start.11) | collective-permute-done | bytes 358432 | tf_op jit(solution)/shard_map/ppermute | solution.py:752
  121.4 9.6 %collective-permute-done.12 = bf16[200,896]{1,0:T(8,128)(2,1)S(1)} collective-permute-done((bf16[200,896]{1,0:T(8,128)(2,1)S(1)}, bf16[200,896]{1,0:T(8,128)(2,1)S(1)}, u32[]{:S(2)}, u32[]{:S(2)}) %collective-permute-start.12) | collective-permute-done | bytes 358432 | tf_op jit(solution)/shard_map/ppermute | solution.py:752
  135.4 3.2 collective-permute-done.17.refs_9_
  138.6 49.8 %pointwise.1 = (f32[4,200,896]{2,1,0:T(8,128)}, f32[4,200,256]{2,1,0:T(8,128)}, bf16[4,200,896]{2,1,0:T(8,128)(2,1)}, bf16[4,200,256]{2,1,0:T(8,128)(2,1)}, f32[...) custom-call(s32[22]{0:T(128)} %copy-done.5, ...), custom_call_target="tpu_custom_call" | custom-call | flops 13416667136 | tf_op jit(solution)/shard_map/pointwise/pallas_call | solution.py:665
  190.8 3.2 collective-permute-done.21
  194.0 8.5 %collective-permute-start.23 = (f32[4,2,200]{2,1,0:T(2,128)S(1)}, f32[4,2,200]{2,1,0:T(2,128)S(1)}, u32[]{:S(2)}, u32[]{:S(2)}) collective-permute-start(f32[4,2,200]{2,1,0:T(2,128)S(1)} %add.177), channel_id=1, source_target_pairs={{0,16},{8,24},{16,0},{24,8},{1,17},{9,25},{17,1},{25,9},{2,18},{10... | collective-permute-start | bytes 19208 | tf_op jit(solution)/shard_map/ppermute | solution.py:739
  204.3 2.0 collective-permute-done.22
  212.8 3.5 fusion.11
  219.2 2.6 fusion.7
  221.8 5.5 %collective-permute-done.28.refs_1_ = bf16[200,896]{1,0:T(8,128)(2,1)} collective-permute-done((bf16[200,896]{1,0:T(8,128)(2,1)}, bf16[200,896]{1,0:T(8,128)(2,1)}, u32[]{:S(2)}, u32[]{:S(2)}) %collective-permute-start.28) | collective-permute-done | bytes 358432 | tf_op jit(solution)/shard_map/ppermute | solution.py:752
  227.3 20.2 %collective-permute-done.29.refs_2_ = bf16[200,896]{1,0:T(8,128)(2,1)} collective-permute-done((bf16[200,896]{1,0:T(8,128)(2,1)}, bf16[200,896]{1,0:T(8,128)(2,1)}, u32[]{:S(2)}, u32[]{:S(2)}) %collective-permute-start.29) | collective-permute-done | bytes 358432 | tf_op jit(solution)/shard_map/ppermute | solution.py:752
  247.5 2.3 broadcast_in_dim.87.column_ref
  251.1 9.3 %reduce-scatter.7.cloned.1.call-done = bf16[1,4,2,104,808]{4,3,2,1,0:T(8,128)(2,1)} async-done(((bf16[4,4,2,104,808]{4,3,2,1,0:T(8,128)(2,1)}), bf16[1,4,2,104,808]{4,3,2,1,0:T(8,128)(2,1)}) %reduce-scatter.7.cloned.1.call-update) | async-done | bytes 1344528
  261.2 31.2 %input_gradient.1 = (bf16[2,48,48,200]{3,2,1,0:T(8,128)(2,1)}, f32[2,2,54,64,128]{4,3,2,1,0:T(8,128)}) custom-call(s32[22]{0:T(128)} %copy-done.5, bf16[2,48,48,128]{3,2,1,0:T(8,128)(2,1)} %copy-done.2, bf16[2,48,48,200]{3,2,1,0:T(8,128)(2,1)} %cot_ref.3, f32[4,2,12,48,200]{4,3,2,1,0:T(8,128)} %copy-done.8, f32[2,49,8,128]{3,2,1,0:T(8,128)} %copy-done.4, ...), custom_call_target="tpu_custom_call" | custom-call | flops 5366666752 | tf_op jit(solution)/shard_map/input_gradient/pallas_call | solution.py:406
  292.4 4.5 %reduce-scatter.5.cloned.1.call-done = bf16[1,2,104,808]{3,2,1,0:T(8,128)(2,1)} async-done(((bf16[4,2,104,808]{3,2,1,0:T(8,128)(2,1)}), bf16[1,2,104,808]{3,2,1,0:T(8,128)(2,1)}) %reduce-scatter.5.cloned.1.call-update) | async-done | bytes 336144 | tf_op jit(solution)/shard_map/reduce_scatter | solution.py:888
  298.4 2.2 collective-permute-start.33
  300.6 21.0 %taps_gradient.1 = f32[2,49,8,128]{3,2,1,0:T(8,128)} custom-call(bf16[2,48,48,200]{3,2,1,0:T(8,128)(2,1)} %x_ref.2, bf16[2,48,48,128]{3,2,1,0:T(8,128)(2,1)} %copy-done.2, f32[2,2,54,64,128]{4,3,2,1,0:T(8,128)} %get-tuple-element.188.gs_ref), custom_call_target="tpu_custom_call" | custom-call | flops 4216666624 | tf_op jit(solution)/shard_map/taps_gradient/pallas_call | solution.py:464
  327.6 2.2 collective-permute-done.32.refs_2_
  330.7 10.1 %make_output.1 = bf16[2,48,48,200]{3,2,1,0:T(8,128)(2,1)} custom-call(s32[22]{0:T(128)} %copy-done.5, bf16[2,48,48,200]{3,2,1,0:T(8,128)(2,1)} %x_ref.2, bf16[2,48,48,128]{3,2,1,0:T(8,128)(2,1)} %copy-done.2, f32[1,200]{1,0:T(1,128)} %bitcast.156, s32[4,2,576,128]{3,2,1,0:T(8,128)} %broadcast_in_dim.87.column_ref, ...), custom_call_target="tpu_custom_call" | custom-call | flops 2300000000 | tf_op jit(solution)/shard_map/make_output/pallas_call | solution.py:334
  341.5 2.0 copy-done.6
  343.5 3.2 finish_weight_gradients.1
  (201 shorter events, 58.6 us)
Async XLA Ops:
  7.2 61.0 %all-gather.5.cloned.1.call-start = ((), (), s32[]{:S(2)}) async-start(), calls=%async_computation.8 | async-start | bytes 1863680 | tf_op jit(solution)/shard_map/all_gather | solution.py:781
  10.0 6.2 %collective-permute-start.3 = (s32[4]{0:T(128)S(1)}, s32[4]{0:T(128)S(1)}, u32[]{:S(2)}, u32[]{:S(2)}) collective-permute-start(s32[4]{0:T(128)S(1)} %convert_element_type.207), channel_id=1, source_target_pairs={{0,4},{4,0},{1,5},{5,1},{2,6},{6,2},{3,7},{7,3},{8,12},{12,8},{9,1... | collective-permute-start | bytes 56 | tf_op jit(solution)/shard_map/ppermute | solution.py:760
  27.0 56.7 %all-to-all-start.4 = ((bf16[4,200,896]{2,1,0:T(8,128)(2,1)}), bf16[4,200,896]{2,1,0:T(8,128)(2,1)}, u32[]{:S(2)}, u32[]{:S(2)}) async-start(bf16[4,200,896]{2,1,0:T(8,128)(2,1)} %get-tuple-element.124), calls=%async_computation.4 | async-start | bytes 2867200 | tf_op jit(solution)/shard_map/all_to_all | solution.py:755
  32.9 227.5 %reduce-scatter.7.cloned.1.call-start = ((), (), s32[]{:S(2)}) async-start(), calls=%async_computation.10 | async-start | bytes 7454720
  63.0 4.5 %collective-permute-start.7 = (f32[4,200]{1,0:T(4,128)S(1)}, f32[4,200]{1,0:T(4,128)S(1)}, u32[]{:S(2)}, u32[]{:S(2)}) collective-permute-start(f32[4,200]{1,0:T(4,128)S(1)} %fusion.40), channel_id=1, source_target_pairs={{0,24},{8,16},{16,8},{24,0},{1,25},{9,17},{17,9},{25,1},{2,26},{10... | collective-permute-start | bytes 9608 | tf_op jit(solution)/shard_map/ppermute | solution.py:739
  69.7 17.9 %collective-permute-start.8 = (bf16[4,104,808]{2,1,0:T(8,128)(2,1)S(1)}, bf16[4,104,808]{2,1,0:T(8,128)(2,1)}, u32[]{:S(2)}, u32[]{:S(2)}) collective-permute-start(bf16[4,104,808]{2,1,0:T(8,128)(2,1)S(1)} %get-tuple-element.133.refs_0_), channel_id=1, source_target_pairs={{0,8},{8,0},{16,24},{24,16},{1,9},{9,1},{17,25},{25,17},{2,10},{10... | collective-permute-start | bytes 2016776 | tf_op jit(solution)/shard_map/ppermute | solution.py:827
  71.1 17.5 %collective-permute-start.9 = (bf16[4,104,808]{2,1,0:T(8,128)(2,1)S(1)}, bf16[4,104,808]{2,1,0:T(8,128)(2,1)}, u32[]{:S(2)}, u32[]{:S(2)}) collective-permute-start(bf16[4,104,808]{2,1,0:T(8,128)(2,1)S(1)} %get-tuple-element.137.refs_4_), channel_id=1, source_target_pairs={{0,16},{8,24},{16,0},{24,8},{1,17},{9,25},{17,1},{25,9},{2,18},{10... | collective-permute-start | bytes 2016776 | tf_op jit(solution)/shard_map/ppermute | solution.py:827
  88.6 18.7 %collective-permute-start.10 = (bf16[200,896]{1,0:T(8,128)(2,1)S(1)}, bf16[200,896]{1,0:T(8,128)(2,1)S(1)}, u32[]{:S(2)}, u32[]{:S(2)}) collective-permute-start(bf16[200,896]{1,0:T(8,128)(2,1)S(1)} %get-tuple-element.126), channel_id=1, source_target_pairs={{0,1},{1,2},{2,3},{3,0},{4,5},{5,6},{6,7},{7,4},{8,9},{9,10},{10,1... | collective-permute-start | bytes 1075208 | tf_op jit(solution)/shard_map/ppermute | solution.py:752
  90.1 30.6 %collective-permute-start.11 = (bf16[200,896]{1,0:T(8,128)(2,1)S(1)}, bf16[200,896]{1,0:T(8,128)(2,1)S(1)}, u32[]{:S(2)}, u32[]{:S(2)}) collective-permute-start(bf16[200,896]{1,0:T(8,128)(2,1)S(1)} %get-tuple-element.127), channel_id=1, source_target_pairs={{0,2},{1,3},{2,0},{3,1},{4,6},{5,7},{6,4},{7,5},{8,10},{9,11},{10,... | collective-permute-start | bytes 1075208 | tf_op jit(solution)/shard_map/ppermute | solution.py:752
  98.5 32.5 %collective-permute-start.13 = (bf16[4,104,808]{2,1,0:T(8,128)(2,1)S(1)}, bf16[4,104,808]{2,1,0:T(8,128)(2,1)S(1)}, u32[]{:S(2)}, u32[]{:S(2)}) collective-permute-start(bf16[4,104,808]{2,1,0:T(8,128)(2,1)S(1)} %get-tuple-element.133.refs_0_), channel_id=1, source_target_pairs={{0,16},{8,24},{16,0},{24,8},{1,17},{9,25},{17,1},{25,9},{2,18},{10... | collective-permute-start | bytes 2016776 | tf_op jit(solution)/shard_map/ppermute | solution.py:827
  100.0 31.4 %collective-permute-start.14 = (bf16[4,104,808]{2,1,0:T(8,128)(2,1)}, bf16[4,104,808]{2,1,0:T(8,128)(2,1)S(1)}, u32[]{:S(2)}, u32[]{:S(2)}) collective-permute-start(bf16[4,104,808]{2,1,0:T(8,128)(2,1)} %collective-permute-done.8.refs_1_), channel_id=1, source_target_pairs={{0,16},{8,24},{16,0},{24,8},{1,17},{9,25},{17,1},{25,9},{2,18},{10... | collective-permute-start | bytes 2016776 | tf_op jit(solution)/shard_map/ppermute | solution.py:827
  100.5 30.9 %collective-permute-start.15 = (bf16[4,104,808]{2,1,0:T(8,128)(2,1)S(1)}, bf16[4,104,808]{2,1,0:T(8,128)(2,1)S(1)}, u32[]{:S(2)}, u32[]{:S(2)}) collective-permute-start(bf16[4,104,808]{2,1,0:T(8,128)(2,1)S(1)} %get-tuple-element.137.refs_4_), channel_id=1, source_target_pairs={{0,8},{8,0},{16,24},{24,16},{1,9},{9,1},{17,25},{25,17},{2,10},{10... | collective-permute-start | bytes 2016776 | tf_op jit(solution)/shard_map/ppermute | solution.py:827
  107.3 25.5 %collective-permute-start.16 = (bf16[4,104,808]{2,1,0:T(8,128)(2,1)}, bf16[4,104,808]{2,1,0:T(8,128)(2,1)S(1)}, u32[]{:S(2)}, u32[]{:S(2)}) collective-permute-start(bf16[4,104,808]{2,1,0:T(8,128)(2,1)} %collective-permute-done.9.refs_6_), channel_id=1, source_target_pairs={{0,8},{8,0},{16,24},{24,16},{1,9},{9,1},{17,25},{25,17},{2,10},{10... | collective-permute-start | bytes 2016776 | tf_op jit(solution)/shard_map/ppermute | solution.py:827
  120.7 10.3 %collective-permute-start.12 = (bf16[200,896]{1,0:T(8,128)(2,1)S(1)}, bf16[200,896]{1,0:T(8,128)(2,1)S(1)}, u32[]{:S(2)}, u32[]{:S(2)}) collective-permute-start(bf16[200,896]{1,0:T(8,128)(2,1)S(1)} %get-tuple-element.128), channel_id=1, source_target_pairs={{0,3},{1,0},{2,1},{3,2},{4,7},{5,4},{6,5},{7,6},{8,11},{9,8},{10,9... | collective-permute-start | bytes 1075208 | tf_op jit(solution)/shard_map/ppermute | solution.py:752
  131.0 4.3 %collective-permute-start.18 = (bf16[4,200,896]{2,1,0:T(8,128)(2,1)}, bf16[4,200,896]{2,1,0:T(8,128)(2,1)}, u32[]{:S(2)}, u32[]{:S(2)}) collective-permute-start(bf16[4,200,896]{2,1,0:T(8,128)(2,1)} %all-to-all-done.4.refs_10_), channel_id=1, source_target_pairs={{0,4},{4,0},{1,5},{5,1},{2,6},{6,2},{3,7},{7,3},{8,12},{12,8},{9,1... | collective-permute-start | bytes 4300808 | tf_op jit(solution)/shard_map/ppermute | solution.py:760
  188.4 108.4 %reduce-scatter.5.cloned.1.call-start = ((), (), s32[]{:S(2)}) async-start(), calls=%async_computation.7 | async-start | bytes 1863680 | tf_op jit(solution)/shard_map/reduce_scatter | solution.py:888
  189.8 23.1 %collective-permute-start.20 = (bf16[4,200,896]{2,1,0:T(8,128)(2,1)S(1)}, bf16[4,200,896]{2,1,0:T(8,128)(2,1)}, u32[]{:S(2)}, u32[]{:S(2)}) collective-permute-start(bf16[4,200,896]{2,1,0:T(8,128)(2,1)S(1)} %copy-done.27), channel_id=1, source_target_pairs={{0,4},{4,0},{1,5},{5,1},{2,6},{6,2},{3,7},{7,3},{8,12},{12,8},{9,1... | collective-permute-start | bytes 4300808 | tf_op jit(solution)/shard_map/ppermute | solution.py:760
  189.9 29.3 %collective-permute-start.19 = (bf16[4,200,896]{2,1,0:T(8,128)(2,1)}, bf16[4,200,896]{2,1,0:T(8,128)(2,1)}, u32[]{:S(2)}, u32[]{:S(2)}) collective-permute-start(bf16[4,200,896]{2,1,0:T(8,128)(2,1)} %get-tuple-element.150), channel_id=1, source_target_pairs={{0,4},{4,0},{1,5},{5,1},{2,6},{6,2},{3,7},{7,3},{8,12},{12,8},{9,1... | collective-permute-start | bytes 4300808 | tf_op jit(solution)/shard_map/ppermute | solution.py:760
  194.0 9.9 %collective-permute-start.24 = (f32[4,2,200]{2,1,0:T(2,128)S(1)}, f32[4,2,200]{2,1,0:T(2,128)S(1)}, u32[]{:S(2)}, u32[]{:S(2)}) collective-permute-start(f32[4,2,200]{2,1,0:T(2,128)S(1)} %add.177), channel_id=1, source_target_pairs={{0,24},{8,16},{16,8},{24,0},{1,25},{9,17},{17,9},{25,1},{2,26},{10... | collective-permute-start | bytes 19208 | tf_op jit(solution)/shard_map/ppermute | solution.py:739
  194.0 10.3 %collective-permute-start.23 = (f32[4,2,200]{2,1,0:T(2,128)S(1)}, f32[4,2,200]{2,1,0:T(2,128)S(1)}, u32[]{:S(2)}, u32[]{:S(2)}) collective-permute-start(f32[4,2,200]{2,1,0:T(2,128)S(1)} %add.177), channel_id=1, source_target_pairs={{0,16},{8,24},{16,0},{24,8},{1,17},{9,25},{17,1},{25,9},{2,18},{10... | collective-permute-start | bytes 19208 | tf_op jit(solution)/shard_map/ppermute | solution.py:739
  206.4 4.5 %collective-permute-start.26 = (f32[2,200]{1,0:T(2,128)S(1)}, f32[2,200]{1,0:T(2,128)S(1)}, u32[]{:S(2)}, u32[]{:S(2)}) collective-permute-start(f32[2,200]{1,0:T(2,128)S(1)} %get-tuple-element.225), channel_id=1, source_target_pairs={{0,2},{1,3},{2,0},{3,1},{4,6},{5,7},{6,4},{7,5},{8,10},{9,11},{10,... | collective-permute-start | bytes 4808 | tf_op jit(solution)/shard_map/ppermute | solution.py:752
  207.4 5.4 %collective-permute-start.27 = (f32[2,200]{1,0:T(2,128)S(1)}, f32[2,200]{1,0:T(2,128)S(1)}, u32[]{:S(2)}, u32[]{:S(2)}) collective-permute-start(f32[2,200]{1,0:T(2,128)S(1)} %get-tuple-element.224), channel_id=1, source_target_pairs={{0,1},{1,2},{2,3},{3,0},{4,5},{5,6},{6,7},{7,4},{8,9},{9,10},{10,1... | collective-permute-start | bytes 4808 | tf_op jit(solution)/shard_map/ppermute | solution.py:752
  216.4 10.9 %collective-permute-start.28 = (bf16[200,896]{1,0:T(8,128)(2,1)}, bf16[200,896]{1,0:T(8,128)(2,1)}, u32[]{:S(2)}, u32[]{:S(2)}) collective-permute-start(bf16[200,896]{1,0:T(8,128)(2,1)} %get-tuple-element.156), channel_id=1, source_target_pairs={{0,3},{1,0},{2,1},{3,2},{4,7},{5,4},{6,5},{7,6},{8,11},{9,8},{10,9... | collective-permute-start | bytes 1075208 | tf_op jit(solution)/shard_map/ppermute | solution.py:752
  218.2 29.3 %collective-permute-start.29 = (bf16[200,896]{1,0:T(8,128)(2,1)}, bf16[200,896]{1,0:T(8,128)(2,1)}, u32[]{:S(2)}, u32[]{:S(2)}) collective-permute-start(bf16[200,896]{1,0:T(8,128)(2,1)} %get-tuple-element.157), channel_id=1, source_target_pairs={{0,2},{1,3},{2,0},{3,1},{4,6},{5,7},{6,4},{7,5},{8,10},{9,11},{10,... | collective-permute-start | bytes 1075208 | tf_op jit(solution)/shard_map/ppermute | solution.py:752
  218.2 29.3 %collective-permute-start.30 = (bf16[200,896]{1,0:T(8,128)(2,1)}, bf16[200,896]{1,0:T(8,128)(2,1)}, u32[]{:S(2)}, u32[]{:S(2)}) collective-permute-start(bf16[200,896]{1,0:T(8,128)(2,1)} %get-tuple-element.158), channel_id=1, source_target_pairs={{0,1},{1,2},{2,3},{3,0},{4,5},{5,6},{6,7},{7,4},{8,9},{9,10},{10,1... | collective-permute-start | bytes 1075208 | tf_op jit(solution)/shard_map/ppermute | solution.py:752
  261.0 80.5 %all-gather.7.cloned.1.call-start = ((), (), s32[]{:S(2)}) async-start(), calls=%async_computation.9 | async-start | bytes 3354624 | tf_op jit(solution)/shard_map/all_gather | solution.py:893
  296.9 30.2 %collective-permute-start.31 = (bf16[200,896]{1,0:T(8,128)(2,1)S(1)}, bf16[200,896]{1,0:T(8,128)(2,1)S(1)}, u32[]{:S(2)}, u32[]{:S(2)}) collective-permute-start(bf16[200,896]{1,0:T(8,128)(2,1)S(1)} %copy-done.21), channel_id=1, source_target_pairs={{0,3},{1,0},{2,1},{3,2},{4,7},{5,4},{6,5},{7,6},{8,11},{9,8},{10,9... | collective-permute-start | bytes 1075208 | tf_op jit(solution)/shard_map/ppermute | solution.py:752
  298.3 31.5 %collective-permute-start.32 = (bf16[200,896]{1,0:T(8,128)(2,1)S(1)}, bf16[200,896]{1,0:T(8,128)(2,1)S(1)}, u32[]{:S(2)}, u32[]{:S(2)}) collective-permute-start(bf16[200,896]{1,0:T(8,128)(2,1)S(1)} %copy-done.20), channel_id=1, source_target_pairs={{0,2},{1,3},{2,0},{3,1},{4,6},{5,7},{6,4},{7,5},{8,10},{9,11},{10,... | collective-permute-start | bytes 1075208 | tf_op jit(solution)/shard_map/ppermute | solution.py:752
  298.4 31.4 %collective-permute-start.33 = (bf16[200,896]{1,0:T(8,128)(2,1)S(1)}, bf16[200,896]{1,0:T(8,128)(2,1)S(1)}, u32[]{:S(2)}, u32[]{:S(2)}) collective-permute-start(bf16[200,896]{1,0:T(8,128)(2,1)S(1)} %get-tuple-element.172), channel_id=1, source_target_pairs={{0,1},{1,2},{2,3},{3,0},{4,5},{5,6},{6,7},{7,4},{8,9},{9,10},{10,1... | collective-permute-start | bytes 1075208 | tf_op jit(solution)/shard_map/ppermute | solution.py:752
  324.1 16.8 %collective-permute-start.35 = (f32[49,256]{1,0:T(8,128)S(1)}, f32[49,256]{1,0:T(8,128)S(1)}, u32[]{:S(2)}, u32[]{:S(2)}) collective-permute-start(f32[49,256]{1,0:T(8,128)S(1)} %add.184), channel_id=1, source_target_pairs={{0,8},{8,0},{16,24},{24,16},{1,9},{9,1},{17,25},{25,17},{2,10},{10... | collective-permute-start | bytes 150536 | tf_op jit(solution)/shard_map/ppermute | solution.py:739
  325.6 15.3 %collective-permute-start.36 = (f32[49,256]{1,0:T(8,128)S(1)}, f32[49,256]{1,0:T(8,128)S(1)}, u32[]{:S(2)}, u32[]{:S(2)}) collective-permute-start(f32[49,256]{1,0:T(8,128)S(1)} %add.184), channel_id=1, source_target_pairs={{0,16},{8,24},{16,0},{24,8},{1,17},{9,25},{17,1},{25,9},{2,18},{10... | collective-permute-start | bytes 150536 | tf_op jit(solution)/shard_map/ppermute | solution.py:739
  327.1 13.8 %collective-permute-start.37 = (f32[49,256]{1,0:T(8,128)S(1)}, f32[49,256]{1,0:T(8,128)S(1)}, u32[]{:S(2)}, u32[]{:S(2)}) collective-permute-start(f32[49,256]{1,0:T(8,128)S(1)} %add.184), channel_id=1, source_target_pairs={{0,24},{8,16},{16,8},{24,0},{1,25},{9,17},{17,9},{25,1},{2,26},{10... | collective-permute-start | bytes 150536 | tf_op jit(solution)/shard_map/ppermute | solution.py:739
  (42 other events, 403.2 us)
Sparse Core Ops, SparseCore 0:
  13.8 54.3 all-gather.4
  188.6 71.7 reduce-scatter.6
  262.7 34.1 reduce-scatter.4
  298.8 31.3 all-gather.6

commit v4 on v3

--- a/solution.py
+++ b/solution.py
@@ -188,41 +188,35 @@
             ref[width:, lo : lo + count] = jnp.zeros((ref.shape[0] - width, count), BF)
 
 
-def pack_normed_kernel(at_ref, conv_ref, vec_ref, slot_ref, *out_refs):
-    k = pl.program_id(0)
-    base_refs, over_ref = out_refs[:-1], out_refs[-1]
-    part = lax.rem(at_ref[0] + k, len(base_refs))
+def pack_normed_kernel(at_ref, conv_ref, vec_ref, slot_ref, base_ref, over_ref):
     normed = (conv_ref[0] * vec_ref[0:1, :] + vec_ref[1:2, :]).T.astype(BF)
-    for j, base_ref in enumerate(base_refs):
-
-        @pl.when(k == j)
-        def _():
-            pack_columns(normed, slot_ref[0], at_ref[1 + part], base_ref, over_ref.at[part])
+    used = at_ref[1 + pl.program_id(0)]
+    pack_columns(normed, slot_ref[0], used, base_ref.at[0], over_ref.at[0])
 
 
 def pack_normed(at, conv, vec, slots, base, over):
     parts, cells, width = conv.shape
     wide = ceil_to(width, 8)
-    part = lambda k, at: (lax.rem(at[0] + k, parts), 0, 0)
-    *pieces, more = pl.pallas_call(
+    return pl.pallas_call(
         pack_normed_kernel,
         grid_spec=pltpu.PrefetchScalarGridSpec(
             num_scalar_prefetch=1,
             grid=(parts,),
             in_specs=[
-                pl.BlockSpec((1, cells, width), part),
+                pl.BlockSpec((1, cells, width), lambda k, at: (k, 0, 0)),
                 pl.BlockSpec(vec.shape, lambda k, at: (0, 0)),
-                pl.BlockSpec((1, 1, cells), part),
+                pl.BlockSpec((1, 1, cells), lambda k, at: (k, 0, 0)),
             ],
-            out_specs=[pl.BlockSpec((wide, base), lambda k, at: (0, 0))] * parts
-            + [pl.BlockSpec((parts, wide, over), lambda k, at: (0, 0, 0))],
+            out_specs=[
+                pl.BlockSpec((1, wide, base), lambda k, at: (k, 0, 0)),
+                pl.BlockSpec((1, wide, over), lambda k, at: (k, 0, 0)),
+            ],
         ),
-        out_shape=[jax.ShapeDtypeStruct((wide, base), BF)] * parts + [jax.ShapeDtypeStruct((parts, wide, over), BF)],
+        out_shape=[jax.ShapeDtypeStruct((parts, wide, base), BF), jax.ShapeDtypeStruct((parts, wide, over), BF)],
         compiler_params=params(32),
         cost_estimate=cost(8),
         name="pack_normed",
     )(at, conv, vec, slots)
-    return pieces, more
 
 
 def pack_cotangent_kernel(at_ref, cot_ref, m_ref, slot_ref, base_ref, over_ref, sum_ref, rows):
@@ -537,7 +531,7 @@
     _, slab, wide = up_refs[0].shape
     units = chips * parts * slab
     channels = parts * width
-    block = units // 8
+    block = LANES
     me, chip = at_ref[0], at_ref[1 + 2 * parts]
     used = at_ref[1 + whose * parts + me]
 
@@ -583,9 +577,8 @@
             def _():
                 for refs, place in ((x_refs, x_place), (g_refs, g_place)):
                     for s in range(parts):
-                        k = lax.rem(me - s + parts, parts) if place is x_place else s
                         at = slice(s * width, (s + 1) * width)
-                        values = [refs[is_over][s if is_over else k, :, lanes].astype(F32) for is_over, lanes, _ in found]
+                        values = [refs[is_over][s, :, lanes].astype(F32) for is_over, lanes, _ in found]
                         filled = sum(v.shape[1] for v in values)
                         if filled < TILE:
                             values.append(jnp.zeros((width, TILE - filled), F32))
@@ -614,11 +607,12 @@
         def fold(v):
             return sum(v[:, lo : lo + LANES] for lo in range(0, TILE, LANES))
 
+        branches = nn(down_t[...], hidden[...])
+        normeds = nn(up_t[...], grad_pre[...])
         for s in range(parts):
             rows = slice(s * width, (s + 1) * width)
             k = lax.rem(me - s + parts, parts)
-            branch = nn(down_t[rows, :], hidden[...])
-            normed = nn(up_t[rows, :], grad_pre[...])
+            branch, normed = branches[rows, :], normeds[rows, :]
             sums_ref[k, 0] += fold(normed)
             sums_ref[k, 1] += fold(normed * x_place[rows, :])
             for side in range(2):
@@ -840,14 +834,15 @@
     affine = jnp.stack([scale, shift - channel_mean * scale])
     normed_base, normed_over = pack_normed(at, convolved.reshape(parts, cells, width), affine, slots, base, over)
     places = sorted(ups), sorted(downs)
-    *both, grad_base = after(*normed_base, *[ups[p] for p in places[0]], *[downs[p] for p in places[1]], grad_base)
-    normed_base, held = both[:parts], both[parts:]
+    normed_base, grad_base, *held = after(
+        normed_base, grad_base, *[ups[p] for p in places[0]], *[downs[p] for p in places[1]]
+    )
     ups, downs = dict(zip(places[0], held)), dict(zip(places[1], held[len(ups) :]))
     for j in range(1, len(bits)):
         ups, downs = double(ups, bits[j]), double(downs, bits[-1 - j])
     ups, downs = [ups[p] for p in range(chips)], [downs[p] for p in range(chips)]
-    *both, crowded = after(*to_parts(normed_base), *ups, *downs, overflows)
-    x_base, ups, downs = jnp.stack(both[:parts]), both[parts : parts + chips], both[parts + chips :]
+    x_base, crowded, *held = after(exchange(normed_base), overflows, *ups, *downs)
+    ups, downs = held[:chips], held[chips:]
 
     def overflow_in():
         own = jnp.stack([exchange(normed_over), exchange(cot_over)])

time: 358 us -> 347 us (0.969)
  Pallas kernels: 153 us -> 147 us
    ppermute x12 -> x9, waiting for transfers between devices: 61.1 us -> 31.8 us  [to_parts(): lax.ppermute(pieces[k], 'mp', ring(k))]
    ppermute x6, waiting for transfers between devices: 6.17 us -> 33 us  [double(): lax.ppermute(value, 'xy', pairs)]
    all_to_all x1 -> x2, starting transfers between devices: 5.92 us -> 16.6 us  [exchange(): return lax.all_to_all(by_part, 'mp', 0, 0, tiled=True)]
    ppermute x12 -> x9, starting transfers between devices: 18.6 us -> 11 us  [to_parts(): lax.ppermute(pieces[k], 'mp', ring(k))]
    ppermute x12, starting transfers between devices: 17.3 us -> 10.9 us  [everywhere(): lax.ppermute(value, axis, [(i, i ^ j) for i in range(size)])]
    pallas_call x1, Pallas kernels: 49.8 us -> 44.2 us  [pointwise(): pl.pallas_call(functools.partial(pointwise_kernel, chips=chips, parts=par...]
    unnamed x72 -> x70, local copies, waits for them, and re-layouts: 13.7 us -> 14 us
  transfers between devices with their start and end apart: 40 -> 38, of which waited for: 25 -> 22; matrix products, arithmetic and copies ran while one was open for 7% -> 7% of each run, Pallas kernels for 28% -> 29%
where the time goes in v4:
time: 347 us; the launch traced here: 343 us
  Pallas kernels  147 us (42%)
  waiting for transfers between devices  93.1 us (27%)
  starting transfers between devices  46.7 us (13%)
  local copies, waits for them, and re-layouts  25 us (7%)
  between operations  15.6 us (4%)
  other arithmetic  14.8 us (4%)
    pallas_call x1, Pallas kernels, pointwise(): pl.pallas_call(functools.partial(pointwise_kernel, chips=chips, parts=par...  44.2 us
    ppermute x6, waiting for transfers between devices, double(): lax.ppermute(value, 'xy', pairs)  33 us
    ppermute x9, waiting for transfers between devices, to_parts(): lax.ppermute(pieces[k], 'mp', ring(k))  31.8 us
    pallas_call x1, Pallas kernels, input_gradient(): pl.pallas_call(functools.partial(input_gradient_kernel, taps=taps, rows=r...  31.2 us
    pallas_call x1, Pallas kernels, conv_forward(): pl.pallas_call(functools.partial(forward_kernel, taps=taps, rows=rows, gr...  22 us
    pallas_call x1, Pallas kernels, taps_gradient(): pl.pallas_call(functools.partial(taps_gradient_kernel, taps=taps, rows=ro...  21 us
    all_to_all x2, starting transfers between devices, exchange(): return lax.all_to_all(by_part, 'mp', 0, 0, tiled=True)  16.6 us
    unnamed x70, local copies, waits for them, and re-layouts  14 us
  transfers between devices with their start and end apart: 38, of which 22 were waited for; matrix products, arithmetic and copies ran while one was open for 7% of the time, Pallas kernels for 29%

profile of v4, /device:TPU:0, one launch (start us, length us, event | category | flops | bytes accessed | tf_op | source)
XLA Modules:
  0.0 342.7 jit_solution(4041925426043037426)
XLA Ops:
  18.7 8.2 %pack_cotangent.1 = (bf16[4,200,896]{2,1,0:T(8,128)(2,1)}, bf16[4,200,256]{2,1,0:T(8,128)(2,1)}, f32[8,200]{1,0:T(8,128)S(1)}) custom-call(s32[22]{0:T(128)S(1)} %concatenate.9.at_ref, bf16[2,48,48,200]{3,2,1,0:T(8,128)(2,1)S(1)} %copy-done.7, bf16[2,48,48,128]{3,2,1,0:T(8,128)(2,1)S(1)} %broadcast_in_dim.74.m_ref, s32[4,1,1152]{2,1,0:T(1,128)S(1)} %reshape.141.slot_ref), custom_call_target="tpu_custom_call" | custom-call | flops 1916666624 | tf_op jit(solution)/shard_map/pack_cotangent/pallas_call | solution.py:254
  27.0 5.9 %all-to-all-start.4 = ((bf16[4,200,896]{2,1,0:T(8,128)(2,1)}), bf16[4,200,896]{2,1,0:T(8,128)(2,1)S(1)}, u32[]{:S(2)}, u32[]{:S(2)}) async-start(bf16[4,200,896]{2,1,0:T(8,128)(2,1)} %get-tuple-element.111), calls=%async_computation.4 | async-start | bytes 2867200 | tf_op jit(solution)/shard_map/all_to_all | solution.py:749
  35.3 22.0 %depthwise_forward.1 = (f32[4,2,12,48,200]{4,3,2,1,0:T(8,128)S(1)}, f32[2,2,2,8,128]{4,3,2,1,0:T(8,128)S(1)}) custom-call(bf16[2,48,48,200]{3,2,1,0:T(8,128)(2,1)S(1)} %copy-done.3, bf16[2,48,48,128]{3,2,1,0:T(8,128)(2,1)S(1)} %broadcast_in_dim.74.m_ref, f32[2,49,8,128]{3,2,1,0:T(8,128)S(1)} %broadcast_in_dim.83.w_ref), custom_call_target="tpu_custom_call" | custom-call | flops 4216666624 | tf_op jit(solution)/shard_map/depthwise_forward/pallas_call | solution.py:130
  57.4 2.1 copy-done.8
  62.5 1.9 collective-permute-start.7
  70.3 2.2 collective-permute-start.9
  74.3 2.3 copy-done.9
  76.6 6.9 %pack_normed.1 = (bf16[4,200,896]{2,1,0:T(8,128)(2,1)}, bf16[4,200,256]{2,1,0:T(8,128)(2,1)}) custom-call(s32[22]{0:T(128)S(1)} %concatenate.9.at_ref, f32[4,1152,200]{2,1,0:T(8,128)S(1)} %bitcast.107, f32[2,200]{1,0:T(2,128)S(1)} %pad_maximum_fusion.6.vec_ref, s32[4,1,1152]{2,1,0:T(1,128)S(1)} %reshape.141.slot_ref), custom_call_target="tpu_custom_call" | custom-call | flops 1533333376 | tf_op jit(solution)/shard_map/pack_normed/pallas_call | solution.py:200
  83.6 3.9 %collective-permute-done.8.refs_1_ = bf16[4,104,808]{2,1,0:T(8,128)(2,1)} collective-permute-done((bf16[4,104,808]{2,1,0:T(8,128)(2,1)S(1)}, bf16[4,104,808]{2,1,0:T(8,128)(2,1)}, u32[]{:S(2)}, u32[]{:S(2)}) %collective-permute-start.8) | collective-permute-done | bytes 672288 | tf_op jit(solution)/shard_map/ppermute | solution.py:821
  88.2 10.7 %all-to-all-start.5 = ((bf16[4,200,896]{2,1,0:T(8,128)(2,1)}), bf16[4,200,896]{2,1,0:T(8,128)(2,1)}, u32[]{:S(2)}, u32[]{:S(2)}) async-start(bf16[4,200,896]{2,1,0:T(8,128)(2,1)} %get-tuple-element.113), calls=%async_computation.5 | async-start | bytes 2867200 | tf_op jit(solution)/shard_map/all_to_all | solution.py:749
  103.8 14.8 %collective-permute-done.10.refs_2_ = bf16[4,104,808]{2,1,0:T(8,128)(2,1)S(1)} collective-permute-done((bf16[4,104,808]{2,1,0:T(8,128)(2,1)S(1)}, bf16[4,104,808]{2,1,0:T(8,128)(2,1)S(1)}, u32[]{:S(2)}, u32[]{:S(2)}) %collective-permute-start.10) | collective-permute-done | bytes 672288 | tf_op jit(solution)/shard_map/ppermute | solution.py:821
  118.6 13.6 %collective-permute-done.11.refs_3_ = bf16[4,104,808]{2,1,0:T(8,128)(2,1)S(1)} collective-permute-done((bf16[4,104,808]{2,1,0:T(8,128)(2,1)}, bf16[4,104,808]{2,1,0:T(8,128)(2,1)S(1)}, u32[]{:S(2)}, u32[]{:S(2)}) %collective-permute-start.11) | collective-permute-done | bytes 672288 | tf_op jit(solution)/shard_map/ppermute | solution.py:821
  134.3 3.2 collective-permute-done.14.refs_9_
  137.5 44.2 %pointwise.1 = (f32[4,200,896]{2,1,0:T(8,128)}, f32[4,200,256]{2,1,0:T(8,128)}, bf16[4,200,896]{2,1,0:T(8,128)(2,1)}, bf16[4,200,256]{2,1,0:T(8,128)(2,1)}, f32[...) custom-call(s32[22]{0:T(128)} %copy-done.5, ...), custom_call_target="tpu_custom_call" | custom-call | flops 13416667136 | tf_op jit(solution)/shard_map/pointwise/pallas_call | solution.py:659
  184.1 3.1 collective-permute-done.18
  192.9 3.5 %collective-permute-start.22 = (f32[2,200]{1,0:T(2,128)S(1)}, f32[2,200]{1,0:T(2,128)S(1)}, u32[]{:S(2)}, u32[]{:S(2)}) collective-permute-start(f32[2,200]{1,0:T(2,128)S(1)} %get-tuple-element.205), channel_id=1, source_target_pairs={{0,3},{1,0},{2,1},{3,2},{4,7},{5,4},{6,5},{7,6},{8,11},{9,8},{10,9... | collective-permute-start | bytes 4808 | tf_op jit(solution)/shard_map/ppermute | solution.py:746
  197.7 3.2 collective-permute-done.23
  201.8 3.6 %fusion.11 = (bf16[200,896]{1,0:T(8,128)(2,1)}, bf16[200,896]{1,0:T(8,128)(2,1)}, bf16[200,896]{1,0:T(8,128)(2,1)}, bf16[200,896]{1,0:T(8,128)(2,1)}) fusion(f32[4,200,896]{2,1,0:T(8,128)} %get-tuple-element.133, bf16[4,200,896]{2,1,0:T(8,128)(2,1)} %collective-permute-done.17), kind=kLoop, calls=%fused_computation.37 | loop fusion | flops 2150400 | bytes 5734400 | tf_op jit(solution)/shard_map/convert_element_type | solution.py:858
  206.5 2.0 collective-permute-start.27
  208.6 2.4 fusion.7
  211.1 4.4 %collective-permute-done.25.refs_1_ = bf16[200,896]{1,0:T(8,128)(2,1)} collective-permute-done((bf16[200,896]{1,0:T(8,128)(2,1)}, bf16[200,896]{1,0:T(8,128)(2,1)}, u32[]{:S(2)}, u32[]{:S(2)}) %collective-permute-start.25) | collective-permute-done | bytes 358432 | tf_op jit(solution)/shard_map/ppermute | solution.py:746
  215.5 20.6 %collective-permute-done.26.refs_2_ = bf16[200,896]{1,0:T(8,128)(2,1)} collective-permute-done((bf16[200,896]{1,0:T(8,128)(2,1)}, bf16[200,896]{1,0:T(8,128)(2,1)}, u32[]{:S(2)}, u32[]{:S(2)}) %collective-permute-start.26) | collective-permute-done | bytes 358432 | tf_op jit(solution)/shard_map/ppermute | solution.py:746
  236.1 2.3 broadcast_in_dim.87.column_ref
  239.6 9.6 %reduce-scatter.7.cloned.1.call-done = bf16[1,4,2,104,808]{4,3,2,1,0:T(8,128)(2,1)} async-done(((bf16[4,4,2,104,808]{4,3,2,1,0:T(8,128)(2,1)}), bf16[1,4,2,104,808]{4,3,2,1,0:T(8,128)(2,1)}) %reduce-scatter.7.cloned.1.call-update) | async-done | bytes 1344528
  250.1 31.2 %input_gradient.1 = (bf16[2,48,48,200]{3,2,1,0:T(8,128)(2,1)}, f32[2,2,54,64,128]{4,3,2,1,0:T(8,128)}) custom-call(s32[22]{0:T(128)} %copy-done.5, bf16[2,48,48,128]{3,2,1,0:T(8,128)(2,1)} %copy-done.2, bf16[2,48,48,200]{3,2,1,0:T(8,128)(2,1)} %cot_ref.3, f32[4,2,12,48,200]{4,3,2,1,0:T(8,128)} %copy-done.8, f32[2,49,8,128]{3,2,1,0:T(8,128)} %copy-done.4, ...), custom_call_target="tpu_custom_call" | custom-call | flops 5366666752 | tf_op jit(solution)/shard_map/input_gradient/pallas_call | solution.py:400
  281.2 4.5 %reduce-scatter.5.cloned.1.call-done = bf16[1,2,104,808]{3,2,1,0:T(8,128)(2,1)} async-done(((bf16[4,2,104,808]{3,2,1,0:T(8,128)(2,1)}), bf16[1,2,104,808]{3,2,1,0:T(8,128)(2,1)}) %reduce-scatter.5.cloned.1.call-update) | async-done | bytes 336144 | tf_op jit(solution)/shard_map/reduce_scatter | solution.py:883
  287.3 1.9 collective-permute-start.30
  289.2 21.0 %taps_gradient.1 = f32[2,49,8,128]{3,2,1,0:T(8,128)} custom-call(bf16[2,48,48,200]{3,2,1,0:T(8,128)(2,1)} %x_ref.2, bf16[2,48,48,128]{3,2,1,0:T(8,128)(2,1)} %copy-done.2, f32[2,2,54,64,128]{4,3,2,1,0:T(8,128)} %get-tuple-element.170.gs_ref), custom_call_target="tpu_custom_call" | custom-call | flops 4216666624 | tf_op jit(solution)/shard_map/taps_gradient/pallas_call | solution.py:458
  316.3 2.4 collective-permute-done.29.refs_2_
  319.5 10.2 %make_output.1 = bf16[2,48,48,200]{3,2,1,0:T(8,128)(2,1)} custom-call(s32[22]{0:T(128)} %copy-done.5, bf16[2,48,48,200]{3,2,1,0:T(8,128)(2,1)} %x_ref.2, bf16[2,48,48,128]{3,2,1,0:T(8,128)(2,1)} %copy-done.2, f32[1,200]{1,0:T(1,128)} %bitcast.148, s32[4,2,576,128]{3,2,1,0:T(8,128)} %broadcast_in_dim.87.column_ref, ...), custom_call_target="tpu_custom_call" | custom-call | flops 2300000000 | tf_op jit(solution)/shard_map/make_output/pallas_call | solution.py:328
  330.4 2.0 copy-done.6
  332.3 3.2 finish_weight_gradients.1
  (194 shorter events, 54.2 us)
Async XLA Ops:
  7.2 60.9 %all-gather.5.cloned.1.call-start = ((), (), s32[]{:S(2)}) async-start(), calls=%async_computation.9 | async-start | bytes 1863680 | tf_op jit(solution)/shard_map/all_gather | solution.py:775
  10.0 6.2 %collective-permute-start.3 = (s32[4]{0:T(128)S(1)}, s32[4]{0:T(128)S(1)}, u32[]{:S(2)}, u32[]{:S(2)}) collective-permute-start(s32[4]{0:T(128)S(1)} %convert_element_type.207), channel_id=1, source_target_pairs={{0,4},{4,0},{1,5},{5,1},{2,6},{6,2},{3,7},{7,3},{8,12},{12,8},{9,1... | collective-permute-start | bytes 56 | tf_op jit(solution)/shard_map/ppermute | solution.py:754
  27.0 56.6 %all-to-all-start.4 = ((bf16[4,200,896]{2,1,0:T(8,128)(2,1)}), bf16[4,200,896]{2,1,0:T(8,128)(2,1)S(1)}, u32[]{:S(2)}, u32[]{:S(2)}) async-start(bf16[4,200,896]{2,1,0:T(8,128)(2,1)} %get-tuple-element.111), calls=%async_computation.4 | async-start | bytes 2867200 | tf_op jit(solution)/shard_map/all_to_all | solution.py:749
  62.5 4.5 %collective-permute-start.7 = (f32[4,200]{1,0:T(4,128)S(1)}, f32[4,200]{1,0:T(4,128)S(1)}, u32[]{:S(2)}, u32[]{:S(2)}) collective-permute-start(f32[4,200]{1,0:T(4,128)S(1)} %fusion.40), channel_id=1, source_target_pairs={{0,24},{8,16},{16,8},{24,0},{1,25},{9,17},{17,9},{25,1},{2,26},{10... | collective-permute-start | bytes 9608 | tf_op jit(solution)/shard_map/ppermute | solution.py:733
  69.6 17.8 %collective-permute-start.8 = (bf16[4,104,808]{2,1,0:T(8,128)(2,1)S(1)}, bf16[4,104,808]{2,1,0:T(8,128)(2,1)}, u32[]{:S(2)}, u32[]{:S(2)}) collective-permute-start(bf16[4,104,808]{2,1,0:T(8,128)(2,1)S(1)} %get-tuple-element.118.refs_0_), channel_id=1, source_target_pairs={{0,8},{8,0},{16,24},{24,16},{1,9},{9,1},{17,25},{25,17},{2,10},{10... | collective-permute-start | bytes 2016776 | tf_op jit(solution)/shard_map/ppermute | solution.py:821
  70.3 18.0 %collective-permute-start.9 = (bf16[4,104,808]{2,1,0:T(8,128)(2,1)S(1)}, bf16[4,104,808]{2,1,0:T(8,128)(2,1)}, u32[]{:S(2)}, u32[]{:S(2)}) collective-permute-start(bf16[4,104,808]{2,1,0:T(8,128)(2,1)S(1)} %get-tuple-element.122.refs_4_), channel_id=1, source_target_pairs={{0,16},{8,24},{16,0},{24,8},{1,17},{9,25},{17,1},{25,9},{2,18},{10... | collective-permute-start | bytes 2016776 | tf_op jit(solution)/shard_map/ppermute | solution.py:821
  88.2 45.7 %all-to-all-start.5 = ((bf16[4,200,896]{2,1,0:T(8,128)(2,1)}), bf16[4,200,896]{2,1,0:T(8,128)(2,1)}, u32[]{:S(2)}, u32[]{:S(2)}) async-start(bf16[4,200,896]{2,1,0:T(8,128)(2,1)} %get-tuple-element.113), calls=%async_computation.5 | async-start | bytes 2867200 | tf_op jit(solution)/shard_map/all_to_all | solution.py:749
  99.0 150.2 %reduce-scatter.7.cloned.1.call-start = ((), (), s32[]{:S(2)}) async-start(), calls=%async_computation.11 | async-start | bytes 7454720
  99.0 19.7 %collective-permute-start.10 = (bf16[4,104,808]{2,1,0:T(8,128)(2,1)S(1)}, bf16[4,104,808]{2,1,0:T(8,128)(2,1)S(1)}, u32[]{:S(2)}, u32[]{:S(2)}) collective-permute-start(bf16[4,104,808]{2,1,0:T(8,128)(2,1)S(1)} %get-tuple-element.118.refs_0_), channel_id=1, source_target_pairs={{0,16},{8,24},{16,0},{24,8},{1,17},{9,25},{17,1},{25,9},{2,18},{10... | collective-permute-start | bytes 2016776 | tf_op jit(solution)/shard_map/ppermute | solution.py:821
  100.7 31.5 %collective-permute-start.11 = (bf16[4,104,808]{2,1,0:T(8,128)(2,1)}, bf16[4,104,808]{2,1,0:T(8,128)(2,1)S(1)}, u32[]{:S(2)}, u32[]{:S(2)}) collective-permute-start(bf16[4,104,808]{2,1,0:T(8,128)(2,1)} %collective-permute-done.8.refs_1_), channel_id=1, source_target_pairs={{0,16},{8,24},{16,0},{24,8},{1,17},{9,25},{17,1},{25,9},{2,18},{10... | collective-permute-start | bytes 2016776 | tf_op jit(solution)/shard_map/ppermute | solution.py:821
  101.1 31.1 %collective-permute-start.12 = (bf16[4,104,808]{2,1,0:T(8,128)(2,1)S(1)}, bf16[4,104,808]{2,1,0:T(8,128)(2,1)S(1)}, u32[]{:S(2)}, u32[]{:S(2)}) collective-permute-start(bf16[4,104,808]{2,1,0:T(8,128)(2,1)S(1)} %get-tuple-element.122.refs_4_), channel_id=1, source_target_pairs={{0,8},{8,0},{16,24},{24,16},{1,9},{9,1},{17,25},{25,17},{2,10},{10... | collective-permute-start | bytes 2016776 | tf_op jit(solution)/shard_map/ppermute | solution.py:821
  101.6 32.4 %collective-permute-start.13 = (bf16[4,104,808]{2,1,0:T(8,128)(2,1)}, bf16[4,104,808]{2,1,0:T(8,128)(2,1)}, u32[]{:S(2)}, u32[]{:S(2)}) collective-permute-start(bf16[4,104,808]{2,1,0:T(8,128)(2,1)} %collective-permute-done.9.refs_6_), channel_id=1, source_target_pairs={{0,8},{8,0},{16,24},{24,16},{1,9},{9,1},{17,25},{25,17},{2,10},{10... | collective-permute-start | bytes 2016776 | tf_op jit(solution)/shard_map/ppermute | solution.py:821
  103.8 30.6 %collective-permute-start.15 = (bf16[4,200,896]{2,1,0:T(8,128)(2,1)S(1)}, bf16[4,200,896]{2,1,0:T(8,128)(2,1)}, u32[]{:S(2)}, u32[]{:S(2)}) collective-permute-start(bf16[4,200,896]{2,1,0:T(8,128)(2,1)S(1)} %all-to-all-done.4.refs_10_), channel_id=1, source_target_pairs={{0,4},{4,0},{1,5},{5,1},{2,6},{6,2},{3,7},{7,3},{8,12},{12,8},{9,1... | collective-permute-start | bytes 4300808 | tf_op jit(solution)/shard_map/ppermute | solution.py:754
  181.8 104.0 %reduce-scatter.5.cloned.1.call-start = ((), (), s32[]{:S(2)}) async-start(), calls=%async_computation.8 | async-start | bytes 1863680 | tf_op jit(solution)/shard_map/reduce_scatter | solution.py:883
  183.1 18.7 %collective-permute-start.17 = (bf16[4,200,896]{2,1,0:T(8,128)(2,1)S(1)}, bf16[4,200,896]{2,1,0:T(8,128)(2,1)}, u32[]{:S(2)}, u32[]{:S(2)}) collective-permute-start(bf16[4,200,896]{2,1,0:T(8,128)(2,1)S(1)} %copy-done.27), channel_id=1, source_target_pairs={{0,4},{4,0},{1,5},{5,1},{2,6},{6,2},{3,7},{7,3},{8,12},{12,8},{9,1... | collective-permute-start | bytes 4300808 | tf_op jit(solution)/shard_map/ppermute | solution.py:754
  183.2 25.4 %collective-permute-start.16 = (bf16[4,200,896]{2,1,0:T(8,128)(2,1)}, bf16[4,200,896]{2,1,0:T(8,128)(2,1)}, u32[]{:S(2)}, u32[]{:S(2)}) collective-permute-start(bf16[4,200,896]{2,1,0:T(8,128)(2,1)} %get-tuple-element.132), channel_id=1, source_target_pairs={{0,4},{4,0},{1,5},{5,1},{2,6},{6,2},{3,7},{7,3},{8,12},{12,8},{9,1... | collective-permute-start | bytes 4300808 | tf_op jit(solution)/shard_map/ppermute | solution.py:754
  187.2 4.7 %collective-permute-start.21 = (f32[4,2,200]{2,1,0:T(2,128)S(1)}, f32[4,2,200]{2,1,0:T(2,128)S(1)}, u32[]{:S(2)}, u32[]{:S(2)}) collective-permute-start(f32[4,2,200]{2,1,0:T(2,128)S(1)} %add.177), channel_id=1, source_target_pairs={{0,24},{8,16},{16,8},{24,0},{1,25},{9,17},{17,9},{25,1},{2,26},{10... | collective-permute-start | bytes 19208 | tf_op jit(solution)/shard_map/ppermute | solution.py:733
  187.2 4.6 %collective-permute-start.20 = (f32[4,2,200]{2,1,0:T(2,128)S(1)}, f32[4,2,200]{2,1,0:T(2,128)S(1)}, u32[]{:S(2)}, u32[]{:S(2)}) collective-permute-start(f32[4,2,200]{2,1,0:T(2,128)S(1)} %add.177), channel_id=1, source_target_pairs={{0,16},{8,24},{16,0},{24,8},{1,17},{9,25},{17,1},{25,9},{2,18},{10... | collective-permute-start | bytes 19208 | tf_op jit(solution)/shard_map/ppermute | solution.py:733
  189.1 3.8 %collective-permute-start.19 = (f32[4,2,200]{2,1,0:T(2,128)S(1)}, f32[4,2,200]{2,1,0:T(2,128)S(1)}, u32[]{:S(2)}, u32[]{:S(2)}) collective-permute-start(f32[4,2,200]{2,1,0:T(2,128)S(1)} %add.177), channel_id=1, source_target_pairs={{0,8},{8,0},{16,24},{24,16},{1,9},{9,1},{17,25},{25,17},{2,10},{10... | collective-permute-start | bytes 19208 | tf_op jit(solution)/shard_map/ppermute | solution.py:733
  192.9 4.8 %collective-permute-start.22 = (f32[2,200]{1,0:T(2,128)S(1)}, f32[2,200]{1,0:T(2,128)S(1)}, u32[]{:S(2)}, u32[]{:S(2)}) collective-permute-start(f32[2,200]{1,0:T(2,128)S(1)} %get-tuple-element.205), channel_id=1, source_target_pairs={{0,3},{1,0},{2,1},{3,2},{4,7},{5,4},{6,5},{7,6},{8,11},{9,8},{10,9... | collective-permute-start | bytes 4808 | tf_op jit(solution)/shard_map/ppermute | solution.py:746
  196.4 4.5 %collective-permute-start.23 = (f32[2,200]{1,0:T(2,128)S(1)}, f32[2,200]{1,0:T(2,128)S(1)}, u32[]{:S(2)}, u32[]{:S(2)}) collective-permute-start(f32[2,200]{1,0:T(2,128)S(1)} %get-tuple-element.207), channel_id=1, source_target_pairs={{0,2},{1,3},{2,0},{3,1},{4,6},{5,7},{6,4},{7,5},{8,10},{9,11},{10,... | collective-permute-start | bytes 4808 | tf_op jit(solution)/shard_map/ppermute | solution.py:746
  196.4 5.4 %collective-permute-start.24 = (f32[2,200]{1,0:T(2,128)S(1)}, f32[2,200]{1,0:T(2,128)S(1)}, u32[]{:S(2)}, u32[]{:S(2)}) collective-permute-start(f32[2,200]{1,0:T(2,128)S(1)} %get-tuple-element.206), channel_id=1, source_target_pairs={{0,1},{1,2},{2,3},{3,0},{4,5},{5,6},{6,7},{7,4},{8,9},{9,10},{10,1... | collective-permute-start | bytes 4808 | tf_op jit(solution)/shard_map/ppermute | solution.py:746
  205.5 10.0 %collective-permute-start.25 = (bf16[200,896]{1,0:T(8,128)(2,1)}, bf16[200,896]{1,0:T(8,128)(2,1)}, u32[]{:S(2)}, u32[]{:S(2)}) collective-permute-start(bf16[200,896]{1,0:T(8,128)(2,1)} %get-tuple-element.138), channel_id=1, source_target_pairs={{0,3},{1,0},{2,1},{3,2},{4,7},{5,4},{6,5},{7,6},{8,11},{9,8},{10,9... | collective-permute-start | bytes 1075208 | tf_op jit(solution)/shard_map/ppermute | solution.py:746
  206.3 29.8 %collective-permute-start.26 = (bf16[200,896]{1,0:T(8,128)(2,1)}, bf16[200,896]{1,0:T(8,128)(2,1)}, u32[]{:S(2)}, u32[]{:S(2)}) collective-permute-start(bf16[200,896]{1,0:T(8,128)(2,1)} %get-tuple-element.139), channel_id=1, source_target_pairs={{0,2},{1,3},{2,0},{3,1},{4,6},{5,7},{6,4},{7,5},{8,10},{9,11},{10,... | collective-permute-start | bytes 1075208 | tf_op jit(solution)/shard_map/ppermute | solution.py:746
  206.5 29.6 %collective-permute-start.27 = (bf16[200,896]{1,0:T(8,128)(2,1)}, bf16[200,896]{1,0:T(8,128)(2,1)}, u32[]{:S(2)}, u32[]{:S(2)}) collective-permute-start(bf16[200,896]{1,0:T(8,128)(2,1)} %get-tuple-element.140), channel_id=1, source_target_pairs={{0,1},{1,2},{2,3},{3,0},{4,5},{5,6},{6,7},{7,4},{8,9},{9,10},{10,1... | collective-permute-start | bytes 1075208 | tf_op jit(solution)/shard_map/ppermute | solution.py:746
  249.9 80.5 %all-gather.7.cloned.1.call-start = ((), (), s32[]{:S(2)}) async-start(), calls=%async_computation.10 | async-start | bytes 3354624 | tf_op jit(solution)/shard_map/all_gather | solution.py:888
  285.8 29.9 %collective-permute-start.28 = (bf16[200,896]{1,0:T(8,128)(2,1)S(1)}, bf16[200,896]{1,0:T(8,128)(2,1)S(1)}, u32[]{:S(2)}, u32[]{:S(2)}) collective-permute-start(bf16[200,896]{1,0:T(8,128)(2,1)S(1)} %copy-done.21), channel_id=1, source_target_pairs={{0,3},{1,0},{2,1},{3,2},{4,7},{5,4},{6,5},{7,6},{8,11},{9,8},{10,9... | collective-permute-start | bytes 1075208 | tf_op jit(solution)/shard_map/ppermute | solution.py:746
  287.2 31.5 %collective-permute-start.29 = (bf16[200,896]{1,0:T(8,128)(2,1)S(1)}, bf16[200,896]{1,0:T(8,128)(2,1)S(1)}, u32[]{:S(2)}, u32[]{:S(2)}) collective-permute-start(bf16[200,896]{1,0:T(8,128)(2,1)S(1)} %copy-done.20), channel_id=1, source_target_pairs={{0,2},{1,3},{2,0},{3,1},{4,6},{5,7},{6,4},{7,5},{8,10},{9,11},{10,... | collective-permute-start | bytes 1075208 | tf_op jit(solution)/shard_map/ppermute | solution.py:746
  287.3 31.3 %collective-permute-start.30 = (bf16[200,896]{1,0:T(8,128)(2,1)S(1)}, bf16[200,896]{1,0:T(8,128)(2,1)S(1)}, u32[]{:S(2)}, u32[]{:S(2)}) collective-permute-start(bf16[200,896]{1,0:T(8,128)(2,1)S(1)} %get-tuple-element.154), channel_id=1, source_target_pairs={{0,1},{1,2},{2,3},{3,0},{4,5},{5,6},{6,7},{7,4},{8,9},{9,10},{10,1... | collective-permute-start | bytes 1075208 | tf_op jit(solution)/shard_map/ppermute | solution.py:746
  312.7 17.0 %collective-permute-start.32 = (f32[49,256]{1,0:T(8,128)S(1)}, f32[49,256]{1,0:T(8,128)S(1)}, u32[]{:S(2)}, u32[]{:S(2)}) collective-permute-start(f32[49,256]{1,0:T(8,128)S(1)} %add.184), channel_id=1, source_target_pairs={{0,8},{8,0},{16,24},{24,16},{1,9},{9,1},{17,25},{25,17},{2,10},{10... | collective-permute-start | bytes 150536 | tf_op jit(solution)/shard_map/ppermute | solution.py:733
  314.3 15.4 %collective-permute-start.33 = (f32[49,256]{1,0:T(8,128)S(1)}, f32[49,256]{1,0:T(8,128)S(1)}, u32[]{:S(2)}, u32[]{:S(2)}) collective-permute-start(f32[49,256]{1,0:T(8,128)S(1)} %add.184), channel_id=1, source_target_pairs={{0,16},{8,24},{16,0},{24,8},{1,17},{9,25},{17,1},{25,9},{2,18},{10... | collective-permute-start | bytes 150536 | tf_op jit(solution)/shard_map/ppermute | solution.py:733
  315.7 14.0 %collective-permute-start.34 = (f32[49,256]{1,0:T(8,128)S(1)}, f32[49,256]{1,0:T(8,128)S(1)}, u32[]{:S(2)}, u32[]{:S(2)}) collective-permute-start(f32[49,256]{1,0:T(8,128)S(1)} %add.184), channel_id=1, source_target_pairs={{0,24},{8,16},{16,8},{24,0},{1,25},{9,17},{17,9},{25,1},{2,26},{10... | collective-permute-start | bytes 150536 | tf_op jit(solution)/shard_map/ppermute | solution.py:733
  (39 other events, 462.4 us)
Sparse Core Ops, SparseCore 0:
  13.8 54.3 all-gather.4
  181.9 67.2 reduce-scatter.6
  251.5 34.1 reduce-scatter.4
  287.7 31.4 all-gather.6

commit v5 on v4

--- a/solution.py
+++ b/solution.py
@@ -834,9 +834,8 @@
     affine = jnp.stack([scale, shift - channel_mean * scale])
     normed_base, normed_over = pack_normed(at, convolved.reshape(parts, cells, width), affine, slots, base, over)
     places = sorted(ups), sorted(downs)
-    normed_base, grad_base, *held = after(
-        normed_base, grad_base, *[ups[p] for p in places[0]], *[downs[p] for p in places[1]]
-    )
+    normed_base, grad_base = after(normed_base, grad_base)
+    held = [ups[p] for p in places[0]] + [downs[p] for p in places[1]]
     ups, downs = dict(zip(places[0], held)), dict(zip(places[1], held[len(ups) :]))
     for j in range(1, len(bits)):
         ups, downs = double(ups, bits[j]), double(downs, bits[-1 - j])

time: 347 us -> 357 us (1.029)
  waiting for transfers between devices: 93.1 us -> 112 us
  starting transfers between devices: 46.7 us -> 42.8 us
    ppermute x6, waiting for transfers between devices: 33 us -> 42.5 us  [double(): lax.ppermute(value, 'xy', pairs)]
    all_gather x1, waiting for transfers between devices: 1.12 us -> 7.35 us  [per_device(): lax.all_gather(jnp.stack([up_rows, down_rows]), 'mp', axis=1, tiled=False)]
    all_to_all x2, starting transfers between devices: 16.6 us -> 10.5 us  [exchange(): return lax.all_to_all(by_part, 'mp', 0, 0, tiled=True)]
    ppermute x12, starting transfers between devices: 10.9 us -> 15.3 us  [everywhere(): lax.ppermute(value, axis, [(i, i ^ j) for i in range(size)])]
    unnamed x70 -> x74, local copies, waits for them, and re-layouts: 14 us -> 13.5 us
  transfers between devices with their start and end apart: 38 -> 38, of which waited for: 22 -> 22; matrix products, arithmetic and copies ran while one was open for 7% -> 6% of each run, Pallas kernels for 29% -> 28%
where the time goes in v5:
time: 357 us; the launch traced here: 356 us
  Pallas kernels  147 us (41%)
  waiting for transfers between devices  112 us (31%)
  starting transfers between devices  42.8 us (12%)
  local copies, waits for them, and re-layouts  23.3 us (7%)
  between operations  15.7 us (4%)
  other arithmetic  14.8 us (4%)
    pallas_call x1, Pallas kernels, pointwise(): pl.pallas_call(functools.partial(pointwise_kernel, chips=chips, parts=par...  44.2 us
    ppermute x6, waiting for transfers between devices, double(): lax.ppermute(value, 'xy', pairs)  42.5 us
    ppermute x9, waiting for transfers between devices, to_parts(): lax.ppermute(pieces[k], 'mp', ring(k))  32.1 us
    pallas_call x1, Pallas kernels, input_gradient(): pl.pallas_call(functools.partial(input_gradient_kernel, taps=taps, rows=r...  31.2 us
    pallas_call x1, Pallas kernels, conv_forward(): pl.pallas_call(functools.partial(forward_kernel, taps=taps, rows=rows, gr...  22 us
    pallas_call x1, Pallas kernels, taps_gradient(): pl.pallas_call(functools.partial(taps_gradient_kernel, taps=taps, rows=ro...  21 us
    ppermute x12, starting transfers between devices, everywhere(): lax.ppermute(value, axis, [(i, i ^ j) for i in range(size)])  15.3 us
    unnamed x74, local copies, waits for them, and re-layouts  13.5 us
  transfers between devices with their start and end apart: 38, of which 22 were waited for; matrix products, arithmetic and copies ran while one was open for 6% of the time, Pallas kernels for 28%

profile of v5, /device:TPU:0, one launch (start us, length us, event | category | flops | bytes accessed | tf_op | source)
XLA Modules:
  0.0 355.8 jit_solution(11018552830474217948)
XLA Ops:
  17.3 8.2 %pack_cotangent.1 = (bf16[4,200,896]{2,1,0:T(8,128)(2,1)}, bf16[4,200,256]{2,1,0:T(8,128)(2,1)}, f32[8,200]{1,0:T(8,128)S(1)}) custom-call(s32[22]{0:T(128)S(1)} %concatenate.9.at_ref, bf16[2,48,48,200]{3,2,1,0:T(8,128)(2,1)S(1)} %copy-done.7, bf16[2,48,48,128]{3,2,1,0:T(8,128)(2,1)S(1)} %broadcast_in_dim.74.m_ref, s32[4,1,1152]{2,1,0:T(1,128)S(1)} %reshape.141.slot_ref), custom_call_target="tpu_custom_call" | custom-call | flops 1916666624 | tf_op jit(solution)/shard_map/pack_cotangent/pallas_call | solution.py:254
  25.6 6.0 %all-to-all-start.4 = ((bf16[4,200,896]{2,1,0:T(8,128)(2,1)}), bf16[4,200,896]{2,1,0:T(8,128)(2,1)}, u32[]{:S(2)}, u32[]{:S(2)}) async-start(bf16[4,200,896]{2,1,0:T(8,128)(2,1)} %get-tuple-element.107), calls=%async_computation.4 | async-start | bytes 2867200 | tf_op jit(solution)/shard_map/all_to_all | solution.py:749
  35.4 22.0 %depthwise_forward.1 = (f32[4,2,12,48,200]{4,3,2,1,0:T(8,128)S(1)}, f32[2,2,2,8,128]{4,3,2,1,0:T(8,128)S(1)}) custom-call(bf16[2,48,48,200]{3,2,1,0:T(8,128)(2,1)S(1)} %copy-done.3, bf16[2,48,48,128]{3,2,1,0:T(8,128)(2,1)S(1)} %broadcast_in_dim.74.m_ref, f32[2,49,8,128]{3,2,1,0:T(8,128)S(1)} %broadcast_in_dim.83.w_ref), custom_call_target="tpu_custom_call" | custom-call | flops 4216666624 | tf_op jit(solution)/shard_map/depthwise_forward/pallas_call | solution.py:130
  57.5 2.2 copy-done.8
  66.0 2.5 collective-permute-done.7
  68.5 7.4 %all-gather.5.cloned.1.call-done = bf16[2,416,808]{2,1,0:T(8,128)(2,1)} async-done(((bf16[2,104,808]{2,1,0:T(8,128)(2,1)}), bf16[2,416,808]{2,1,0:T(8,128)(2,1)}) %all-gather.5.cloned.1.call-update) | async-done | bytes 1344528 | tf_op jit(solution)/shard_map/all_gather | solution.py:775
  77.7 2.3 copy-done.9
  80.1 6.9 %pack_normed.1 = (bf16[4,200,896]{2,1,0:T(8,128)(2,1)}, bf16[4,200,256]{2,1,0:T(8,128)(2,1)}) custom-call(s32[22]{0:T(128)S(1)} %concatenate.9.at_ref, f32[4,1152,200]{2,1,0:T(8,128)S(1)} %bitcast.107, f32[2,200]{1,0:T(2,128)S(1)} %pad_maximum_fusion.6.vec_ref, s32[4,1,1152]{2,1,0:T(1,128)S(1)} %reshape.141.slot_ref), custom_call_target="tpu_custom_call" | custom-call | flops 1533333376 | tf_op jit(solution)/shard_map/pack_normed/pallas_call | solution.py:200
  87.0 4.5 %all-to-all-start.5 = ((bf16[4,200,896]{2,1,0:T(8,128)(2,1)}), bf16[4,200,896]{2,1,0:T(8,128)(2,1)}, u32[]{:S(2)}, u32[]{:S(2)}) async-start(bf16[4,200,896]{2,1,0:T(8,128)(2,1)} %get-tuple-element.108), calls=%async_computation.5 | async-start | bytes 2867200 | tf_op jit(solution)/shard_map/all_to_all | solution.py:749
  93.8 2.0 collective-permute-start.9
  95.8 15.5 %collective-permute-done.8.refs_1_ = bf16[4,104,808]{2,1,0:T(8,128)(2,1)S(1)} collective-permute-done((bf16[4,104,808]{2,1,0:T(8,128)(2,1)S(1)}, bf16[4,104,808]{2,1,0:T(8,128)(2,1)S(1)}, u32[]{:S(2)}, u32[]{:S(2)}) %collective-permute-start.8) | collective-permute-done | bytes 672288 | tf_op jit(solution)/shard_map/ppermute | solution.py:821
  114.1 13.2 %collective-permute-done.11.refs_5_ = bf16[4,104,808]{2,1,0:T(8,128)(2,1)S(1)} collective-permute-done((bf16[4,104,808]{2,1,0:T(8,128)(2,1)S(1)}, bf16[4,104,808]{2,1,0:T(8,128)(2,1)S(1)}, u32[]{:S(2)}, u32[]{:S(2)}) %collective-permute-start.11) | collective-permute-done | bytes 672288 | tf_op jit(solution)/shard_map/ppermute | solution.py:821
  127.4 13.6 %collective-permute-done.10.refs_3_ = bf16[4,104,808]{2,1,0:T(8,128)(2,1)S(1)} collective-permute-done((bf16[4,104,808]{2,1,0:T(8,128)(2,1)S(1)}, bf16[4,104,808]{2,1,0:T(8,128)(2,1)S(1)}, u32[]{:S(2)}, u32[]{:S(2)}) %collective-permute-start.10) | collective-permute-done | bytes 672288 | tf_op jit(solution)/shard_map/ppermute | solution.py:821
  142.3 3.2 collective-permute-done.14.refs_9_
  145.5 44.2 %pointwise.1 = (f32[4,200,896]{2,1,0:T(8,128)}, f32[4,200,256]{2,1,0:T(8,128)}, bf16[4,200,896]{2,1,0:T(8,128)(2,1)}, bf16[4,200,256]{2,1,0:T(8,128)(2,1)}, f32[...) custom-call(s32[22]{0:T(128)} %copy-done.5, ...), custom_call_target="tpu_custom_call" | custom-call | flops 13416667136 | tf_op jit(solution)/shard_map/pointwise/pallas_call | solution.py:659
  192.1 3.1 collective-permute-done.18
  195.2 6.8 %collective-permute-start.21 = (f32[4,2,200]{2,1,0:T(2,128)S(1)}, f32[4,2,200]{2,1,0:T(2,128)S(1)}, u32[]{:S(2)}, u32[]{:S(2)}) collective-permute-start(f32[4,2,200]{2,1,0:T(2,128)S(1)} %add.177), channel_id=1, source_target_pairs={{0,24},{8,16},{16,8},{24,0},{1,25},{9,17},{17,9},{25,1},{2,26},{10... | collective-permute-start | bytes 19208 | tf_op jit(solution)/shard_map/ppermute | solution.py:733
  203.8 2.1 collective-permute-done.20
  205.9 3.2 collective-permute-start.23
  210.7 3.8 %collective-permute-done.24 = f32[2,200]{1,0:T(2,128)S(1)} collective-permute-done((f32[2,200]{1,0:T(2,128)S(1)}, f32[2,200]{1,0:T(2,128)S(1)}, u32[]{:S(2)}, u32[]{:S(2)}) %collective-permute-start.24) | collective-permute-done | bytes 1632 | tf_op jit(solution)/shard_map/ppermute | solution.py:746
  214.5 3.6 %fusion.11 = (bf16[200,896]{1,0:T(8,128)(2,1)}, bf16[200,896]{1,0:T(8,128)(2,1)}, bf16[200,896]{1,0:T(8,128)(2,1)}, bf16[200,896]{1,0:T(8,128)(2,1)}) fusion(f32[4,200,896]{2,1,0:T(8,128)} %get-tuple-element.125, bf16[4,200,896]{2,1,0:T(8,128)(2,1)} %collective-permute-done.17), kind=kLoop, calls=%fused_computation.37 | loop fusion | flops 2150400 | bytes 5734400 | tf_op jit(solution)/shard_map/convert_element_type | solution.py:857
  220.3 2.5 fusion.7
  222.7 5.2 %collective-permute-done.25.refs_1_ = bf16[200,896]{1,0:T(8,128)(2,1)} collective-permute-done((bf16[200,896]{1,0:T(8,128)(2,1)}, bf16[200,896]{1,0:T(8,128)(2,1)}, u32[]{:S(2)}, u32[]{:S(2)}) %collective-permute-start.25) | collective-permute-done | bytes 358432 | tf_op jit(solution)/shard_map/ppermute | solution.py:746
  227.9 20.6 %collective-permute-done.26.refs_2_ = bf16[200,896]{1,0:T(8,128)(2,1)} collective-permute-done((bf16[200,896]{1,0:T(8,128)(2,1)}, bf16[200,896]{1,0:T(8,128)(2,1)}, u32[]{:S(2)}, u32[]{:S(2)}) %collective-permute-start.26) | collective-permute-done | bytes 358432 | tf_op jit(solution)/shard_map/ppermute | solution.py:746
  248.5 2.3 broadcast_in_dim.87.column_ref
  252.1 10.2 %reduce-scatter.7.cloned.1.call-done = bf16[1,4,2,104,808]{4,3,2,1,0:T(8,128)(2,1)} async-done(((bf16[4,4,2,104,808]{4,3,2,1,0:T(8,128)(2,1)}), bf16[1,4,2,104,808]{4,3,2,1,0:T(8,128)(2,1)}) %reduce-scatter.7.cloned.1.call-update) | async-done | bytes 1344528
  263.1 31.2 %input_gradient.1 = (bf16[2,48,48,200]{3,2,1,0:T(8,128)(2,1)}, f32[2,2,54,64,128]{4,3,2,1,0:T(8,128)}) custom-call(s32[22]{0:T(128)} %copy-done.5, bf16[2,48,48,128]{3,2,1,0:T(8,128)(2,1)} %copy-done.2, bf16[2,48,48,200]{3,2,1,0:T(8,128)(2,1)} %cot_ref.3, f32[4,2,12,48,200]{4,3,2,1,0:T(8,128)} %copy-done.8, f32[2,49,8,128]{3,2,1,0:T(8,128)} %copy-done.4, ...), custom_call_target="tpu_custom_call" | custom-call | flops 5366666752 | tf_op jit(solution)/shard_map/input_gradient/pallas_call | solution.py:400
  294.3 4.5 %reduce-scatter.5.cloned.1.call-done = bf16[1,2,104,808]{3,2,1,0:T(8,128)(2,1)} async-done(((bf16[4,2,104,808]{3,2,1,0:T(8,128)(2,1)}), bf16[1,2,104,808]{3,2,1,0:T(8,128)(2,1)}) %reduce-scatter.5.cloned.1.call-update) | async-done | bytes 336144 | tf_op jit(solution)/shard_map/reduce_scatter | solution.py:882
  302.3 21.0 %taps_gradient.1 = f32[2,49,8,128]{3,2,1,0:T(8,128)} custom-call(bf16[2,48,48,200]{3,2,1,0:T(8,128)(2,1)} %x_ref.2, bf16[2,48,48,128]{3,2,1,0:T(8,128)(2,1)} %copy-done.2, f32[2,2,54,64,128]{4,3,2,1,0:T(8,128)} %get-tuple-element.162.gs_ref), custom_call_target="tpu_custom_call" | custom-call | flops 4216666624 | tf_op jit(solution)/shard_map/taps_gradient/pallas_call | solution.py:458
  329.4 2.4 collective-permute-done.29.refs_2_
  332.6 10.1 %make_output.1 = bf16[2,48,48,200]{3,2,1,0:T(8,128)(2,1)} custom-call(s32[22]{0:T(128)} %copy-done.5, bf16[2,48,48,200]{3,2,1,0:T(8,128)(2,1)} %x_ref.2, bf16[2,48,48,128]{3,2,1,0:T(8,128)(2,1)} %copy-done.2, f32[1,200]{1,0:T(1,128)} %bitcast.148, s32[4,2,576,128]{3,2,1,0:T(8,128)} %broadcast_in_dim.87.column_ref, ...), custom_call_target="tpu_custom_call" | custom-call | flops 2300000000 | tf_op jit(solution)/shard_map/make_output/pallas_call | solution.py:328
  345.4 3.2 finish_weight_gradients.1
  (198 shorter events, 50.6 us)
Async XLA Ops:
  7.2 68.7 %all-gather.5.cloned.1.call-start = ((), (), s32[]{:S(2)}) async-start(), calls=%async_computation.9 | async-start | bytes 1863680 | tf_op jit(solution)/shard_map/all_gather | solution.py:775
  10.0 4.8 %collective-permute-start.3 = (s32[4]{0:T(128)S(1)}, s32[4]{0:T(128)S(1)}, u32[]{:S(2)}, u32[]{:S(2)}) collective-permute-start(s32[4]{0:T(128)S(1)} %convert_element_type.207), channel_id=1, source_target_pairs={{0,4},{4,0},{1,5},{5,1},{2,6},{6,2},{3,7},{7,3},{8,12},{12,8},{9,1... | collective-permute-start | bytes 56 | tf_op jit(solution)/shard_map/ppermute | solution.py:754
  25.6 61.4 %all-to-all-start.4 = ((bf16[4,200,896]{2,1,0:T(8,128)(2,1)}), bf16[4,200,896]{2,1,0:T(8,128)(2,1)}, u32[]{:S(2)}, u32[]{:S(2)}) async-start(bf16[4,200,896]{2,1,0:T(8,128)(2,1)} %get-tuple-element.107), calls=%async_computation.4 | async-start | bytes 2867200 | tf_op jit(solution)/shard_map/all_to_all | solution.py:749
  64.0 4.5 %collective-permute-start.7 = (f32[4,200]{1,0:T(4,128)S(1)}, f32[4,200]{1,0:T(4,128)S(1)}, u32[]{:S(2)}, u32[]{:S(2)}) collective-permute-start(f32[4,200]{1,0:T(4,128)S(1)} %fusion.40), channel_id=1, source_target_pairs={{0,24},{8,16},{16,8},{24,0},{1,25},{9,17},{17,9},{25,1},{2,26},{10... | collective-permute-start | bytes 9608 | tf_op jit(solution)/shard_map/ppermute | solution.py:733
  87.0 54.9 %all-to-all-start.5 = ((bf16[4,200,896]{2,1,0:T(8,128)(2,1)}), bf16[4,200,896]{2,1,0:T(8,128)(2,1)}, u32[]{:S(2)}, u32[]{:S(2)}) async-start(bf16[4,200,896]{2,1,0:T(8,128)(2,1)} %get-tuple-element.108), calls=%async_computation.5 | async-start | bytes 2867200 | tf_op jit(solution)/shard_map/all_to_all | solution.py:749
  91.5 170.8 %reduce-scatter.7.cloned.1.call-start = ((), (), s32[]{:S(2)}) async-start(), calls=%async_computation.11 | async-start | bytes 7454720
  91.7 19.7 %collective-permute-start.8 = (bf16[4,104,808]{2,1,0:T(8,128)(2,1)S(1)}, bf16[4,104,808]{2,1,0:T(8,128)(2,1)S(1)}, u32[]{:S(2)}, u32[]{:S(2)}) collective-permute-start(bf16[4,104,808]{2,1,0:T(8,128)(2,1)S(1)} %get-tuple-element.110.refs_0_), channel_id=1, source_target_pairs={{0,8},{8,0},{16,24},{24,16},{1,9},{9,1},{17,25},{25,17},{2,10},{10... | collective-permute-start | bytes 2016776 | tf_op jit(solution)/shard_map/ppermute | solution.py:821
  91.8 19.7 %collective-permute-start.12 = (bf16[4,104,808]{2,1,0:T(8,128)(2,1)S(1)}, bf16[4,104,808]{2,1,0:T(8,128)(2,1)S(1)}, u32[]{:S(2)}, u32[]{:S(2)}) collective-permute-start(bf16[4,104,808]{2,1,0:T(8,128)(2,1)S(1)} %get-tuple-element.114.refs_4_), channel_id=1, source_target_pairs={{0,16},{8,24},{16,0},{24,8},{1,17},{9,25},{17,1},{25,9},{2,18},{10... | collective-permute-start | bytes 2016776 | tf_op jit(solution)/shard_map/ppermute | solution.py:821
  92.5 34.8 %collective-permute-start.11 = (bf16[4,104,808]{2,1,0:T(8,128)(2,1)S(1)}, bf16[4,104,808]{2,1,0:T(8,128)(2,1)S(1)}, u32[]{:S(2)}, u32[]{:S(2)}) collective-permute-start(bf16[4,104,808]{2,1,0:T(8,128)(2,1)S(1)} %get-tuple-element.114.refs_4_), channel_id=1, source_target_pairs={{0,8},{8,0},{16,24},{24,16},{1,9},{9,1},{17,25},{25,17},{2,10},{10... | collective-permute-start | bytes 2016776 | tf_op jit(solution)/shard_map/ppermute | solution.py:821
  93.8 33.6 %collective-permute-start.9 = (bf16[4,104,808]{2,1,0:T(8,128)(2,1)S(1)}, bf16[4,104,808]{2,1,0:T(8,128)(2,1)S(1)}, u32[]{:S(2)}, u32[]{:S(2)}) collective-permute-start(bf16[4,104,808]{2,1,0:T(8,128)(2,1)S(1)} %get-tuple-element.110.refs_0_), channel_id=1, source_target_pairs={{0,16},{8,24},{16,0},{24,8},{1,17},{9,25},{17,1},{25,9},{2,18},{10... | collective-permute-start | bytes 2016776 | tf_op jit(solution)/shard_map/ppermute | solution.py:821
  111.4 29.7 %collective-permute-start.10 = (bf16[4,104,808]{2,1,0:T(8,128)(2,1)S(1)}, bf16[4,104,808]{2,1,0:T(8,128)(2,1)S(1)}, u32[]{:S(2)}, u32[]{:S(2)}) collective-permute-start(bf16[4,104,808]{2,1,0:T(8,128)(2,1)S(1)} %collective-permute-done.8.refs_1_), channel_id=1, source_target_pairs={{0,16},{8,24},{16,0},{24,8},{1,17},{9,25},{17,1},{25,9},{2,18},{10... | collective-permute-start | bytes 2016776 | tf_op jit(solution)/shard_map/ppermute | solution.py:821
  111.4 30.5 %collective-permute-start.13 = (bf16[4,104,808]{2,1,0:T(8,128)(2,1)S(1)}, bf16[4,104,808]{2,1,0:T(8,128)(2,1)}, u32[]{:S(2)}, u32[]{:S(2)}) collective-permute-start(bf16[4,104,808]{2,1,0:T(8,128)(2,1)S(1)} %collective-permute-done.12.refs_6_), channel_id=1, source_target_pairs={{0,8},{8,0},{16,24},{24,16},{1,9},{9,1},{17,25},{25,17},{2,10},{10... | collective-permute-start | bytes 2016776 | tf_op jit(solution)/shard_map/ppermute | solution.py:821
  114.0 28.2 %collective-permute-start.15 = (bf16[4,200,896]{2,1,0:T(8,128)(2,1)}, bf16[4,200,896]{2,1,0:T(8,128)(2,1)}, u32[]{:S(2)}, u32[]{:S(2)}) collective-permute-start(bf16[4,200,896]{2,1,0:T(8,128)(2,1)} %all-to-all-done.4.refs_10_), channel_id=1, source_target_pairs={{0,4},{4,0},{1,5},{5,1},{2,6},{6,2},{3,7},{7,3},{8,12},{12,8},{9,1... | collective-permute-start | bytes 4300808 | tf_op jit(solution)/shard_map/ppermute | solution.py:754
  189.7 109.1 %reduce-scatter.5.cloned.1.call-start = ((), (), s32[]{:S(2)}) async-start(), calls=%async_computation.8 | async-start | bytes 1863680 | tf_op jit(solution)/shard_map/reduce_scatter | solution.py:882
  191.1 23.5 %collective-permute-start.17 = (bf16[4,200,896]{2,1,0:T(8,128)(2,1)S(1)}, bf16[4,200,896]{2,1,0:T(8,128)(2,1)}, u32[]{:S(2)}, u32[]{:S(2)}) collective-permute-start(bf16[4,200,896]{2,1,0:T(8,128)(2,1)S(1)} %copy-done.27), channel_id=1, source_target_pairs={{0,4},{4,0},{1,5},{5,1},{2,6},{6,2},{3,7},{7,3},{8,12},{12,8},{9,1... | collective-permute-start | bytes 4300808 | tf_op jit(solution)/shard_map/ppermute | solution.py:754
  191.2 29.1 %collective-permute-start.16 = (bf16[4,200,896]{2,1,0:T(8,128)(2,1)}, bf16[4,200,896]{2,1,0:T(8,128)(2,1)}, u32[]{:S(2)}, u32[]{:S(2)}) collective-permute-start(bf16[4,200,896]{2,1,0:T(8,128)(2,1)} %get-tuple-element.124), channel_id=1, source_target_pairs={{0,4},{4,0},{1,5},{5,1},{2,6},{6,2},{3,7},{7,3},{8,12},{12,8},{9,1... | collective-permute-start | bytes 4300808 | tf_op jit(solution)/shard_map/ppermute | solution.py:754
  195.2 8.5 %collective-permute-start.21 = (f32[4,2,200]{2,1,0:T(2,128)S(1)}, f32[4,2,200]{2,1,0:T(2,128)S(1)}, u32[]{:S(2)}, u32[]{:S(2)}) collective-permute-start(f32[4,2,200]{2,1,0:T(2,128)S(1)} %add.177), channel_id=1, source_target_pairs={{0,24},{8,16},{16,8},{24,0},{1,25},{9,17},{17,9},{25,1},{2,26},{10... | collective-permute-start | bytes 19208 | tf_op jit(solution)/shard_map/ppermute | solution.py:733
  202.0 3.8 %collective-permute-start.20 = (f32[4,2,200]{2,1,0:T(2,128)S(1)}, f32[4,2,200]{2,1,0:T(2,128)S(1)}, u32[]{:S(2)}, u32[]{:S(2)}) collective-permute-start(f32[4,2,200]{2,1,0:T(2,128)S(1)} %add.177), channel_id=1, source_target_pairs={{0,16},{8,24},{16,0},{24,8},{1,17},{9,25},{17,1},{25,9},{2,18},{10... | collective-permute-start | bytes 19208 | tf_op jit(solution)/shard_map/ppermute | solution.py:733
  202.0 3.8 %collective-permute-start.19 = (f32[4,2,200]{2,1,0:T(2,128)S(1)}, f32[4,2,200]{2,1,0:T(2,128)S(1)}, u32[]{:S(2)}, u32[]{:S(2)}) collective-permute-start(f32[4,2,200]{2,1,0:T(2,128)S(1)} %add.177), channel_id=1, source_target_pairs={{0,8},{8,0},{16,24},{24,16},{1,9},{9,1},{17,25},{25,17},{2,10},{10... | collective-permute-start | bytes 19208 | tf_op jit(solution)/shard_map/ppermute | solution.py:733
  205.9 4.7 %collective-permute-start.22 = (f32[2,200]{1,0:T(2,128)S(1)}, f32[2,200]{1,0:T(2,128)S(1)}, u32[]{:S(2)}, u32[]{:S(2)}) collective-permute-start(f32[2,200]{1,0:T(2,128)S(1)} %get-tuple-element.197), channel_id=1, source_target_pairs={{0,3},{1,0},{2,1},{3,2},{4,7},{5,4},{6,5},{7,6},{8,11},{9,8},{10,9... | collective-permute-start | bytes 4808 | tf_op jit(solution)/shard_map/ppermute | solution.py:746
  205.9 4.8 %collective-permute-start.23 = (f32[2,200]{1,0:T(2,128)S(1)}, f32[2,200]{1,0:T(2,128)S(1)}, u32[]{:S(2)}, u32[]{:S(2)}) collective-permute-start(f32[2,200]{1,0:T(2,128)S(1)} %get-tuple-element.199), channel_id=1, source_target_pairs={{0,2},{1,3},{2,0},{3,1},{4,6},{5,7},{6,4},{7,5},{8,10},{9,11},{10,... | collective-permute-start | bytes 4808 | tf_op jit(solution)/shard_map/ppermute | solution.py:746
  209.1 5.4 %collective-permute-start.24 = (f32[2,200]{1,0:T(2,128)S(1)}, f32[2,200]{1,0:T(2,128)S(1)}, u32[]{:S(2)}, u32[]{:S(2)}) collective-permute-start(f32[2,200]{1,0:T(2,128)S(1)} %get-tuple-element.198), channel_id=1, source_target_pairs={{0,1},{1,2},{2,3},{3,0},{4,5},{5,6},{6,7},{7,4},{8,9},{9,10},{10,1... | collective-permute-start | bytes 4808 | tf_op jit(solution)/shard_map/ppermute | solution.py:746
  218.1 9.8 %collective-permute-start.25 = (bf16[200,896]{1,0:T(8,128)(2,1)}, bf16[200,896]{1,0:T(8,128)(2,1)}, u32[]{:S(2)}, u32[]{:S(2)}) collective-permute-start(bf16[200,896]{1,0:T(8,128)(2,1)} %get-tuple-element.130), channel_id=1, source_target_pairs={{0,3},{1,0},{2,1},{3,2},{4,7},{5,4},{6,5},{7,6},{8,11},{9,8},{10,9... | collective-permute-start | bytes 1075208 | tf_op jit(solution)/shard_map/ppermute | solution.py:746
  218.3 30.2 %collective-permute-start.26 = (bf16[200,896]{1,0:T(8,128)(2,1)}, bf16[200,896]{1,0:T(8,128)(2,1)}, u32[]{:S(2)}, u32[]{:S(2)}) collective-permute-start(bf16[200,896]{1,0:T(8,128)(2,1)} %get-tuple-element.131), channel_id=1, source_target_pairs={{0,2},{1,3},{2,0},{3,1},{4,6},{5,7},{6,4},{7,5},{8,10},{9,11},{10,... | collective-permute-start | bytes 1075208 | tf_op jit(solution)/shard_map/ppermute | solution.py:746
  219.5 29.0 %collective-permute-start.27 = (bf16[200,896]{1,0:T(8,128)(2,1)}, bf16[200,896]{1,0:T(8,128)(2,1)}, u32[]{:S(2)}, u32[]{:S(2)}) collective-permute-start(bf16[200,896]{1,0:T(8,128)(2,1)} %get-tuple-element.132), channel_id=1, source_target_pairs={{0,1},{1,2},{2,3},{3,0},{4,5},{5,6},{6,7},{7,4},{8,9},{9,10},{10,1... | collective-permute-start | bytes 1075208 | tf_op jit(solution)/shard_map/ppermute | solution.py:746
  262.9 80.5 %all-gather.7.cloned.1.call-start = ((), (), s32[]{:S(2)}) async-start(), calls=%async_computation.10 | async-start | bytes 3354624 | tf_op jit(solution)/shard_map/all_gather | solution.py:887
  298.9 29.9 %collective-permute-start.28 = (bf16[200,896]{1,0:T(8,128)(2,1)S(1)}, bf16[200,896]{1,0:T(8,128)(2,1)S(1)}, u32[]{:S(2)}, u32[]{:S(2)}) collective-permute-start(bf16[200,896]{1,0:T(8,128)(2,1)S(1)} %copy-done.21), channel_id=1, source_target_pairs={{0,3},{1,0},{2,1},{3,2},{4,7},{5,4},{6,5},{7,6},{8,11},{9,8},{10,9... | collective-permute-start | bytes 1075208 | tf_op jit(solution)/shard_map/ppermute | solution.py:746
  300.3 31.5 %collective-permute-start.29 = (bf16[200,896]{1,0:T(8,128)(2,1)S(1)}, bf16[200,896]{1,0:T(8,128)(2,1)S(1)}, u32[]{:S(2)}, u32[]{:S(2)}) collective-permute-start(bf16[200,896]{1,0:T(8,128)(2,1)S(1)} %copy-done.20), channel_id=1, source_target_pairs={{0,2},{1,3},{2,0},{3,1},{4,6},{5,7},{6,4},{7,5},{8,10},{9,11},{10,... | collective-permute-start | bytes 1075208 | tf_op jit(solution)/shard_map/ppermute | solution.py:746
  300.4 31.4 %collective-permute-start.30 = (bf16[200,896]{1,0:T(8,128)(2,1)S(1)}, bf16[200,896]{1,0:T(8,128)(2,1)S(1)}, u32[]{:S(2)}, u32[]{:S(2)}) collective-permute-start(bf16[200,896]{1,0:T(8,128)(2,1)S(1)} %get-tuple-element.146), channel_id=1, source_target_pairs={{0,1},{1,2},{2,3},{3,0},{4,5},{5,6},{6,7},{7,4},{8,9},{9,10},{10,1... | collective-permute-start | bytes 1075208 | tf_op jit(solution)/shard_map/ppermute | solution.py:746
  325.8 17.0 %collective-permute-start.32 = (f32[49,256]{1,0:T(8,128)S(1)}, f32[49,256]{1,0:T(8,128)S(1)}, u32[]{:S(2)}, u32[]{:S(2)}) collective-permute-start(f32[49,256]{1,0:T(8,128)S(1)} %add.184), channel_id=1, source_target_pairs={{0,8},{8,0},{16,24},{24,16},{1,9},{9,1},{17,25},{25,17},{2,10},{10... | collective-permute-start | bytes 150536 | tf_op jit(solution)/shard_map/ppermute | solution.py:733
  327.3 15.5 %collective-permute-start.33 = (f32[49,256]{1,0:T(8,128)S(1)}, f32[49,256]{1,0:T(8,128)S(1)}, u32[]{:S(2)}, u32[]{:S(2)}) collective-permute-start(f32[49,256]{1,0:T(8,128)S(1)} %add.184), channel_id=1, source_target_pairs={{0,16},{8,24},{16,0},{24,8},{1,17},{9,25},{17,1},{25,9},{2,18},{10... | collective-permute-start | bytes 150536 | tf_op jit(solution)/shard_map/ppermute | solution.py:733
  328.8 14.0 %collective-permute-start.34 = (f32[49,256]{1,0:T(8,128)S(1)}, f32[49,256]{1,0:T(8,128)S(1)}, u32[]{:S(2)}, u32[]{:S(2)}) collective-permute-start(f32[49,256]{1,0:T(8,128)S(1)} %add.184), channel_id=1, source_target_pairs={{0,24},{8,16},{16,8},{24,0},{1,25},{9,17},{17,9},{25,1},{2,26},{10... | collective-permute-start | bytes 150536 | tf_op jit(solution)/shard_map/ppermute | solution.py:733
  (41 other events, 514.2 us)
Sparse Core Ops, SparseCore 0:
  13.8 62.0 all-gather.4
  189.9 72.3 reduce-scatter.6
  264.6 34.1 reduce-scatter.4
  300.7 31.4 all-gather.6
